TPU v7x, 32 devices: a whole 2x2x4 slice. The times are simulated.
32 devices in a mesh: seq: 8 (over z, x), row: 4 (over y, core).
Axes of the slice: x: 2, y: 2, z: 4, core: 2. Of those that a mesh axis runs over, the one named last changes fastest.
Arguments:
- block_input: bfloat16 [4, 1024, 1024], P('row', 'seq'), may hold values from -6 to 6
- cotangent: bfloat16 [4, 1024, 1024], P('row', 'seq'), may hold values from -6 to 6
- doc_starts: int32 [4, 8], P('row'), may hold values from 0 to 1023, as said below
- qkv_weight: bfloat16 [1024, 3072], P('seq'), may hold values from -0.1875 to 0.1875
- beta_weight: bfloat16 [1024, 8], P('seq'), may hold values from -0.1875 to 0.1875
- conv_weight: bfloat16 [4, 3072], P(None, 'seq'), may hold values from -3 to 3
- norm_gains: bfloat16 [2, 1024], P(None, 'seq'), may hold values from 0.25 to 1.75
- head_gain: bfloat16 [128], P('seq'), may hold values from 0.25 to 1.75
- out_weight: bfloat16 [1024, 1024], P('seq'), may hold values from -0.1875 to 0.1875
- gate_up_weight: bfloat16 [1024, 5632], P('seq'), may hold values from -0.1875 to 0.1875
- down_weight: bfloat16 [2816, 1024], P('seq'), may hold values from -0.109375 to 0.109375
Outputs:
- mixed: bfloat16 [4, 1024, 1024], P('row', 'seq')
- block_input_gradient: bfloat16 [4, 1024, 1024], P('row', 'seq')
- grad_qkv: float32 [1024, 3072], P('seq')
- grad_beta: float32 [1024, 8], P('seq')
- grad_conv: float32 [4, 3072], P(None, 'seq')
- grad_gains: float32 [2, 1024], P(None, 'seq')
- grad_head_gain: float32 [128], P('seq')
- grad_out: float32 [1024, 1024], P('seq')
- grad_gate_up: float32 [1024, 5632], P('seq')
- grad_down: float32 [2816, 1024], P('seq')
Inputs may be any that keep to these rules, and one draw needn't show every extreme that they name: `doc_starts`: in each row the starts are non-decreasing, the first is 0 and the last is 1024 - 1 (a document may be empty); one document begins among the row's first 128 tokens and ends among its last 128.
All inputs are finite; a program needn't handle non-finite values.
Results may differ from a plain program's by a relative error of at most 0.023.
Values may be sent and summed in bfloat16 or wider, within the bound.
No kernel may reach another device: no remote copies, remote signals or barrier semaphores. Data moves between devices by JAX's collectives and lax.ppermute only.
A program may use at most 256 MiB of HBM per device.

v0:
```python
import functools

import jax
import jax.numpy as jnp
from jax import lax
from jax.experimental import pallas as pl
from jax.experimental.pallas import tpu as pltpu
from jax.sharding import PartitionSpec as P

H = 8
DK = 128
GROUP = 64


EPS_NORM = 1e-06
EPS_HEAD = 1e-05
EPS_UNIT = 1e-06
HIGH = lax.Precision.HIGHEST


def shifted(block, axis, distance):
    devices = range(lax.axis_size(axis))
    route = [(i - distance, i) for i in devices if i - distance in devices]
    return lax.ppermute(block, axis, route)


def dotf(first_op, second_op):
    return jnp.matmul(first_op, second_op, precision=HIGH)


def swap_last(matrix):
    return jnp.swapaxes(matrix, -1, -2)


def tok_dot(first_op, second_op):
    return lax.dot_general(
        first_op, second_op, (((0,), (0,)), ((), ())), preferred_element_type=jnp.float32
    )


def back_dot(first_op, second_op):
    return lax.dot_general(
        first_op, second_op, (((1,), (1,)), ((), ())), preferred_element_type=jnp.float32
    )


def unit_inverse(lower):
    identity = jnp.eye(lower.shape[-1], dtype=lower.dtype)
    power = lower
    result = identity - lower
    for step_index in range(lower.shape[-1].bit_length() - 2):
        power = dotf(power, power)
        result = dotf(result, identity + power)
    return result


def doc_index(positions, starts):
    return jnp.sum((starts[None, :] <= positions[:, None]).astype(jnp.int32), axis=1) - 1


def root_mean_square_backward(grad_in, normed, inverse):
    return inverse * (grad_in - normed * jnp.mean(grad_in * normed, -1, keepdims=True))


def silu_back(grad_in, pre):
    sig = jax.nn.sigmoid(pre)
    return grad_in * sig * (1.0 + pre * (1.0 - sig))


def on_device(
    block_input,
    cotangent,
    doc_starts,
    qkv_weight,
    beta_weight,
    conv_weight,
    norm_gains,
    head_gain,
    out_weight,
    gate_up_weight,
    down_weight,
):
    token_rows = block_input[0].astype(jnp.float32)
    cot_low = cotangent[0]
    seq_len = token_rows.shape[0]
    width = token_rows.shape[1]
    n_groups = seq_len // GROUP
    scale = DK ** (-0.5)
    w_qkv, w_beta, w_conv, w_gains, w_head, w_out, w_gu, w_down = (
        lax.all_gather(qkv_weight, "seq", axis=0, tiled=True),
        lax.all_gather(beta_weight, "seq", axis=0, tiled=True),
        lax.all_gather(conv_weight, "seq", axis=1, tiled=True),
        lax.all_gather(norm_gains, "seq", axis=1, tiled=True),
        lax.all_gather(head_gain, "seq", axis=0, tiled=True),
        lax.all_gather(out_weight, "seq", axis=0, tiled=True),
        lax.all_gather(gate_up_weight, "seq", axis=0, tiled=True),
        lax.all_gather(down_weight, "seq", axis=0, tiled=True),
    )
    conv_f = w_conv.astype(jnp.float32)
    float_gains = w_gains.astype(jnp.float32)
    head_f = w_head.astype(jnp.float32)
    seq_count = lax.axis_size("seq")
    seq_place = lax.axis_index("seq")
    starts = doc_starts[0]
    positions = seq_place * seq_len + jnp.arange(seq_len, dtype=jnp.int32)
    doc = doc_index(positions, starts)
    rim = conv_f.shape[0] - 1
    rim_doc = doc_index(seq_place * seq_len - rim + jnp.arange(rim, dtype=jnp.int32), starts)
    first_inverse_norm = lax.rsqrt(jnp.mean(token_rows * token_rows, -1, keepdims=True) + EPS_NORM)
    normalized_input = token_rows * first_inverse_norm
    first_activation = (normalized_input * float_gains[0]).astype(jnp.bfloat16)
    proj = jnp.dot(first_activation, w_qkv, preferred_element_type=jnp.float32).astype(jnp.bfloat16)
    rates_tok = jax.nn.sigmoid(
        jnp.dot(first_activation, w_beta, preferred_element_type=jnp.float32)
    )
    rim_vals = shifted(proj[seq_len - rim :], "seq", 1)
    extended = jnp.concatenate([rim_vals, proj], 0).astype(jnp.float32)
    ext_doc = jnp.concatenate([rim_doc, doc])
    matches = [
        (ext_doc[rim - tap : rim - tap + seq_len] == doc).astype(jnp.float32)[:, None]
        for tap in range(rim + 1)
    ]
    pre = jnp.zeros((seq_len, extended.shape[1]), jnp.float32)
    for tap in range(rim + 1):
        pre = pre + conv_f[tap] * extended[rim - tap : rim - tap + seq_len] * matches[tap]
    act = jax.nn.silu(pre)
    q_raw = act[:, :width].reshape(seq_len, H, DK)
    k_raw = act[:, width : 2 * width].reshape(seq_len, H, DK)
    v_raw = act[:, 2 * width :].reshape(seq_len, H, DK)
    q_inv = lax.rsqrt(jnp.sum(q_raw * q_raw, -1, keepdims=True) + EPS_UNIT)
    k_inv = lax.rsqrt(jnp.sum(k_raw * k_raw, -1, keepdims=True) + EPS_UNIT)
    q_unit = q_raw * q_inv
    k_unit = k_raw * k_inv

    def to_groups(arr):
        return (
            arr.astype(jnp.bfloat16)
            .astype(jnp.float32)
            .reshape(n_groups, GROUP, H, DK)
            .transpose(0, 2, 1, 3)
        )

    scaled_q = to_groups(q_unit) * scale
    keys = to_groups(k_unit)
    values = to_groups(v_raw)
    rates = rates_tok.reshape(n_groups, GROUP, H).transpose(0, 2, 1)
    block_doc = doc.reshape(n_groups, GROUP)
    prev_doc = doc_index(
        seq_place * seq_len + jnp.arange(n_groups, dtype=jnp.int32) * GROUP - 1, starts
    )
    places = jnp.arange(GROUP)
    same = block_doc[:, :, None] == block_doc[:, None, :]
    strict = ((places[:, None] > places[None, :])[None] & same)[:, None].astype(jnp.float32)
    incl = ((places[:, None] >= places[None, :])[None] & same)[:, None].astype(jnp.float32)
    keep = (block_doc == prev_doc[:, None]).astype(jnp.float32)[:, None, :, None]
    tail = (block_doc == block_doc[:, -1:]).astype(jnp.float32)[:, None, :, None]
    whole = keep[:, 0, -1, 0]
    scaled = keys * rates[..., None]
    lower = jnp.einsum("nhid,nhjd->nhij", scaled, keys, precision=HIGH) * strict
    inverse = unit_inverse(lower)
    w_mat = dotf(inverse, scaled)
    base = dotf(inverse, values * rates[..., None])
    eye_heads = jnp.broadcast_to(jnp.eye(DK, dtype=jnp.float32), (H, DK, DK))
    zero_heads = jnp.zeros((H, DK, DK), jnp.float32)

    def chain_step(maps, inputs):
        c_keys, c_w, c_base, c_keep, c_tail, c_whole = inputs
        mixed_maps = dotf(c_w[None], maps)
        reduce_part = jnp.einsum(
            "hcd,shce->shde", c_keys * (c_tail * c_keep), mixed_maps, precision=HIGH
        )
        maps = c_whole * maps - reduce_part
        shift_add = jnp.einsum("hcd,hce->hde", c_keys * c_tail, c_base, precision=HIGH)
        return (jnp.stack([maps[0], maps[1] + shift_add]), None)

    block_maps, unused = lax.scan(
        chain_step, jnp.stack([eye_heads, zero_heads]), (keys, w_mat, base, keep, tail, whole)
    )
    every_map, every_shift = (
        lax.all_gather(block_maps[0][None].astype(jnp.bfloat16), "seq", axis=0, tiled=True).astype(
            jnp.float32
        ),
        lax.all_gather(block_maps[1][None].astype(jnp.bfloat16), "seq", axis=0, tiled=True).astype(
            jnp.float32
        ),
    )

    def apply_map(position, state):
        return jnp.where(
            position < seq_place, dotf(every_map[position], state) + every_shift[position], state
        )

    state_in = lax.fori_loop(0, seq_count, apply_map, zero_heads)

    def out_step(state, inputs):
        c_q, c_keys, c_w, c_base, c_keep, c_tail, c_whole, c_incl = inputs
        pseudo = c_base - c_keep * dotf(c_w, state)
        scores = jnp.einsum("hid,hjd->hij", c_q, c_keys, precision=HIGH) * c_incl
        output = c_keep * dotf(c_q, state) + dotf(scores, pseudo)
        new_state = c_whole * state + jnp.einsum(
            "hcd,hce->hde", c_keys * c_tail, pseudo, precision=HIGH
        )
        return (new_state, (output, state))

    last_state, (outputs, block_states) = lax.scan(
        out_step, state_in, (scaled_q, keys, w_mat, base, keep, tail, whole, incl)
    )
    mixed_o = outputs.transpose(0, 2, 1, 3).reshape(seq_len, H, DK)
    head_inv = lax.rsqrt(jnp.mean(mixed_o * mixed_o, -1, keepdims=True) + EPS_HEAD)
    ohat = mixed_o * head_inv
    act_two = (ohat * head_f).reshape(seq_len, width).astype(jnp.bfloat16)
    resid = token_rows + jnp.dot(act_two, w_out, preferred_element_type=jnp.float32)
    inv_two = lax.rsqrt(jnp.mean(resid * resid, -1, keepdims=True) + EPS_NORM)
    rhat = resid * inv_two
    act_three = (rhat * float_gains[1]).astype(jnp.bfloat16)
    gate_up = jnp.dot(act_three, w_gu, preferred_element_type=jnp.float32)
    hidden_units = gate_up.shape[1] // 2
    gate = gate_up[:, :hidden_units]
    up_part = gate_up[:, hidden_units:]
    act_four = (jax.nn.silu(gate) * up_part).astype(jnp.bfloat16)
    mixed = (resid + jnp.dot(act_four, w_down, preferred_element_type=jnp.float32)).astype(
        jnp.bfloat16
    )
    grad_down = tok_dot(act_four, cot_low)
    d_act_four = back_dot(cot_low, w_down)
    d_gate = silu_back(d_act_four * up_part, gate)
    d_up = d_act_four * jax.nn.silu(gate)
    d_gate_up = jnp.concatenate([d_gate, d_up], 1).astype(jnp.bfloat16)
    grad_gate_up = tok_dot(act_three, d_gate_up)
    d_act_three = back_dot(d_gate_up, w_gu)
    grad_gain_two = jnp.sum(d_act_three * rhat, 0)
    residual_gradient = cot_low.astype(jnp.float32) + root_mean_square_backward(
        d_act_three * float_gains[1], rhat, inv_two
    )
    d_resid_low = residual_gradient.astype(jnp.bfloat16)
    grad_out = tok_dot(act_two, d_resid_low)
    d_act_two = back_dot(d_resid_low, w_out).reshape(seq_len, H, DK)
    grad_head = jnp.sum(d_act_two * ohat, (0, 1))
    d_mixed_o = root_mean_square_backward(d_act_two * head_f, ohat, head_inv)
    d_out_groups = d_mixed_o.reshape(n_groups, GROUP, H, DK).transpose(0, 2, 1, 3)

    def state_grad(grad_state, inputs):
        c_q, c_keys, c_scaled, c_inverse, c_keep, c_tail, c_whole, c_incl, c_dout = inputs
        scores = jnp.einsum("hid,hjd->hij", c_q, c_keys, precision=HIGH) * c_incl
        d_pseudo = jnp.einsum("hij,hid->hjd", scores, c_dout, precision=HIGH) + c_tail * dotf(
            c_keys, grad_state
        )
        d_res = jnp.einsum("hij,hid->hjd", c_inverse, d_pseudo, precision=HIGH)
        prior = (
            jnp.einsum("hcd,hce->hde", c_q * c_keep, c_dout, precision=HIGH) + c_whole * grad_state
        )
        return (prior - jnp.einsum("hcd,hce->hde", c_scaled * c_keep, d_res, precision=HIGH), None)

    local_grad, unused = lax.scan(
        state_grad,
        zero_heads,
        (scaled_q, keys, scaled, inverse, keep, tail, whole, incl, d_out_groups),
        reverse=True,
    )
    back_maps = swap_last(block_maps[0])
    every_back, every_grad = (
        lax.all_gather(back_maps[None].astype(jnp.bfloat16), "seq", axis=0, tiled=True).astype(
            jnp.float32
        ),
        lax.all_gather(local_grad[None].astype(jnp.bfloat16), "seq", axis=0, tiled=True).astype(
            jnp.float32
        ),
    )

    def apply_back(step_index, grad_state):
        position = seq_count - 1 - step_index
        return jnp.where(
            position > seq_place,
            dotf(every_back[position], grad_state) + every_grad[position],
            grad_state,
        )

    grad_state_out = lax.fori_loop(0, seq_count, apply_back, zero_heads)

    def full_back(grad_state, inputs):
        (
            c_q,
            c_keys,
            c_values,
            c_rates,
            c_scaled,
            c_inverse,
            c_w,
            c_base,
            c_keep,
            c_tail,
            c_whole,
            c_strict,
            c_incl,
            c_dout,
            c_state,
        ) = inputs
        pseudo = c_base - c_keep * dotf(c_w, c_state)
        scores = jnp.einsum("hid,hjd->hij", c_q, c_keys, precision=HIGH) * c_incl
        d_pseudo = jnp.einsum("hij,hid->hjd", scores, c_dout, precision=HIGH) + c_tail * dotf(
            c_keys, grad_state
        )
        d_res = jnp.einsum("hij,hid->hjd", c_inverse, d_pseudo, precision=HIGH)
        prior = (
            jnp.einsum("hcd,hce->hde", c_q * c_keep, c_dout, precision=HIGH) + c_whole * grad_state
        )
        prior = prior - jnp.einsum("hcd,hce->hde", c_scaled * c_keep, d_res, precision=HIGH)
        d_scores = jnp.einsum("hid,hjd->hij", c_dout, pseudo, precision=HIGH) * c_incl
        d_query = c_keep * dotf(c_dout, swap_last(c_state)) + dotf(d_scores, c_keys)
        d_keys = jnp.einsum("hij,hid->hjd", d_scores, c_q, precision=HIGH) + c_tail * dotf(
            pseudo, swap_last(grad_state)
        )
        d_lower = -jnp.einsum("hid,hjd->hij", d_res, pseudo, precision=HIGH) * c_strict
        d_scaled = -c_keep * dotf(d_res, swap_last(c_state)) + dotf(d_lower, c_keys)
        d_keys = (
            d_keys
            + jnp.einsum("hij,hid->hjd", d_lower, c_scaled, precision=HIGH)
            + c_rates[..., None] * d_scaled
        )
        d_values = c_rates[..., None] * d_res
        d_rates = jnp.sum(d_res * c_values, -1) + jnp.sum(d_scaled * c_keys, -1)
        return (prior, (d_query * scale, d_keys, d_values, d_rates))

    first_grad, (d_q_groups, d_k_groups, d_v_groups, d_rate_groups) = lax.scan(
        full_back,
        grad_state_out,
        (
            scaled_q,
            keys,
            values,
            rates,
            scaled,
            inverse,
            w_mat,
            base,
            keep,
            tail,
            whole,
            strict,
            incl,
            d_out_groups,
            block_states,
        ),
        reverse=True,
    )

    def from_groups(arr):
        return arr.transpose(0, 2, 1, 3).reshape(seq_len, H, DK)

    d_q_unit = from_groups(d_q_groups)
    d_k_unit = from_groups(d_k_groups)
    d_q_raw = q_inv * (d_q_unit - q_unit * jnp.sum(d_q_unit * q_unit, -1, keepdims=True))
    d_k_raw = k_inv * (d_k_unit - k_unit * jnp.sum(d_k_unit * k_unit, -1, keepdims=True))
    d_act = jnp.concatenate(
        [
            d_q_raw.reshape(seq_len, width),
            d_k_raw.reshape(seq_len, width),
            from_groups(d_v_groups).reshape(seq_len, width),
        ],
        1,
    )
    d_pre = silu_back(d_act, pre)
    d_extended = jnp.zeros((seq_len + rim, d_pre.shape[1]), jnp.float32)
    conv_grads = []
    for tap in range(rim + 1):
        masked = d_pre * matches[tap]
        d_extended = d_extended + jnp.pad(conv_f[tap] * masked, ((rim - tap, tap), (0, 0)))
        conv_grads.append(jnp.sum(masked * extended[rim - tap : rim - tap + seq_len], 0))
    grad_conv = jnp.stack(conv_grads)
    rim_back = shifted(d_extended[:rim].astype(jnp.bfloat16), "seq", -1).astype(jnp.float32)
    d_proj = (d_extended[rim:] + jnp.pad(rim_back, ((seq_len - rim, 0), (0, 0)))).astype(
        jnp.bfloat16
    )
    d_rates_tok = d_rate_groups.transpose(0, 2, 1).reshape(seq_len, H)
    d_logits = (d_rates_tok * rates_tok * (1.0 - rates_tok)).astype(jnp.bfloat16)
    grad_qkv = tok_dot(first_activation, d_proj)
    grad_beta = tok_dot(first_activation, d_logits)
    first_activation_gradient = back_dot(d_proj, w_qkv) + back_dot(d_logits, w_beta)
    first_gain_gradient = jnp.sum(first_activation_gradient * normalized_input, 0)
    block_input_gradient = (
        residual_gradient
        + root_mean_square_backward(
            first_activation_gradient * float_gains[0], normalized_input, first_inverse_norm
        )
    ).astype(jnp.bfloat16)
    grad_gains = jnp.stack([first_gain_gradient, grad_gain_two])
    red_qkv, red_beta, red_conv, red_gains, red_head, red_out, red_gu, red_down = (
        lax.psum_scatter(
            grad_qkv.astype(jnp.bfloat16), "seq", scatter_dimension=0, tiled=True
        ).astype(jnp.float32),
        lax.psum_scatter(
            grad_beta.astype(jnp.bfloat16), "seq", scatter_dimension=0, tiled=True
        ).astype(jnp.float32),
        lax.psum_scatter(
            grad_conv.astype(jnp.bfloat16), "seq", scatter_dimension=1, tiled=True
        ).astype(jnp.float32),
        lax.psum_scatter(
            grad_gains.astype(jnp.bfloat16), "seq", scatter_dimension=1, tiled=True
        ).astype(jnp.float32),
        lax.psum_scatter(
            grad_head.astype(jnp.bfloat16), "seq", scatter_dimension=0, tiled=True
        ).astype(jnp.float32),
        lax.psum_scatter(
            grad_out.astype(jnp.bfloat16), "seq", scatter_dimension=0, tiled=True
        ).astype(jnp.float32),
        lax.psum_scatter(
            grad_gate_up.astype(jnp.bfloat16), "seq", scatter_dimension=0, tiled=True
        ).astype(jnp.float32),
        lax.psum_scatter(
            grad_down.astype(jnp.bfloat16), "seq", scatter_dimension=0, tiled=True
        ).astype(jnp.float32),
    )
    red_qkv, red_beta, red_conv, red_gains, red_head, red_out, red_gu, red_down = (
        lax.psum(red_qkv.astype(jnp.bfloat16), "row").astype(jnp.float32),
        lax.psum(red_beta.astype(jnp.bfloat16), "row").astype(jnp.float32),
        lax.psum(red_conv.astype(jnp.bfloat16), "row").astype(jnp.float32),
        lax.psum(red_gains.astype(jnp.bfloat16), "row").astype(jnp.float32),
        lax.psum(red_head.astype(jnp.bfloat16), "row").astype(jnp.float32),
        lax.psum(red_out.astype(jnp.bfloat16), "row").astype(jnp.float32),
        lax.psum(red_gu.astype(jnp.bfloat16), "row").astype(jnp.float32),
        lax.psum(red_down.astype(jnp.bfloat16), "row").astype(jnp.float32),
    )
    return (
        mixed[None],
        block_input_gradient[None],
        red_qkv,
        red_beta,
        red_conv,
        red_gains,
        red_head,
        red_out,
        red_gu,
        red_down,
    )


BF = jnp.bfloat16
F32 = jnp.float32
RIM = 8
NN = (((1,), (0,)), ((), ()))
NT = (((1,), (1,)), ((), ()))
TN = (((0,), (0,)), ((), ()))


def dot_low(a, b, dims=NN):
    return lax.dot_general(a, b, dims, preferred_element_type=F32)


def parts_of(a):
    if a.dtype == BF:
        return (a,)
    high = a.astype(BF)
    return high, (a - high.astype(F32)).astype(BF)


def mm(a, b, dims=NN):
    a_parts, b_parts = parts_of(a), parts_of(b)
    total = dot_low(a_parts[0], b_parts[0], dims)
    if len(b_parts) > 1:
        total = total + dot_low(a_parts[0], b_parts[1], dims)
    if len(a_parts) > 1:
        total = total + dot_low(a_parts[1], b_parts[0], dims)
    return total


def mm1(a, b, dims=NN):
    return dot_low(a.astype(BF), b.astype(BF), dims)


def begin_of(pos, starts_ref):
    begin = jnp.zeros_like(pos)
    for i in range(starts_ref.shape[0]):
        begin = jnp.maximum(begin, jnp.where(pos >= starts_ref[i], starts_ref[i], 0))
    return begin


def begin_at(pos, starts_ref):
    begin = jnp.int32(0)
    for i in range(starts_ref.shape[0]):
        begin = jnp.maximum(begin, jnp.where(starts_ref[i] <= pos, starts_ref[i], 0))
    return begin


def mark_table(chunks, size, taps, starts_ref):
    pos = lax.broadcasted_iota(jnp.int32, (chunks, size), 0) * size
    pos = pos + lax.broadcasted_iota(jnp.int32, (chunks, size), 1)
    rows = begin_of(pos, starts_ref)
    later = [
        ((begin_of(pos + tap, starts_ref) <= pos) & (pos + tap < chunks * size)).astype(F32)
        for tap in range(1, taps)
    ]
    down = lax.broadcasted_iota(jnp.int32, (size, size), 0)
    eye = (down == lax.broadcasted_iota(jnp.int32, (size, size), 1)).astype(BF)
    rows = rows.astype(F32)
    return rows, mm(eye, rows, NT), [mm(eye, v, NT) for v in later]


def chunk_marks(n, size, table, starts_ref):
    first = n * size
    col = table[1][:, n : n + 1]
    last = begin_at(first + size - 1, starts_ref)
    keep = (col < float(first)).astype(F32)
    tail = (col == last.astype(F32)).astype(F32)
    whole = (last < first).astype(F32)
    return col, keep, tail, whole


def chunk_masks(n, size, col, table):
    here = lax.broadcasted_iota(jnp.int32, (size, size), 0)
    there = lax.broadcasted_iota(jnp.int32, (size, size), 1)
    same = col == table[0][n : n + 1]
    return here, there, same & (here > there), same & (here >= there)


def conv_chunk(n, size, pad, conv, col):
    depth = (n * size + lax.broadcasted_iota(jnp.int32, (size, 1), 0)).astype(F32) - col
    pre = conv[0:1, :] * pad[pl.ds(RIM + n * size, size), :]
    for tap in range(1, conv.shape[0]):
        match = (depth >= float(tap)).astype(F32)
        pre = pre + conv[tap : tap + 1, :] * pad[pl.ds(RIM - tap + n * size, size), :] * match
    return pre


def front_kernel(taps, place_ref, starts_ref, *refs):
    n_seq = refs[-1].shape[0]
    n_row = n_seq // 2
    x_ref, got_ref, got_y_ref, got_cores_ref = refs[:4]
    got_refs = (got_ref, got_cores_ref.at[0], got_y_ref, got_cores_ref.at[1])
    (
        weight_ref,
        act1_ref,
        proj_ref,
        rates_ref,
        o_ref,
        act2_ref,
        inv_ref,
        w_ref,
        att_ref,
        p_ref,
        u_ref,
        s_ref,
        conv_ref,
        gains_ref,
        beta_ref,
        head_ref,
        pad,
        lower,
        tmp,
        q_scr,
        k_scr,
        v_scr,
        add,
    ) = refs[4:]
    place, row = place_ref[0], place_ref[1]
    size = s_ref.shape[1]
    part_rows = size // n_row
    dk = o_ref.shape[1]
    base = 3 * part_rows
    gains = jnp.concatenate([got_ref[s, base + 4 : base + 6, :] for s in range(n_seq)], 1).astype(F32)
    gains_ref[...] = jnp.zeros_like(gains_ref)
    gains_ref[0:2, :] = gains
    beta = jnp.concatenate([got_ref[s, base + 8 : base + 16, :] for s in range(n_seq)], 1)
    beta_ref[...] = beta
    head_gain = got_ref[0, base + 6 : base + 7, :].astype(F32)
    for s in range(1, n_seq):
        head_gain = head_gain + got_ref[s, base + 6 : base + 7, :].astype(F32)
    head_ref[...] = jnp.broadcast_to(head_gain, head_ref.shape)
    conv_parts = []
    for part in range(3):
        block = part * n_seq + place
        shard = block // 3
        offset = pl.multiple_of(base + (block - shard * 3) * 16, 16)
        conv_parts.append(got_ref[shard, pl.ds(offset, 16), :][0:8])
    conv = jnp.concatenate(conv_parts, 1).astype(F32)
    conv_ref[...] = conv
    conv = conv[0:taps]
    for m, ref in enumerate(got_refs):
        for s in range(n_seq):
            at = pl.multiple_of(s * size + (row ^ m) * part_rows, part_rows)
            for kind in range(3):
                block = ref[s, kind * part_rows : (kind + 1) * part_rows, :]
                weight_ref[pl.ds(at, part_rows), kind * dk : (kind + 1) * dk] = block
    weight = weight_ref[...]
    lanes = lax.broadcasted_iota(jnp.int32, (2 * size, 8), 1)
    pad[0:RIM, :] = jnp.zeros((RIM, 3 * dk), F32)
    for n in range(0, n_seq, 2):
        rows_at = pl.ds(n * size, 2 * size)
        rows = x_ref[rows_at, :].astype(F32)
        inv = lax.rsqrt(jnp.mean(rows * rows, -1, keepdims=True) + EPS_NORM)
        act = ((rows * inv) * gains[0:1]).astype(BF)
        act1_ref[rows_at, :] = act
        proj = dot_low(act, weight).astype(BF)
        proj_ref[rows_at, :] = proj
        pad[pl.ds(RIM + n * size, 2 * size), :] = proj.astype(F32)
        logits = dot_low(act, beta, NT)
        rate = jax.nn.sigmoid(jnp.sum(jnp.where(lanes == place, logits, 0.0), 1, keepdims=True))
        rates_ref[rows_at, :] = jnp.broadcast_to(rate, (2 * size, dk))
    table = mark_table(n_seq, size, taps, starts_ref)
    marks = []
    for n in range(n_seq):
        at = n * size
        col, keep, tail, whole = chunk_marks(n, size, table, starts_ref)
        marks.append((keep, tail, whole))
        pre = conv_chunk(n, size, pad, conv, col)
        act = pre * jax.nn.sigmoid(pre)
        q_raw, k_raw, v_raw = act[:, :dk], act[:, dk : 2 * dk], act[:, 2 * dk :]
        q = (q_raw * lax.rsqrt(jnp.sum(q_raw * q_raw, -1, keepdims=True) + EPS_UNIT)).astype(BF)
        key = (k_raw * lax.rsqrt(jnp.sum(k_raw * k_raw, -1, keepdims=True) + EPS_UNIT)).astype(BF)
        q_scr[pl.ds(at, size), :] = q
        k_scr[pl.ds(at, size), :] = key
        v_scr[pl.ds(at, size), :] = v_raw.astype(BF)
        here, there, strict, incl = chunk_masks(n, size, col, table)
        rate = rates_ref[pl.ds(at, size), :]
        low = jnp.where(strict, dot_low(key, key, NT) * rate, 0.0)
        att_ref[n] = jnp.where(incl, dot_low(q, key, NT) * (dk**-0.5), 0.0)
        lower[n] = low
        eye = (here == there).astype(F32)
        inv_ref[n] = eye - jnp.where((here // 2) == (there // 2), low, 0.0)
    span = 2
    while span < size:
        here = lax.broadcasted_iota(jnp.int32, (size, size), 0)
        there = lax.broadcasted_iota(jnp.int32, (size, size), 1)
        cross = ((here // (2 * span)) == (there // (2 * span))) & ((here // span) != (there // span))
        for n in range(n_seq):
            tmp[n] = mm(inv_ref[n], jnp.where(cross, lower[n], 0.0))
        for n in range(n_seq):
            inv_ref[n] = inv_ref[n] - mm(tmp[n], inv_ref[n])
        span *= 2
    for n in range(n_seq):
        keep, tail, whole = marks[n]
        rows = pl.ds(n * size, size)
        rate = rates_ref[rows, :]
        key = k_scr[rows, :]
        inv = inv_ref[n]
        w = mm(inv, rate * key.astype(F32))
        base = mm(inv, rate * v_scr[rows, :].astype(F32))
        w_ref[n] = w
        u_ref[n] = base
        p_ref[n] = mm(key, (tail * keep) * w, TN)
        add[n] = mm(key, tail * base, TN)
    state = jnp.zeros((dk, dk), F32)
    for n in range(n_seq):
        s_ref[n] = state
        if n + 1 < n_seq:
            state = marks[n][2] * state - mm(p_ref[n], state) + add[n]
    for n in range(n_seq):
        keep, tail, whole = marks[n]
        rows = pl.ds(n * size, size)
        state = s_ref[n]
        u = u_ref[n] - keep * mm(w_ref[n], state)
        u_ref[n] = u
        out = (keep * (dk**-0.5)) * mm(q_scr[rows, :], state) + mm(att_ref[n], u)
        o_ref[rows, :] = out
        inv = lax.rsqrt(jnp.mean(out * out, -1, keepdims=True) + EPS_HEAD)
        act2_ref[n] = ((out * inv) * head_gain).astype(BF)


def back_kernel(taps, place_ref, starts_ref, *refs):
    (
        dact_ref,
        o_ref,
        head_ref,
        conv_ref,
        proj_ref,
        rates_ref,
        inv_ref,
        w_ref,
        att_ref,
        p_ref,
        u_ref,
        s_ref,
        weight_ref,
        beta_ref,
        dproj_ref,
        part_ref,
        dlog_ref,
        gconv_ref,
        ghead_ref,
        logit_scr,
        pad,
        pre_scr,
        dpre,
        do_scr,
        g_scr,
        add,
        x_scr,
        q_scr,
        k_scr,
    ) = refs
    n_seq, size, dk = dact_ref.shape
    scale = dk**-0.5
    place = place_ref[0]
    beta_all = beta_ref[...].astype(F32)
    beta_lane = lax.broadcasted_iota(jnp.int32, beta_all.shape, 0) == place
    beta_row = jnp.sum(jnp.where(beta_lane, beta_all, 0.0), 0, keepdims=True)
    head_gain = head_ref[0:1, :]
    conv = conv_ref[0:taps, :]
    total = n_seq * size
    pad[0:RIM, :] = jnp.zeros((RIM, 3 * dk), F32)
    pad[pl.ds(RIM, total), :] = proj_ref[...].astype(F32)
    dpre[pl.ds(total, RIM), :] = jnp.zeros((RIM, 3 * dk), F32)
    table = mark_table(n_seq, size, taps, starts_ref)
    marks = []
    ghead = jnp.zeros((1, dk), F32)
    for n in range(n_seq):
        rows = pl.ds(n * size, size)
        col, keep, tail, whole = chunk_marks(n, size, table, starts_ref)
        marks.append((col, keep, tail, whole))
        pre = conv_chunk(n, size, pad, conv, col)
        pre_scr[rows, :] = pre
        act = pre * jax.nn.sigmoid(pre)
        q_raw, k_raw = act[:, :dk], act[:, dk : 2 * dk]
        q = (q_raw * lax.rsqrt(jnp.sum(q_raw * q_raw, -1, keepdims=True) + EPS_UNIT)).astype(BF)
        key = (k_raw * lax.rsqrt(jnp.sum(k_raw * k_raw, -1, keepdims=True) + EPS_UNIT)).astype(BF)
        q_scr[rows, :] = q
        k_scr[rows, :] = key
        out = o_ref[rows, :]
        inv = lax.rsqrt(jnp.mean(out * out, -1, keepdims=True) + EPS_HEAD)
        ohat = out * inv
        d_act2 = dact_ref[n].astype(F32)
        ghead = ghead + jnp.sum(d_act2 * ohat, 0, keepdims=True)
        lean = d_act2 * head_gain
        d_out = inv * (lean - ohat * jnp.mean(lean * ohat, -1, keepdims=True))
        do_scr[rows, :] = d_out
        g_scr[rows, :] = mm(att_ref[n], d_out, TN)
    ghead_ref[...] = jnp.broadcast_to(ghead, ghead_ref.shape)
    for n in range(n_seq):
        rows = pl.ds(n * size, size)
        col, keep, tail, whole = marks[n]
        add[n] = mm(q_scr[rows, :], (scale * keep) * do_scr[rows, :], TN) - mm(w_ref[n], keep * g_scr[rows, :], TN)
    grad = jnp.zeros((dk, dk), F32)
    for n in range(n_seq - 1, -1, -1):
        x_scr[n] = grad
        if n > 0:
            grad = marks[n][3] * grad - mm(p_ref[n], grad, TN) + add[n]
    gconv = [jnp.zeros((1, 3 * dk), F32) for _ in range(taps)]
    for n in range(n_seq - 1, -1, -1):
        rows = pl.ds(n * size, size)
        col, keep, tail, whole = marks[n]
        here, there, strict, incl = chunk_masks(n, size, col, table)
        rate = rates_ref[rows, :]
        key, q = k_scr[rows, :], q_scr[rows, :]
        key_f, q_f = key.astype(F32), q.astype(F32)
        pre = pre_scr[rows, :]
        sig = jax.nn.sigmoid(pre)
        act = pre * sig
        value = act[:, 2 * dk :].astype(BF).astype(F32)
        grad, state, u = x_scr[n], s_ref[n], u_ref[n]
        d_out = do_scr[rows, :]
        d_u = g_scr[rows, :] + tail * mm(key, grad)
        d_r = mm(inv_ref[n], d_u, TN)
        d_att = jnp.where(incl, mm(d_out, u, NT), 0.0)
        d_low = jnp.where(strict, -mm(d_r, u, NT), 0.0)
        d_q = keep * mm(d_out, state, NT) + mm(d_att, key)
        d_kb = mm(d_low, key) - keep * mm(d_r, state, NT)
        d_k = (
            scale * mm(d_att, q, TN)
            + mm(d_low, rate * key_f, TN)
            + tail * mm(u, grad, NT)
            + rate * d_kb
        )
        d_v = rate * d_r
        d_rate = jnp.sum(d_r * value + d_kb * key_f, -1, keepdims=True)
        d_q = d_q * scale
        q_raw, k_raw = act[:, :dk], act[:, dk : 2 * dk]
        q_inv = lax.rsqrt(jnp.sum(q_raw * q_raw, -1, keepdims=True) + EPS_UNIT)
        k_inv = lax.rsqrt(jnp.sum(k_raw * k_raw, -1, keepdims=True) + EPS_UNIT)
        q_unit, k_unit = q_raw * q_inv, k_raw * k_inv
        d_q = q_inv * (d_q - q_unit * jnp.sum(d_q * q_unit, -1, keepdims=True))
        d_k = k_inv * (d_k - k_unit * jnp.sum(d_k * k_unit, -1, keepdims=True))
        d_act = jnp.concatenate([d_q, d_k, d_v], 1)
        d_pre = d_act * sig * (1.0 + pre * (1.0 - sig))
        dpre[rows, :] = d_pre
        depth = (n * size + lax.broadcasted_iota(jnp.int32, (size, 1), 0)).astype(F32) - col
        d_proj = conv[0:1, :] * d_pre
        gconv[0] = gconv[0] + jnp.sum(d_pre * pad[pl.ds(RIM + n * size, size), :], 0, keepdims=True)
        for tap in range(1, taps):
            match = table[2][tap - 1][:, n : n + 1]
            d_proj = d_proj + conv[tap : tap + 1, :] * dpre[pl.ds(n * size + tap, size), :] * match
            reach = (depth >= float(tap)).astype(F32)
            gconv[tap] = gconv[tap] + jnp.sum(
                d_pre * reach * pad[pl.ds(RIM - tap + n * size, size), :], 0, keepdims=True
            )
        d_proj = d_proj.astype(BF)
        dproj_ref[rows, :] = d_proj
        one_rate = rate[:, 0:1]
        d_logit = (d_rate * one_rate * (1.0 - one_rate)).astype(BF).astype(F32)
        logit_scr[rows, :] = jnp.broadcast_to(d_logit, (size, dk))
        dlog_ref[pl.ds(n, 1), :] = jnp.broadcast_to(d_logit, (size, dk)).T[0:1]
    for n in range(0, n_seq, 2):
        rows = pl.ds(n * size, 2 * size)
        d_act1 = dot_low(dproj_ref[rows, :], weight_ref[...], NT) + logit_scr[rows, 0:1] * beta_row
        part_ref[rows, :] = d_act1.astype(BF)
    gconv_ref[...] = jnp.zeros_like(gconv_ref)
    for tap in range(taps):
        gconv_ref[tap : tap + 1, :] = gconv[tap]


def lead_kernel(place_ref, qkv_ref, conv_ref, gains_ref, head_ref, beta_ref, out_ref, rows):
    place, row = place_ref[0], place_ref[1]
    heads, dk = out_ref.shape[0], out_ref.shape[2]
    part = dk // 4
    from_row = pl.ds(pl.multiple_of(row * part, part), part)
    per = head_ref.shape[1]
    down = lax.broadcasted_iota(jnp.int32, (dk, dk), 0)
    along = lax.broadcasted_iota(jnp.int32, (dk, dk), 1)
    spot = (along == down + place * per)[0:per].astype(BF)
    rows[...] = jnp.zeros_like(rows)
    taps = conv_ref.shape[0]
    for kind in range(3):
        rows[kind * 16 : kind * 16 + taps, :] = conv_ref[:, kind * dk : (kind + 1) * dk].astype(F32)
    rows[4:6, :] = gains_ref[...].astype(F32)
    rows[6:7, :] = dot_low(jnp.broadcast_to(head_ref[...], (16, per)), spot)[0:1]
    rows[8:16, :] = beta_ref[...].astype(F32)
    small = rows[...].astype(BF)
    for h in range(heads):
        for kind in range(3):
            block = qkv_ref[from_row, pl.ds((kind * heads + h) * dk, dk)]
            out_ref[h, kind * part : (kind + 1) * part, :] = block
        out_ref[h, 3 * part : 3 * part + 48, :] = small


SLOT = 96


def columns_kernel(place_ref, gu_ref, down_ref, own_ref, other_ref, rows_ref, wide_own, wide_other):
    side, row = lax.rem(place_ref[0], 2), place_ref[1]
    size, lanes = gu_ref.shape[0], own_ref.shape[1]
    hidden = down_ref.shape[0]
    part, wide = hidden // 4, wide_own.shape[1] // 2
    for ref in (wide_own, wide_other):
        for kind in range(2):
            ref[:, kind * wide + wide - 128 : (kind + 1) * wide] = jnp.zeros((size, 128), F32)

    def take(x, r):
        for ref, block in ((wide_own, x), (wide_other, 1 - x)):
            for kind in range(2):
                for z in range(4):
                    at = (kind * 8 + z * 2 + block) * hidden + r * part
                    to = kind * wide + z * part
                    ref[:, to : to + part] = gu_ref[:, at : at + part].astype(F32)
        for j in range(down_ref.shape[1] // lanes):
            block = down_ref[r * part : (r + 1) * part, j * lanes : (j + 1) * lanes].astype(F32)
            block = jnp.concatenate([block, jnp.zeros((SLOT - part, lanes), F32)], 0)
            rows_ref[j * SLOT : (j + 1) * SLOT, :] = block.astype(BF)

    for x in range(2):
        for r in range(4):
            pl.when((side == x) & (row == r))(functools.partial(take, x, r))
    for ref, out in ((wide_own, own_ref), (wide_other, other_ref)):
        for j in range(2 * wide // lanes):
            out[j * size : (j + 1) * size, :] = ref[:, j * lanes : (j + 1) * lanes].astype(BF)


def mid_kernel(place_ref, act2_ref, own_ref, y_ref, cores_ref, x_ref, gains_ref, resid_ref, act3_ref, weight_ref):
    row = place_ref[1]
    heads, size, dk = act2_ref.shape
    part = dk // 4
    for m in range(4):
        ref = (own_ref, cores_ref.at[0], y_ref, cores_ref.at[1])[m]
        for s in range(heads):
            at = pl.multiple_of((s * 4 + (row ^ m)) * part, part)
            weight_ref[pl.ds(at, part), :] = ref[s]
    act2 = jnp.concatenate([act2_ref[h] for h in range(heads)], 1)
    resid = x_ref[...].astype(F32) + dot_low(act2, weight_ref[...])
    resid_ref[...] = resid
    inv = lax.rsqrt(jnp.mean(resid * resid, -1, keepdims=True) + EPS_NORM)
    act3_ref[...] = ((resid * inv) * gains_ref[1:2, :]).astype(BF)


GROUP_BITS = (0, 2, 4, 6, 1, 3, 5, 7)


def store_part(bits, block, own_ref, next_ref):
    @pl.when((bits & 1) == 0)
    def _():
        own_ref[bits >> 1] = block

    @pl.when((bits & 1) == 1)
    def _():
        next_ref[bits >> 1] = block


def mixed_kernel(place_ref, act4_ref, down_ref, own_ref, next_ref):
    me = lax.rem(place_ref[0], 2) * 4 + place_ref[1]
    size = own_ref.shape[1]
    for i in range(4):
        parts = dot_low(act4_ref[pl.ds(i * 2 * size, 2 * size), :], down_ref[...]).astype(BF)
        for half in range(2):
            store_part(me ^ (2 * i + half), parts[half * size : (half + 1) * size], own_ref, next_ref)


def feed_kernel(hidden, place_ref, *refs):
    act3_refs, core_ref, cot_refs, cot_core_ref, packs_ref = refs[0:4], refs[4], refs[5:9], refs[9], refs[10]
    own_ref, next_ref, act4_ref, dgu_ref, act3_ref, cot_ref, down_ref, gu, down32 = refs[11:]
    place, row = place_ref[0], place_ref[1]
    side = lax.rem(place, 2)
    me = side * 4 + row
    size, width = act3_refs[0].shape
    wide = act4_ref.shape[1]
    lanes = packs_ref.shape[2]
    slot, part = 96, hidden // 4
    gu_rows = gu.shape[0] // 4
    n_cols = gu.shape[1] // lanes
    down32[hidden:wide, :] = jnp.zeros((wide - hidden, width), F32)

    for src in range(4):
        for i in range(2):
            shard = src * 2 + (side if i == 0 else 1 - side)
            rows = pl.ds(pl.multiple_of(shard * size, size), size)
            for j in range(n_cols):
                from_rows = pl.ds((i * n_cols + j) * size, size)
                gu[rows, j * lanes : (j + 1) * lanes] = packs_ref[src, from_rows, :]
        for j in range(width // lanes):
            block = packs_ref[src, pl.ds(n_cols * gu_rows + j * slot, slot), :].astype(F32)
            down32[src * part : (src + 1) * part, j * lanes : (j + 1) * lanes] = block[0:part]
    down_ref[...] = down32[...].astype(BF)
    for i, bits in enumerate(GROUP_BITS):
        at = pl.multiple_of((me ^ bits) * size, size)
        act3_ref[pl.ds(at, size), :] = act3_refs[i][...] if i < 4 else core_ref[i - 4]
        cot_ref[pl.ds(at, size), :] = cot_refs[i][...] if i < 4 else cot_core_ref[i - 4]
    for i in range(4):
        rows = pl.ds(i * 2 * size, 2 * size)
        act3 = act3_ref[rows, :]
        cot = cot_ref[rows, :]
        gate_up = dot_low(act3, gu[...])
        gate, up = gate_up[:, :wide], gate_up[:, wide:]
        sig = jax.nn.sigmoid(gate)
        silu = gate * sig
        act4_ref[rows, :] = (silu * up).astype(BF)
        d_act4 = dot_low(cot, down_ref[...], NT)
        d_gate = d_act4 * up * sig * (1.0 + gate * (1.0 - sig))
        d_gu = jnp.concatenate([d_gate, d_act4 * silu], 1).astype(BF)
        dgu_ref[rows, :] = d_gu
        parts = dot_low(d_gu, gu[...], NT).astype(BF)
        for half in range(2):
            store_part(me ^ (2 * i + half), parts[half * size : (half + 1) * size], own_ref, next_ref)


def grads_kernel(hidden, place_ref, act3_ref, cot_ref, act4_ref, dgu_ref, out_ref, down32):
    side = lax.rem(place_ref[0], 2)
    lanes = out_ref.shape[2]
    slot, part = 96, hidden // 4
    gu_rows = act3_ref.shape[1] // 4
    n_cols = dgu_ref.shape[1] // lanes
    down32[...] = dot_low(act4_ref[...], cot_ref[...], TN)
    for k in range(4):
        at = k * gu_rows
        grad = dot_low(act3_ref[:, at : at + gu_rows], dgu_ref[...], TN).astype(BF)
        size = gu_rows // 2
        for parity in range(2):
            first = jnp.where(side == parity, 0, n_cols * size)
            for j in range(n_cols):
                rows = pl.ds(pl.multiple_of(first + j * size, size), size)
                out_ref[k, rows, :] = grad[parity * size : (parity + 1) * size, j * lanes : (j + 1) * lanes]
        rows = pl.ds(k * part, part)
        for j in range(cot_ref.shape[1] // lanes):
            block = down32[rows, j * lanes : (j + 1) * lanes]
            block = jnp.concatenate([block, jnp.zeros((slot - part, lanes), F32)], 0)
            out_ref[k, pl.ds(n_cols * gu_rows + j * slot, slot), :] = block.astype(BF)


def out_grad_kernel(place_ref, act2_ref, low_ref, same_ref, other_ref, full):
    row = place_ref[1]
    heads, _, dk = act2_ref.shape
    part = dk // 4
    for h in range(heads):
        full[h * dk : (h + 1) * dk, :] = dot_low(act2_ref[h], low_ref[...], TN)
    for m in range(4):
        ref = same_ref if m % 2 == 0 else other_ref
        for h in range(heads):
            at = pl.multiple_of(h * dk + (row ^ m) * part, part)
            ref[m // 2, h] = full[pl.ds(at, part), :].astype(BF)


def qkv_grad_kernel(place_ref, act1_ref, dproj_ref, dlog_ref, gconv_ref, ghead_ref, same_ref, other_ref, full, rows):
    row = place_ref[1]
    shards, total, cols = same_ref.shape[1:]
    dk = cols // 3
    part = total - 16
    for h in range(shards):
        lanes = pl.ds(h * dk, dk)
        full[h * dk : (h + 1) * dk, :] = dot_low(act1_ref[:, lanes], dproj_ref[...], TN)
    g_beta = None
    dlog = dlog_ref[...].astype(BF)
    for n in range(dlog.shape[0]):
        one = jnp.broadcast_to(dlog[n : n + 1], (16, dk))
        term = dot_low(one, act1_ref[n * dk : (n + 1) * dk, :])[0:1]
        g_beta = term if g_beta is None else g_beta + term
    rows[...] = jnp.zeros_like(rows)
    for s in range(shards):
        rows[s, 0:4, :] = gconv_ref[0:4, :]
        rows[s, 4:5, 0:dk] = g_beta[:, s * dk : (s + 1) * dk]
        rows[s, 4:5, dk : 2 * dk] = ghead_ref[0:1, :]
    for m in range(4):
        ref = same_ref if m % 2 == 0 else other_ref
        for s in range(shards):
            at = pl.multiple_of(s * dk + (row ^ m) * part, part)
            ref[m // 2, s, 0:part, :] = full[pl.ds(at, part), :].astype(BF)
            ref[m // 2, s, pl.ds(part, 16), :] = rows[s].astype(BF)


def turn_kernel(heads, own_ref, core_ref, x_ref, y_ref, top_ref, bottom_ref, resid_ref, cot_ref, gains_ref, weight_ref, dresid_ref, low_ref, dact2_ref):
    resid = resid_ref[...]
    inv = lax.rsqrt(jnp.mean(resid * resid, -1, keepdims=True) + EPS_NORM)
    rhat = resid * inv
    d_act3 = own_ref[0].astype(F32) + core_ref[0].astype(F32)
    d_act3 = d_act3 + jnp.concatenate([x_ref[0], y_ref[0]], 0).astype(F32)
    d_act3 = d_act3 + jnp.concatenate([top_ref[...], bottom_ref[...]], 0).astype(F32)
    lean = d_act3 * gains_ref[1:2, :]
    d_resid = cot_ref[...].astype(F32) + inv * (lean - rhat * jnp.mean(lean * rhat, -1, keepdims=True))
    dresid_ref[...] = d_resid
    low = d_resid.astype(BF)
    low_ref[...] = low
    d_act2 = dot_low(low, weight_ref[...], NT).astype(BF)
    dk = d_act2.shape[1] // heads
    for h in range(heads):
        dact2_ref[h] = d_act2[:, h * dk : (h + 1) * dk]


def last_kernel(part_ref, x_ref, gains_ref, dresid_ref, out_ref):
    d_act1 = part_ref[...].astype(F32)
    rows = x_ref[...].astype(F32)
    inv = lax.rsqrt(jnp.mean(rows * rows, -1, keepdims=True) + EPS_NORM)
    xhat = rows * inv
    lean = d_act1 * gains_ref[0:1, :]
    out = dresid_ref[...] + inv * (lean - xhat * jnp.mean(lean * xhat, -1, keepdims=True))
    out_ref[...] = out.astype(BF)


def row_sums(v):
    total = jnp.sum(v, 1, keepdims=True)
    return jnp.broadcast_to(total, (v.shape[0], 128)).T[0:1]


def lay_feed_kernel(place_ref, *refs):
    own_ref, y_ref, cores_ref = refs[0:3]
    packs = (own_ref, cores_ref.at[0], y_ref, cores_ref.at[1])
    weight_ref, gain_ref, gu_out, down_out, gain_out, held = refs[3:]
    side, row = lax.rem(place_ref[0], 2), place_ref[1]
    size, hidden = gain_out.shape[1], down_out.shape[0]
    lanes, slot, part = packs[0].shape[1], 96, hidden // 4
    wide = held.shape[3] // 2
    n_cols = held.shape[3] // lanes
    for m in range(4):
        for own in range(2):
            block = side if own == 0 else 1 - side
            for j in range(n_cols):
                rows = pl.ds((own * n_cols + j) * size, size)
                held[row ^ m, block, :, j * lanes : (j + 1) * lanes] = packs[m][rows, :]
        at = pl.multiple_of((row ^ m) * part, 8)
        for j in range(down_out.shape[1] // lanes):
            block = packs[m][pl.ds(2 * n_cols * size + j * slot, slot), :].astype(F32)
            down_out[pl.ds(at, part), j * lanes : (j + 1) * lanes] = block[0:part]
    total = None
    for kind in range(2):
        for m in range(4):
            for x in range(2):
                for z in range(4):
                    at = kind * wide + z * part
                    piece = held[m, x, :, at : at + part].astype(F32)
                    to = (kind * 8 + z * 2 + x) * hidden + m * part
                    gu_out[:, to : to + part] = piece
                    term = piece * weight_ref[:, to : to + part].astype(F32)
                    total = term if total is None else total + term
    gain_out[...] = row_sums(total) / gain_ref[1:2, :].astype(F32)


def lay_mix_kernel(place_ref, *refs):
    qkv_refs = (refs[0], refs[2].at[0], refs[1], refs[2].at[1])
    out_refs = (refs[3], refs[5].at[0], refs[4], refs[5].at[1])
    weight_ref, beta_ref, gain_ref, second_ref, qkv_out, out_out, gain_out, conv_out, beta_out, head_out = refs[6:]
    place, row = place_ref[0], place_ref[1]
    heads, total, cols = qkv_refs[0].shape
    dk = cols // 3
    part = total - 16
    for m in range(4):
        rows = pl.ds(pl.multiple_of((row ^ m) * part, 8), part)
        out_out[rows, :] = out_refs[m][...].astype(F32)
        for h in range(heads):
            for kind in range(3):
                lanes = pl.ds((kind * heads + h) * dk, dk)
                block = qkv_refs[m][h, 0:part, kind * dk : (kind + 1) * dk]
                qkv_out[rows, lanes] = block.astype(F32)
    sums = jnp.sum(qkv_out[...] * weight_ref[...].astype(F32), 1, keepdims=True)
    ref = qkv_refs[0]
    small = [ref[h, pl.ds(part, 16), :].astype(F32) for h in range(heads)]
    beta_rows = jnp.concatenate([v[4:5, 0:dk] for v in small], 0)
    beta_out[...] = beta_rows
    head = small[0][4:5, dk : 2 * dk]
    for v in small[1:]:
        head = head + v[4:5, dk : 2 * dk]
    per = head_out.shape[1]
    spot = lax.broadcasted_iota(jnp.int32, (dk, per), 0) == (
        lax.broadcasted_iota(jnp.int32, (dk, per), 1) + place * per
    )
    head_out[...] = mm(jnp.broadcast_to(head, (8, dk)), spot.astype(BF))[0:1]
    for i in range(3):
        block = place * 3 + i
        kind = block // heads
        source = block - kind * heads
        lanes = pl.ds(pl.multiple_of(kind * dk, dk), dk)
        conv_out[:, i * dk : (i + 1) * dk] = ref[source, pl.ds(part, 16), lanes].astype(F32)[0 : conv_out.shape[0]]
    weight_rows = beta_ref[...].astype(F32)
    gain = jnp.broadcast_to(sums, (sums.shape[0], 128)).T[0:1]
    gain = gain + jnp.sum(beta_rows * weight_rows, 0, keepdims=True)
    gain_out[0:1, :] = gain / gain_ref[0:1, :].astype(F32)
    gain_out[1:2, :] = second_ref[...]


def local_call(kernel, outs, args, scratch=(), smem=0, us=1, mib=56, name=None):
    space = [pl.BlockSpec(memory_space=pltpu.SMEM)] * smem
    space += [pl.BlockSpec(memory_space=pltpu.VMEM)] * (len(args) - smem)
    return pl.pallas_call(
        kernel,
        out_shape=tuple(outs),
        in_specs=space,
        out_specs=tuple(pl.BlockSpec(memory_space=pltpu.VMEM) for _ in outs),
        scratch_shapes=list(scratch),
        compiler_params=pltpu.CompilerParams(vmem_limit_bytes=mib * 2**20),
        cost_estimate=pl.CostEstimate(flops=us * 10**9, bytes_accessed=1024, transcendentals=0),
        name=name,
    )(*args)


def head_plan(
    block_input,
    cotangent,
    doc_starts,
    qkv_weight,
    beta_weight,
    conv_weight,
    norm_gains,
    head_gain,
    out_weight,
    gate_up_weight,
    down_weight,
):
    x, cot = block_input[0], cotangent[0]
    starts = doc_starts[0]
    size, width = x.shape
    n_seq, n_row = lax.axis_size("seq"), lax.axis_size("row")
    place, row = lax.axis_index("seq"), lax.axis_index("row")
    half = n_seq // 2
    z, side = place // 2, place % 2
    total = n_seq * size
    where_at = jnp.stack([place, row])
    taps = conv_weight.shape[0]
    hidden = down_weight.shape[0]
    wide = -(-hidden // 128) * 128
    shape = jax.ShapeDtypeStruct

    def flip(v):
        return lax.ppermute(v, "seq", [(s, s ^ 1) for s in range(n_seq)])

    def roll(v, k):
        return lax.ppermute(v, "seq", [(s, (s // 2 + k) % half * 2 + s % 2) for s in range(n_seq)])

    def core(v):
        return lax.ppermute(v, "row", [(r, r ^ 1) for r in range(n_row)])

    def across(v):
        return lax.ppermute(v, "row", [(r, r ^ 2) for r in range(n_row)])

    def group_gather(v):
        y, s = across(v), flip(v)
        four = [v, y, s, flip(y)]
        return [*four, core(jnp.stack(four))]

    def row_sum(same, other):
        mine = same.astype(F32) + core(other).astype(F32)
        return mine[0], mine[1].astype(BF)

    def row_relative(v):
        y = across(v)
        return [v, core(v), y, core(y)]

    def stage(*values):
        return lax.optimization_barrier(values)

    def line(v, step, t):
        ends = range(t - 1, half - 1) if step > 0 else range(1, half - t + 1)
        return lax.ppermute(
            v, "seq", [(2 * a + j, 2 * (a + step) + j) for a in ends for j in range(2)]
        )

    part_rows = size // n_row
    dk = width // n_seq
    lead_rows = 3 * part_rows + 48
    row_x = lax.all_gather(x, "seq", tiled=True)
    (payload,) = local_call(
        lead_kernel,
        [shape((n_seq, lead_rows, dk), BF)],
        [where_at, qkv_weight, conv_weight, norm_gains, head_gain.reshape(1, -1), beta_weight.T],
        scratch=[pltpu.VMEM((48, dk), F32)],
        smem=1,
        us=2,
        name="lead",
    )

    rows3 = shape((3 * size, 256), BF)
    pack_rows = 6 * size + 4 * SLOT
    own_cols, other_cols, down_rows = local_call(
        columns_kernel,
        [rows3, rows3, shape((4 * SLOT, 256), BF)],
        [where_at, gate_up_weight, down_weight],
        scratch=[pltpu.VMEM((size, 2 * wide), F32)] * 2,
        smem=1,
        us=2,
        name="columns",
    )
    pack = jnp.concatenate([own_cols, flip(other_cols), down_rows], 0)
    got = lax.all_to_all(payload, "seq", 0, 0)
    got_y = across(got)
    got_cores = core(jnp.stack([got, got_y]))
    out_part = lax.dynamic_slice_in_dim(out_weight, row * part_rows, part_rows, 0)
    out_part = jnp.broadcast_to(out_part[None], (n_seq, part_rows, width))
    groups_z = [[2 * a + j for a in range(half)] for j in range(2)]
    packs = lax.all_gather(pack, "seq", axis_index_groups=groups_z)
    out_part = lax.all_to_all(stage(out_part, pack)[0], "seq", 0, 0)
    row_x, got, got_y, got_cores, out_part, cot, _ = stage(row_x, got, got_y, got_cores, out_part, cot, pack)
    cot_y, cot_x = across(cot), flip(cot)
    out_y = across(out_part)
    square = shape((n_seq, size, dk), F32)
    (
        w_head,
        act1,
        proj,
        rates,
        outs,
        act2,
        inverse,
        w_mat,
        att,
        p_mat,
        u_mat,
        states,
        conv,
        gains,
        beta,
        head,
    ) = local_call(
        functools.partial(front_kernel, taps),
        [
            shape((width, 3 * dk), BF),
            shape((total, width), BF),
            shape((total, 3 * dk), BF),
            shape((total, dk), F32),
            shape((total, dk), F32),
            shape((n_seq, size, dk), BF),
            square,
            square,
            square,
            square,
            square,
            square,
            shape((8, 3 * dk), F32),
            shape((8, width), F32),
            shape((8, width), BF),
            shape((8, dk), F32),
        ],
        [where_at, starts, row_x, got, got_y, got_cores],
        scratch=[
            pltpu.VMEM((RIM + total, 3 * dk), F32),
            pltpu.VMEM((n_seq, size, size), F32),
            pltpu.VMEM((n_seq, size, size), F32),
            pltpu.VMEM((total, dk), BF),
            pltpu.VMEM((total, dk), BF),
            pltpu.VMEM((total, dk), BF),
            pltpu.VMEM((n_seq, dk, dk), F32),
        ],
        smem=2,
        us=4,
        name="front",
    )
    act2, cot_y, cot_x, out_y = stage(act2, cot_y, cot_x, out_y)
    act2 = lax.all_to_all(act2, "seq", 0, 0)
    cot_four = [cot, cot_y, cot_x, flip(cot_y)]
    out_cores = core(jnp.stack([out_part, out_y]))
    act2, out_cores, cot_four[3] = stage(act2, out_cores, cot_four[3])
    cot_all = [*cot_four, core(jnp.stack(cot_four))]
    resid, act3, w_out = local_call(
        mid_kernel,
        [shape((size, width), F32), shape((size, width), BF), shape((width, width), BF)],
        [where_at, act2, out_part, out_y, out_cores, x, gains],
        smem=1,
        us=1,
        mib=24,
        name="mid",
    )
    four = shape((4, size, width), BF)
    d_own, d_next, act4, d_gu, act3_all, cot_all, w_down = local_call(
        functools.partial(feed_kernel, hidden),
        [
            four,
            four,
            shape((total, wide), BF),
            shape((total, 2 * wide), BF),
            shape((total, width), BF),
            shape((total, width), BF),
            shape((wide, width), BF),
        ],
        [where_at, *group_gather(act3), *cot_all, packs],
        scratch=[pltpu.VMEM((width, 2 * wide), BF), pltpu.VMEM((wide, width), F32)],
        smem=1,
        us=3,
        mib=24,
        name="feed",
    )
    d_got, d_own, act4, d_gu, act3_all, cot_all = stage(core(d_next), d_own, act4, d_gu, act3_all, cot_all)
    mid_row = size // 2
    top, low = slice(0, mid_row), slice(mid_row, size)

    def core_sum(i, part):
        return d_own[i, part].astype(F32) + d_got[i, part].astype(F32)

    d_x = flip(jnp.stack([core_sum(2, top), core_sum(3, top)]).astype(BF))
    d_y = across(jnp.stack([core_sum(1, low), core_sum(3, low)]).astype(BF))
    (grads,) = local_call(
        functools.partial(grads_kernel, hidden),
        [shape((half, pack_rows, 256), BF)],
        [where_at, act3_all, cot_all, act4, d_gu],
        scratch=[pltpu.VMEM((wide, width), F32)],
        smem=1,
        us=3,
        mib=24,
        name="grads",
    )
    d_x, d_y, grads, act4 = stage(d_x, d_y, grads, act4)
    grads = lax.psum_scatter(grads, "seq", scatter_dimension=0, axis_index_groups=groups_z)
    d_top = across((core_sum(1, top) + d_x[1].astype(F32)).astype(BF))
    d_bottom = flip((core_sum(2, low) + d_y[1].astype(F32)).astype(BF))
    d_top, d_bottom, act4 = stage(d_top, d_bottom, act4)
    d_resid, d_low, d_act2 = local_call(
        functools.partial(turn_kernel, n_seq),
        [shape((size, width), F32), shape((size, width), BF), shape((n_seq, size, dk), BF)],
        [d_own, d_got, d_x, d_y, d_top, d_bottom, resid, cot, gains, w_out],
        us=1,
        mib=24,
        name="turn",
    )
    d_act2 = lax.all_to_all(d_act2, "seq", 0, 0)
    out_shape = shape((2, n_seq, part_rows, width), BF)
    out_same, out_other = local_call(
        out_grad_kernel,
        [out_shape, out_shape],
        [where_at, act2, d_low],
        scratch=[pltpu.VMEM((width, width), F32)],
        smem=1,
        us=3,
        name="out_grad",
    )
    mixed_own, mixed_next = local_call(
        mixed_kernel, [four, four], [where_at, act4, w_down], smem=1, us=5, name="mixed"
    )
    d_act2, out_same, out_other, mixed_own, mixed_next = stage(d_act2, out_same, out_other, mixed_own, mixed_next)
    mixed_got = core(mixed_next)
    out_got = core(out_other)
    d_proj, parts, d_log, g_conv, g_head = local_call(
        functools.partial(back_kernel, taps),
        [
            shape((total, 3 * dk), BF),
            shape((total, width), BF),
            shape((n_seq, size), F32),
            shape((8, 3 * dk), F32),
            shape((8, dk), F32),
        ],
        [
            where_at,
            starts,
            d_act2,
            outs,
            head,
            conv,
            proj,
            rates,
            inverse,
            w_mat,
            att,
            p_mat,
            u_mat,
            states,
            w_head,
            beta,
        ],
        scratch=[
            pltpu.VMEM((total, dk), F32),
            pltpu.VMEM((RIM + total, 3 * dk), F32),
            pltpu.VMEM((total, 3 * dk), F32),
            pltpu.VMEM((RIM + total, 3 * dk), F32),
            pltpu.VMEM((total, dk), F32),
            pltpu.VMEM((total, dk), F32),
            pltpu.VMEM((n_seq, dk, dk), F32),
            pltpu.VMEM((n_seq, dk, dk), F32),
            pltpu.VMEM((total, dk), BF),
            pltpu.VMEM((total, dk), BF),
        ],
        smem=2,
        us=5,
        name="back",
    )
    d_proj, parts, d_log, g_conv, g_head, out_got, mixed_got, grads = stage(
        d_proj, parts, d_log, g_conv, g_head, out_got, mixed_got, grads
    )
    mixed_both = [mixed_own[i].astype(F32) + mixed_got[i].astype(F32) for i in range(4)]
    mixed_x = flip(jnp.stack([mixed_both[2], mixed_both[3]]).astype(BF))
    d_act1 = lax.psum_scatter(parts, "seq", scatter_dimension=0, tiled=True)
    out_mine = out_same[0].astype(F32) + out_got[0].astype(F32)
    out_y = across((out_same[1].astype(F32) + out_got[1].astype(F32)).astype(BF))
    out_piece = lax.all_to_all((out_mine + out_y.astype(F32)).astype(BF), "seq", 0, 0)
    out_piece = out_piece.astype(F32).sum(0).astype(BF)
    out_y = across(out_piece)
    out_cores = core(jnp.stack([out_piece, out_y]))
    mixed_y = across((mixed_both[1] + mixed_x[1].astype(F32)).astype(BF))
    mixed = (resid + mixed_both[0] + mixed_x[0].astype(F32) + mixed_y.astype(F32)).astype(BF)
    gu_rows = 3 * size
    gu_other = flip(grads[gu_rows : 2 * gu_rows])
    feed_part = jnp.concatenate([grads[:gu_rows], gu_other, grads[2 * gu_rows :]], 0)
    feed_y = across(feed_part)
    feed_cores = core(jnp.stack([feed_part, feed_y]))
    cut_shape = shape((2, n_seq, part_rows + 16, 3 * dk), BF)
    qkv_same, qkv_other = local_call(
        qkv_grad_kernel,
        [cut_shape, cut_shape],
        [where_at, act1, d_proj, d_log, g_conv, g_head],
        scratch=[pltpu.VMEM((width, 3 * dk), F32), pltpu.VMEM((n_seq, 16, 3 * dk), F32)],
        smem=1,
        us=5,
        name="qkv_grad",
    )
    qkv_got = core(qkv_other)
    qkv_mine = qkv_same[0].astype(F32) + qkv_got[0].astype(F32)
    qkv_y = across((qkv_same[1].astype(F32) + qkv_got[1].astype(F32)).astype(BF))
    qkv_piece = lax.all_to_all((qkv_mine + qkv_y.astype(F32)).astype(BF), "seq", 0, 0)
    qkv_y = across(qkv_piece)
    qkv_cores = core(jnp.stack([qkv_piece, qkv_y]))
    (input_gradient,) = local_call(
        last_kernel,
        [shape((size, width), BF)],
        [d_act1, x, gains, d_resid],
        us=3,
        mib=24,
        name="last",
    )
    red_gu, red_down, second_gain = local_call(
        lay_feed_kernel,
        [
            shape((size, 2 * n_seq * hidden), F32),
            shape((hidden, width), F32),
            shape((1, size), F32),
        ],
        [where_at, feed_part, feed_y, feed_cores, gate_up_weight, norm_gains],
        scratch=[pltpu.VMEM((n_row, 2, size, 2 * wide), BF)],
        smem=1,
        us=3,
        mib=24,
        name="lay_feed",
    )
    red_qkv, red_out, red_gains, red_conv, red_beta, red_head = local_call(
        lay_mix_kernel,
        [
            shape((size, 3 * width), F32),
            shape((size, width), F32),
            shape((2, size), F32),
            shape((taps, 3 * dk), F32),
            shape((n_seq, dk), F32),
            shape((1, head_gain.shape[0]), F32),
        ],
        [where_at, qkv_piece, qkv_y, qkv_cores, out_piece, out_y, out_cores, qkv_weight, beta_weight.T, norm_gains, second_gain],
        smem=1,
        us=3,
        mib=24,
        name="lay_mix",
    )
    red_beta = red_beta.T
    red_head = red_head[0]
    return (
        mixed[None],
        input_gradient[None],
        red_qkv,
        red_beta,
        red_conv,
        red_gains,
        red_head,
        red_out,
        red_gu,
        red_down,
    )


def plan(block_input, *rest):
    seq, row = lax.axis_size("seq"), lax.axis_size("row")
    if seq == H and row * 2 == H and block_input.shape[1] == DK:
        return head_plan(block_input, *rest)
    return on_device(block_input, *rest)


def solution(mesh):
    in_specs = (
        P("row", "seq", None),
        P("row", "seq", None),
        P("row", None),
        P("seq", None),
        P("seq", None),
        P(None, "seq"),
        P(None, "seq"),
        P("seq"),
        P("seq", None),
        P("seq", None),
        P("seq", None),
    )
    out_specs = (
        P("row", "seq", None),
        P("row", "seq", None),
        P("seq", None),
        P("seq", None),
        P(None, "seq"),
        P(None, "seq"),
        P("seq"),
        P("seq", None),
        P("seq", None),
        P("seq", None),
    )
    return jax.shard_map(
        plan, mesh=mesh, in_specs=in_specs, out_specs=out_specs, check_vma=False
    )
```

profile of v0, /device:TPU:0, one launch (start us, length us, event | category | flops | bytes accessed | tf_op | source)
XLA Modules:
  0.0 297.8 jit_solution(17414469119857806951)
XLA Ops:
  10.6 7.3 %all-to-all-start = ((bf16[8,144,128]{2,1,0:T(8,128)(2,1)}), bf16[8,144,128]{2,1,0:T(8,128)(2,1)S(1)}, u32[]{:S(2)}, u32[]{:S(2)}) async-start(bf16[8,144,128]{2,1,0:T(8,128)(2,1)} %lead.1), calls=%async_computation | async-start | bytes 589824 | tf_op jit(solution)/shard_map/all_to_all | solution.py:1213
  23.5 8.0 %collective-permute-done.2 = bf16[384,256]{1,0:T(8,128)(2,1)S(1)} collective-permute-done((bf16[384,256]{1,0:T(8,128)(2,1)}, bf16[384,256]{1,0:T(8,128)(2,1)S(1)}, u32[]{:S(2)}, u32[]{:S(2)}) %collective-permute-start.2) | collective-permute-done | bytes 196640 | tf_op jit(solution)/shard_map/ppermute | solution.py:1154
  35.0 4.4 %all-to-all-start.1 = ((bf16[8,32,1024]{2,1,0:T(8,128)(2,1)}), bf16[8,32,1024]{2,1,0:T(8,128)(2,1)S(1)}, u32[]{:S(2)}, u32[]{:S(2)}) async-start(bf16[8,32,1024]{2,1,0:T(8,128)(2,1)} %broadcast_in_dim.12), calls=%async_computation.1 | async-start | bytes 1048576 | tf_op jit(solution)/shard_map/all_to_all | solution.py:1220
  40.7 24.6 %all-to-all-done.1.own_ref = bf16[8,32,1024]{2,1,0:T(8,128)(2,1)S(1)} async-done(((bf16[8,32,1024]{2,1,0:T(8,128)(2,1)}), bf16[8,32,1024]{2,1,0:T(8,128)(2,1)S(1)}, u32[]{:S(2)}, u32[]{:S(2)}) %all-to-all-start.1) | async-done | bytes 524320 | tf_op jit(solution)/shard_map/all_to_all | solution.py:1220
  65.3 5.9 %all-gather.5.cloned.1.call-done = bf16[1,1024,1024]{2,1,0:T(8,128)(2,1)} async-done(((bf16[1,128,1024]{2,1,0:T(8,128)(2,1)}), bf16[1,1024,1024]{2,1,0:T(8,128)(2,1)}) %all-gather.5.cloned.1.call-update) | async-done | bytes 2097168 | tf_op jit(solution)/shard_map/all_gather | solution.py:1190
  74.6 13.5 %front.1 = (bf16[1024,384]{1,0:T(8,128)(2,1)}, bf16[1024,1024]{1,0:T(8,128)(2,1)}, bf16[1024,384]{1,0:T(8,128)(2,1)}, f32[1024,128]{1,0:T(8,128)}, f32[1024,128]...) custom-call(s32[2]{0:T(128)} %pad_add_fusion.place_ref, ...), custom_call_target="tpu_custom_call" | custom-call | flops 4000000000 | bytes 1024 | tf_op jit(solution)/shard_map/front/pallas_call | solution.py:1114
  91.7 3.4 %all-to-all-start.2 = ((bf16[8,128,128]{2,1,0:T(8,128)(2,1)}), bf16[8,128,128]{2,1,0:T(8,128)(2,1)S(1)}, u32[]{:S(2)}, u32[]{:S(2)}) async-start(bf16[8,128,128]{2,1,0:T(8,128)(2,1)} %get-tuple-element.113), calls=%async_computation.2 | async-start | bytes 524288 | tf_op jit(solution)/shard_map/all_to_all | solution.py:1277
  97.5 8.6 %collective-permute-done.7.refs_8_ = bf16[128,1024]{1,0:T(8,128)(2,1)S(1)} collective-permute-done((bf16[128,1024]{1,0:T(8,128)(2,1)S(1)}, bf16[128,1024]{1,0:T(8,128)(2,1)S(1)}, u32[]{:S(2)}, u32[]{:S(2)}) %collective-permute-start.7) | collective-permute-done | bytes 262176 | tf_op jit(solution)/shard_map/ppermute | solution.py:1154
  106.1 6.5 %all-to-all-done.2.act2_ref = bf16[8,128,128]{2,1,0:T(8,128)(2,1)S(1)} async-done(((bf16[8,128,128]{2,1,0:T(8,128)(2,1)}), bf16[8,128,128]{2,1,0:T(8,128)(2,1)S(1)}, u32[]{:S(2)}, u32[]{:S(2)}) %all-to-all-start.2) | async-done | bytes 262176 | tf_op jit(solution)/shard_map/all_to_all | solution.py:1277
  117.0 5.9 %collective-permute-done.8.refs_1_ = bf16[128,1024]{1,0:T(8,128)(2,1)S(1)} collective-permute-done((bf16[128,1024]{1,0:T(8,128)(2,1)S(1)}, bf16[128,1024]{1,0:T(8,128)(2,1)S(1)}, u32[]{:S(2)}, u32[]{:S(2)}) %collective-permute-start.8) | collective-permute-done | bytes 262176 | tf_op jit(solution)/shard_map/ppermute | solution.py:1163
  125.4 4.8 %collective-permute-done.10.refs_3_ = bf16[128,1024]{1,0:T(8,128)(2,1)S(1)} collective-permute-done((bf16[128,1024]{1,0:T(8,128)(2,1)S(1)}, bf16[128,1024]{1,0:T(8,128)(2,1)S(1)}, u32[]{:S(2)}, u32[]{:S(2)}) %collective-permute-start.10) | collective-permute-done | bytes 262176 | tf_op jit(solution)/shard_map/ppermute | solution.py:1154
  138.8 7.6 %feed.1 = (bf16[4,128,1024]{2,1,0:T(8,128)(2,1)S(1)}, bf16[4,128,1024]{2,1,0:T(8,128)(2,1)S(1)}, bf16[1024,384]{1,0:T(8,128)(2,1)S(1)}, bf16[1024,768]{1,0:T(8,1...) custom-call(s32[2]{0:T(128)S(1)} %copy-done.23, ...), custom_call_target="tpu_custom_call" | custom-call | flops 3000000000 | bytes 1024 | tf_op jit(solution)/shard_map/feed/pallas_call | solution.py:1114
  162.7 4.1 %collective-permute-done.17.bottom_ref = bf16[64,1024]{1,0:T(8,128)(2,1)S(1)} collective-permute-done((bf16[64,1024]{1,0:T(8,128)(2,1)S(1)}, bf16[64,1024]{1,0:T(8,128)(2,1)S(1)}, u32[]{:S(2)}, u32[]{:S(2)}) %collective-permute-start.17) | collective-permute-done | bytes 131104 | tf_op jit(solution)/shard_map/ppermute | solution.py:1154
  179.9 4.9 %mixed.1 = (bf16[4,128,1024]{2,1,0:T(8,128)(2,1)}, bf16[4,128,1024]{2,1,0:T(8,128)(2,1)}) custom-call(s32[2]{0:T(128)} %pad_add_fusion.place_ref, bf16[1024,384]{1,0:T(8,128)(2,1)} %copy-done.25, bf16[384,1024]{1,0:T(8,128)(2,1)} %copy-done.26), custom_call_target="tpu_custom_call" | custom-call | flops 5000000000 | bytes 1024 | tf_op jit(solution)/shard_map/mixed/pallas_call | solution.py:1114
  184.8 8.8 %all-to-all-done.3.refs_0_ = bf16[8,128,128]{2,1,0:T(8,128)(2,1)S(1)} async-done(((bf16[8,128,128]{2,1,0:T(8,128)(2,1)}), bf16[8,128,128]{2,1,0:T(8,128)(2,1)S(1)}, u32[]{:S(2)}, u32[]{:S(2)}) %all-to-all-start.3) | async-done | bytes 262176 | tf_op jit(solution)/shard_map/all_to_all | solution.py:1342
  194.3 16.5 %back.1 = (bf16[1024,384]{1,0:T(8,128)(2,1)}, bf16[1024,1024]{1,0:T(8,128)(2,1)}, f32[8,128]{1,0:T(8,128)}, f32[8,384]{1,0:T(8,128)}, f32[8,128]{1,0:T(8,128)}) custom-call(s32[2]{0:T(128)} %pad_add_fusion.place_ref, s32[8]{0:T(128)} %bitcast.92, bf16[8,128,128]{2,1,0:T(8,128)(2,1)} %copy-done.36, f32[1024,128]{1,0:T(8,128)} %get-tuple-element.151.refs_1_, ...), custom_call_target="tpu_custom_call" | custom-call | flops 5000000000 | bytes 1024 | tf_op jit(solution)/shard_map/back/pallas_call | solution.py:1114
  210.8 5.0 %qkv_grad.1 = (bf16[2,8,48,384]{3,2,1,0:T(8,128)(2,1)}, bf16[2,8,48,384]{3,2,1,0:T(8,128)(2,1)}) custom-call(s32[2]{0:T(128)} %pad_add_fusion.place_ref, bf16[1024,1024]{1,0:T(8,128)(2,1)} %get-tuple-element.175.act1_ref, bf16[1024,384]{1,0:T(8,128)(2,1)} %get-tuple-element.176.dproj_ref, f32[8,128]{1,0:T(8,128)} %get-tuple-element.177.dlog_ref, ...), custom_call_target="tpu_custom_call" | custom-call | flops 5000000000 | bytes 1024 | tf_op jit(solution)/shard_map/qkv_grad/pallas_call | solution.py:1114
  224.3 5.2 %collective-permute-done.23 = bf16[8,48,384]{2,1,0:T(8,128)(2,1)S(1)} collective-permute-done((bf16[8,48,384]{2,1,0:T(8,128)(2,1)S(1)}, bf16[8,48,384]{2,1,0:T(8,128)(2,1)S(1)}, u32[]{:S(2)}, u32[]{:S(2)}) %collective-permute-start.23) | collective-permute-done | bytes 294944 | tf_op jit(solution)/shard_map/ppermute | solution.py:1163
  231.3 3.4 %all-to-all-start.4 = ((bf16[8,48,384]{2,1,0:T(8,128)(2,1)}), bf16[8,48,384]{2,1,0:T(8,128)(2,1)S(1)}, u32[]{:S(2)}, u32[]{:S(2)}) async-start(bf16[8,48,384]{2,1,0:T(8,128)(2,1)} %fusion.1), calls=%async_computation.6 | async-start | bytes 589824 | tf_op jit(solution)/shard_map/all_to_all | solution.py:1434
  243.0 6.8 %all-to-all-done.4.refs_0_ = bf16[8,48,384]{2,1,0:T(8,128)(2,1)S(1)} async-done(((bf16[8,48,384]{2,1,0:T(8,128)(2,1)}), bf16[8,48,384]{2,1,0:T(8,128)(2,1)S(1)}, u32[]{:S(2)}, u32[]{:S(2)}) %all-to-all-start.4) | async-done | bytes 294944 | tf_op jit(solution)/shard_map/all_to_all | solution.py:1434
  249.8 3.9 %all-to-all-start.5 = ((bf16[8,32,1024]{2,1,0:T(8,128)(2,1)}), bf16[8,32,1024]{2,1,0:T(8,128)(2,1)S(1)}, u32[]{:S(2)}, u32[]{:S(2)}) async-start(bf16[8,32,1024]{2,1,0:T(8,128)(2,1)} %fusion), calls=%async_computation.7 | async-start | bytes 1048576 | tf_op jit(solution)/shard_map/all_to_all | solution.py:1410
  258.8 8.6 %all-to-all-done.5 = bf16[8,32,1024]{2,1,0:T(8,128)(2,1)S(1)} async-done(((bf16[8,32,1024]{2,1,0:T(8,128)(2,1)}), bf16[8,32,1024]{2,1,0:T(8,128)(2,1)S(1)}, u32[]{:S(2)}, u32[]{:S(2)}) %all-to-all-start.5) | async-done | bytes 524320 | tf_op jit(solution)/shard_map/all_to_all | solution.py:1410
  272.4 9.2 %lay_feed.1 = (f32[128,5632]{1,0:T(8,128)}, f32[352,1024]{1,0:T(8,128)}, f32[1,128]{1,0:T(1,128)S(1)}) custom-call(s32[2]{0:T(128)S(1)} %copy-done.24, bf16[1152,256]{1,0:T(8,128)(2,1)S(1)} %get-tuple-element.203.refs_0_, bf16[1152,256]{1,0:T(8,128)(2,1)S(1)} %collective-permute-done.30.refs_1_, bf16[2,1152,256]{2,1,0:T(8,128)(2,1)} %collective-permute-done.31.refs_2_, ...), custom_call_target="tpu_custom_call" | custom-call | flops 3000000000 | bytes 1024 | tf_op jit(solution)/shard_map/lay_feed/pallas_call | solution.py:1114
  283.8 5.3 %reduce-scatter.5.cloned.1.call-done.part_ref = bf16[128,1024]{1,0:T(8,128)(2,1)} async-done(((bf16[1024,1024]{1,0:T(8,128)(2,1)}), bf16[128,1024]{1,0:T(8,128)(2,1)}) %reduce-scatter.5.cloned.1.call-update) | async-done | bytes 262160 | tf_op jit(solution)/shard_map/reduce_scatter | solution.py:1407
  (182 shorter events, 101.3 us)
Async XLA Ops:
  7.2 64.0 %all-gather.5.cloned.1.call-start = ((), (), s32[]{:S(2)}) async-start(), calls=%async_computation.10 | async-start | bytes 2359296 | tf_op jit(solution)/shard_map/all_gather | solution.py:1190
  10.6 20.9 %all-to-all-start = ((bf16[8,144,128]{2,1,0:T(8,128)(2,1)}), bf16[8,144,128]{2,1,0:T(8,128)(2,1)S(1)}, u32[]{:S(2)}, u32[]{:S(2)}) async-start(bf16[8,144,128]{2,1,0:T(8,128)(2,1)} %lead.1), calls=%async_computation | async-start | bytes 589824 | tf_op jit(solution)/shard_map/all_to_all | solution.py:1213
  35.0 30.3 %all-to-all-start.1 = ((bf16[8,32,1024]{2,1,0:T(8,128)(2,1)}), bf16[8,32,1024]{2,1,0:T(8,128)(2,1)S(1)}, u32[]{:S(2)}, u32[]{:S(2)}) async-start(bf16[8,32,1024]{2,1,0:T(8,128)(2,1)} %broadcast_in_dim.12), calls=%async_computation.1 | async-start | bytes 1048576 | tf_op jit(solution)/shard_map/all_to_all | solution.py:1220
  39.4 92.6 %all-gather.7.cloned.1.call-start = ((), (), s32[]{:S(2)}) async-start(), calls=%async_computation.11 | async-start | bytes 2949120 | tf_op jit(solution)/shard_map/all_gather | solution.py:1219
  40.6 24.7 %collective-permute-start.1 = (bf16[2,8,144,128]{3,2,1,0:T(8,128)(2,1)S(1)}, bf16[2,8,144,128]{3,2,1,0:T(8,128)(2,1)}, u32[]{:S(2)}, u32[]{:S(2)}) collective-permute-start(bf16[2,8,144,128]{3,2,1,0:T(8,128)(2,1)S(1)} %pad_maximum_fusion.4), channel_id=1, source_target_pairs={{0,1},{1,0},{2,3},{3,2},{4,5},{5,4},{6,7},{7,6},{8,9},{9,8},{10,11... | collective-permute-start | bytes 1769480 | tf_op jit(solution)/shard_map/ppermute | solution.py:1160
  71.1 19.5 %collective-permute-start.5 = (bf16[8,32,1024]{2,1,0:T(8,128)(2,1)S(1)}, bf16[8,32,1024]{2,1,0:T(8,128)(2,1)S(1)}, u32[]{:S(2)}, u32[]{:S(2)}) collective-permute-start(bf16[8,32,1024]{2,1,0:T(8,128)(2,1)S(1)} %all-to-all-done.1.own_ref), channel_id=1, source_target_pairs={{0,2},{1,3},{2,0},{3,1},{4,6},{5,7},{6,4},{7,5},{8,10},{9,11},{10,... | collective-permute-start | bytes 1572872 | tf_op jit(solution)/shard_map/ppermute | solution.py:1163
  71.7 16.5 %collective-permute-start.4 = (bf16[128,1024]{1,0:T(8,128)(2,1)S(1)}, bf16[128,1024]{1,0:T(8,128)(2,1)S(1)}, u32[]{:S(2)}, u32[]{:S(2)}) collective-permute-start(bf16[128,1024]{1,0:T(8,128)(2,1)S(1)} %bitcast.65), channel_id=1, source_target_pairs={{0,4},{4,0},{8,12},{12,8},{16,20},{20,16},{24,28},{28,24},{1,5},{5... | collective-permute-start | bytes 786440 | tf_op jit(solution)/shard_map/ppermute | solution.py:1154
  73.1 17.5 %collective-permute-start.3 = (bf16[128,1024]{1,0:T(8,128)(2,1)S(1)}, bf16[128,1024]{1,0:T(8,128)(2,1)S(1)}, u32[]{:S(2)}, u32[]{:S(2)}) collective-permute-start(bf16[128,1024]{1,0:T(8,128)(2,1)S(1)} %bitcast.66), channel_id=1, source_target_pairs={{0,2},{1,3},{2,0},{3,1},{4,6},{5,7},{6,4},{7,5},{8,10},{9,11},{10,... | collective-permute-start | bytes 786440 | tf_op jit(solution)/shard_map/ppermute | solution.py:1163
  91.7 20.9 %collective-permute-start.6 = (bf16[2,8,32,1024]{3,2,1,0:T(8,128)(2,1)}, bf16[2,8,32,1024]{3,2,1,0:T(8,128)(2,1)}, u32[]{:S(2)}, u32[]{:S(2)}) collective-permute-start(bf16[2,8,32,1024]{3,2,1,0:T(8,128)(2,1)} %pad_maximum_fusion.1), channel_id=1, source_target_pairs={{0,1},{1,0},{2,3},{3,2},{4,5},{5,4},{6,7},{7,6},{8,9},{9,8},{10,11... | collective-permute-start | bytes 3145736 | tf_op jit(solution)/shard_map/ppermute | solution.py:1160
  91.7 20.9 %all-to-all-start.2 = ((bf16[8,128,128]{2,1,0:T(8,128)(2,1)}), bf16[8,128,128]{2,1,0:T(8,128)(2,1)S(1)}, u32[]{:S(2)}, u32[]{:S(2)}) async-start(bf16[8,128,128]{2,1,0:T(8,128)(2,1)} %get-tuple-element.113), calls=%async_computation.2 | async-start | bytes 524288 | tf_op jit(solution)/shard_map/all_to_all | solution.py:1277
  95.1 115.7 %reduce-scatter.3.cloned.1.call-start = ((), (), s32[]{:S(2)}) async-start(), calls=%async_computation.8 | async-start | bytes 2949120 | tf_op jit(solution)/shard_map/reduce_scatter | solution.py:1330
  173.2 20.4 %all-to-all-start.3 = ((bf16[8,128,128]{2,1,0:T(8,128)(2,1)}), bf16[8,128,128]{2,1,0:T(8,128)(2,1)S(1)}, u32[]{:S(2)}, u32[]{:S(2)}) async-start(bf16[8,128,128]{2,1,0:T(8,128)(2,1)} %get-tuple-element.141), calls=%async_computation.3 | async-start | bytes 524288 | tf_op jit(solution)/shard_map/all_to_all | solution.py:1342
  176.6 112.5 %reduce-scatter.5.cloned.1.call-start = ((), (), s32[]{:S(2)}) async-start(), calls=%async_computation.9 | async-start | bytes 2359296 | tf_op jit(solution)/shard_map/reduce_scatter | solution.py:1407
  193.6 17.2 %collective-permute-start.18 = (bf16[2,8,32,1024]{3,2,1,0:T(8,128)(2,1)S(1)}, bf16[2,8,32,1024]{3,2,1,0:T(8,128)(2,1)S(1)}, u32[]{:S(2)}, u32[]{:S(2)}) collective-permute-start(bf16[2,8,32,1024]{3,2,1,0:T(8,128)(2,1)S(1)} %copy-done.37), channel_id=1, source_target_pairs={{0,1},{1,0},{2,3},{3,2},{4,5},{5,4},{6,7},{7,6},{8,9},{9,8},{10,11... | collective-permute-start | bytes 3145736 | tf_op jit(solution)/shard_map/ppermute | solution.py:1160
  193.6 17.2 %collective-permute-start.19 = (bf16[4,128,1024]{2,1,0:T(8,128)(2,1)}, bf16[4,128,1024]{2,1,0:T(8,128)(2,1)}, u32[]{:S(2)}, u32[]{:S(2)}) collective-permute-start(bf16[4,128,1024]{2,1,0:T(8,128)(2,1)} %get-tuple-element.170), channel_id=1, source_target_pairs={{0,1},{1,0},{2,3},{3,2},{4,5},{5,4},{6,7},{7,6},{8,9},{9,8},{10,11... | collective-permute-start | bytes 3145736 | tf_op jit(solution)/shard_map/ppermute | solution.py:1160
  221.4 19.4 %collective-permute-start.26 = (bf16[8,32,1024]{2,1,0:T(8,128)(2,1)}, bf16[8,32,1024]{2,1,0:T(8,128)(2,1)}, u32[]{:S(2)}, u32[]{:S(2)}) collective-permute-start(bf16[8,32,1024]{2,1,0:T(8,128)(2,1)} %fusion.2), channel_id=1, source_target_pairs={{0,2},{1,3},{2,0},{3,1},{4,6},{5,7},{6,4},{7,5},{8,10},{9,11},{10,... | collective-permute-start | bytes 1572872 | tf_op jit(solution)/shard_map/ppermute | solution.py:1163
  223.8 29.9 %collective-permute-start.30 = (bf16[1152,256]{1,0:T(8,128)(2,1)S(1)}, bf16[1152,256]{1,0:T(8,128)(2,1)S(1)}, u32[]{:S(2)}, u32[]{:S(2)}) collective-permute-start(bf16[1152,256]{1,0:T(8,128)(2,1)S(1)} %get-tuple-element.203.refs_0_), channel_id=1, source_target_pairs={{0,2},{1,3},{2,0},{3,1},{4,6},{5,7},{6,4},{7,5},{8,10},{9,11},{10,... | collective-permute-start | bytes 1769480 | tf_op jit(solution)/shard_map/ppermute | solution.py:1163
  231.3 18.5 %all-to-all-start.4 = ((bf16[8,48,384]{2,1,0:T(8,128)(2,1)}), bf16[8,48,384]{2,1,0:T(8,128)(2,1)S(1)}, u32[]{:S(2)}, u32[]{:S(2)}) async-start(bf16[8,48,384]{2,1,0:T(8,128)(2,1)} %fusion.1), calls=%async_computation.6 | async-start | bytes 589824 | tf_op jit(solution)/shard_map/all_to_all | solution.py:1434
  237.2 19.1 %collective-permute-start.20 = (bf16[2,128,1024]{2,1,0:T(8,128)(2,1)}, bf16[2,128,1024]{2,1,0:T(8,128)(2,1)}, u32[]{:S(2)}, u32[]{:S(2)}) collective-permute-start(bf16[2,128,1024]{2,1,0:T(8,128)(2,1)} %pad_maximum_fusion.7), channel_id=1, source_target_pairs={{0,4},{4,0},{8,12},{12,8},{16,20},{20,16},{24,28},{28,24},{1,5},{5... | collective-permute-start | bytes 1572872 | tf_op jit(solution)/shard_map/ppermute | solution.py:1154
  249.8 17.6 %all-to-all-start.5 = ((bf16[8,32,1024]{2,1,0:T(8,128)(2,1)}), bf16[8,32,1024]{2,1,0:T(8,128)(2,1)S(1)}, u32[]{:S(2)}, u32[]{:S(2)}) async-start(bf16[8,32,1024]{2,1,0:T(8,128)(2,1)} %fusion), calls=%async_computation.7 | async-start | bytes 1048576 | tf_op jit(solution)/shard_map/all_to_all | solution.py:1410
  254.8 17.6 %collective-permute-start.31 = (bf16[2,1152,256]{2,1,0:T(8,128)(2,1)}, bf16[2,1152,256]{2,1,0:T(8,128)(2,1)}, u32[]{:S(2)}, u32[]{:S(2)}) collective-permute-start(bf16[2,1152,256]{2,1,0:T(8,128)(2,1)} %pad_maximum_fusion), channel_id=1, source_target_pairs={{0,1},{1,0},{2,3},{3,2},{4,5},{5,4},{6,7},{7,6},{8,9},{9,8},{10,11... | collective-permute-start | bytes 3538952 | tf_op jit(solution)/shard_map/ppermute | solution.py:1160
  254.8 14.3 %collective-permute-start.24 = (bf16[8,48,384]{2,1,0:T(8,128)(2,1)S(1)}, bf16[8,48,384]{2,1,0:T(8,128)(2,1)S(1)}, u32[]{:S(2)}, u32[]{:S(2)}) collective-permute-start(bf16[8,48,384]{2,1,0:T(8,128)(2,1)S(1)} %all-to-all-done.4.refs_0_), channel_id=1, source_target_pairs={{0,2},{1,3},{2,0},{3,1},{4,6},{5,7},{6,4},{7,5},{8,10},{9,11},{10,... | collective-permute-start | bytes 884744 | tf_op jit(solution)/shard_map/ppermute | solution.py:1163
  258.2 12.1 %collective-permute-start.21 = (bf16[128,1024]{1,0:T(8,128)(2,1)}, bf16[128,1024]{1,0:T(8,128)(2,1)S(1)}, u32[]{:S(2)}, u32[]{:S(2)}) collective-permute-start(bf16[128,1024]{1,0:T(8,128)(2,1)} %fusion.6), channel_id=1, source_target_pairs={{0,2},{1,3},{2,0},{3,1},{4,6},{5,7},{6,4},{7,5},{8,10},{9,11},{10,... | collective-permute-start | bytes 786440 | tf_op jit(solution)/shard_map/ppermute | solution.py:1163
  269.2 12.4 %collective-permute-start.25 = (bf16[2,8,48,384]{3,2,1,0:T(8,128)(2,1)S(1)}, bf16[2,8,48,384]{3,2,1,0:T(8,128)(2,1)S(1)}, u32[]{:S(2)}, u32[]{:S(2)}) collective-permute-start(bf16[2,8,48,384]{3,2,1,0:T(8,128)(2,1)S(1)} %pad_maximum_fusion.5), channel_id=1, source_target_pairs={{0,1},{1,0},{2,3},{3,2},{4,5},{5,4},{6,7},{7,6},{8,9},{9,8},{10,11... | collective-permute-start | bytes 1769480 | tf_op jit(solution)/shard_map/ppermute | solution.py:1160
  (56 other events, 440.6 us)
Sparse Core Ops, SparseCore 0:
  10.2 60.9 all-gather.4
  73.3 53.7 all-gather.6
  160.9 49.4 reduce-scatter.2
  216.0 73.1 reduce-scatter.4
where the time goes:
time: 302 us; the launch traced here: 298 us
  waiting for transfers between devices  120 us (40%)
  Pallas kernels  75.8 us (25%)
  starting transfers between devices  52.3 us (17%)
  other arithmetic  20.3 us (7%)
  local copies, waits for them, and re-layouts  15.2 us (5%)
  between operations  14.5 us (5%)
    pallas_call x14, Pallas kernels, local_call(): pl.pallas_call(kernel, out_shape=tuple(outs), in_specs=space, out_specs=t...  75.8 us
    ppermute x9, waiting for transfers between devices, flip(): return lax.ppermute(v, 'seq', [(s, s ^ 1) for s in range(n_seq)])  28.3 us
    all_to_all x1, waiting for transfers between devices, head_plan(): out_part = lax.all_to_all(stage(out_part, pack)[0], 'seq', 0, 0)  24.6 us
    ppermute x12, waiting for transfers between devices, across(): return lax.ppermute(v, 'row', [(r, r ^ 2) for r in range(n_row)])  19.7 us
    ppermute x9, starting transfers between devices, flip(): return lax.ppermute(v, 'seq', [(s, s ^ 1) for s in range(n_seq)])  13.8 us
    unnamed x78, local copies, waits for them, and re-layouts  13.3 us
    ppermute x12, starting transfers between devices, across(): return lax.ppermute(v, 'row', [(r, r ^ 2) for r in range(n_row)])  11 us
    all_to_all x1, waiting for transfers between devices, head_plan(): d_act2 = lax.all_to_all(d_act2, 'seq', 0, 0)  8.76 us
  transfers between devices with their start and end apart: 42, of which 23 were waited for; matrix products, arithmetic and copies ran while one was open for 7% of the time, Pallas kernels for 21%

commit v1 on v0

--- a/solution.py
+++ b/solution.py
@@ -524,7 +524,8 @@
 def front_kernel(taps, place_ref, starts_ref, *refs):
     n_seq = refs[-1].shape[0]
     n_row = n_seq // 2
-    x_ref, got_ref, got_y_ref, got_cores_ref = refs[:4]
+    top_ref, low_refs = refs[0], refs[1 : 1 + n_seq]
+    got_ref, got_y_ref, got_cores_ref = refs[1 + n_seq : 4 + n_seq]
     got_refs = (got_ref, got_cores_ref.at[0], got_y_ref, got_cores_ref.at[1])
     (
         weight_ref,
@@ -549,8 +550,9 @@
         q_scr,
         k_scr,
         v_scr,
+        low_rows,
         add,
-    ) = refs[4:]
+    ) = refs[4 + n_seq :]
     place, row = place_ref[0], place_ref[1]
     size = s_ref.shape[1]
     part_rows = size // n_row
@@ -582,10 +584,25 @@
                 weight_ref[pl.ds(at, part_rows), kind * dk : (kind + 1) * dk] = block
     weight = weight_ref[...]
     lanes = lax.broadcasted_iota(jnp.int32, (2 * size, 8), 1)
+    half = n_seq // 2
+    z, side = place // 2, lax.rem(place, 2)
+    for i, ref in enumerate(low_refs):
+        chunk = lax.rem(z - i // 2 + half, half) * 2 + (side if i % 2 == 0 else 1 - side)
+        at = pl.multiple_of(chunk * (size // 2), size // 2)
+        low_rows[pl.ds(at, size // 2), :] = ref[...]
     pad[0:RIM, :] = jnp.zeros((RIM, 3 * dk), F32)
     for n in range(0, n_seq, 2):
         rows_at = pl.ds(n * size, 2 * size)
-        rows = x_ref[rows_at, :].astype(F32)
+        part = size // 2
+        rows = jnp.concatenate(
+            [
+                top_ref[n * part : (n + 1) * part, :],
+                low_rows[n * part : (n + 1) * part, :],
+                top_ref[(n + 1) * part : (n + 2) * part, :],
+                low_rows[(n + 1) * part : (n + 2) * part, :],
+            ],
+            0,
+        ).astype(F32)
         inv = lax.rsqrt(jnp.mean(rows * rows, -1, keepdims=True) + EPS_NORM)
         act = ((rows * inv) * gains[0:1]).astype(BF)
         act1_ref[rows_at, :] = act
@@ -1061,8 +1078,9 @@
                     piece = held[m, x, :, at : at + part].astype(F32)
                     to = (kind * 8 + z * 2 + x) * hidden + m * part
                     gu_out[:, to : to + part] = piece
-                    term = piece * weight_ref[:, to : to + part].astype(F32)
-                    total = term if total is None else total + term
+    for at in range(0, gu_out.shape[1], lanes):
+        term = gu_out[:, at : at + lanes] * weight_ref[:, at : at + lanes].astype(F32)
+        total = term if total is None else total + term
     gain_out[...] = row_sums(total) / gain_ref[1:2, :].astype(F32)
 
 
@@ -1187,7 +1205,10 @@
     part_rows = size // n_row
     dk = width // n_seq
     lead_rows = 3 * part_rows + 48
-    row_x = lax.all_gather(x, "seq", tiled=True)
+    mid_row = size // 2
+    row_top = lax.all_gather(x[:mid_row], "seq", tiled=True)
+    far = {k: roll(x[mid_row:], k) for k in (2, 1, 3)}
+    near = flip(x[mid_row:])
     (payload,) = local_call(
         lead_kernel,
         [shape((n_seq, lead_rows, dk), BF)],
@@ -1217,8 +1238,14 @@
     out_part = jnp.broadcast_to(out_part[None], (n_seq, part_rows, width))
     groups_z = [[2 * a + j for a in range(half)] for j in range(2)]
     packs = lax.all_gather(pack, "seq", axis_index_groups=groups_z)
-    out_part = lax.all_to_all(stage(out_part, pack)[0], "seq", 0, 0)
-    row_x, got, got_y, got_cores, out_part, cot, _ = stage(row_x, got, got_y, got_cores, out_part, cot, pack)
+    out_part, _, near, far[1], far[2], far[3] = stage(out_part, pack, near, far[1], far[2], far[3])
+    out_part = lax.all_to_all(out_part, "seq", 0, 0)
+    row_low = [x[mid_row:], near]
+    for k in range(1, half):
+        row_low += [far[k], flip(far[k])]
+    row_top, got, got_y, got_cores, out_part, cot, _, *row_low = stage(
+        row_top, got, got_y, got_cores, out_part, cot, pack, *row_low
+    )
     cot_y, cot_x = across(cot), flip(cot)
     out_y = across(out_part)
     square = shape((n_seq, size, dk), F32)
@@ -1259,7 +1286,7 @@
             shape((8, width), BF),
             shape((8, dk), F32),
         ],
-        [where_at, starts, row_x, got, got_y, got_cores],
+        [where_at, starts, row_top, *row_low, got, got_y, got_cores],
         scratch=[
             pltpu.VMEM((RIM + total, 3 * dk), F32),
             pltpu.VMEM((n_seq, size, size), F32),
@@ -1267,6 +1294,7 @@
             pltpu.VMEM((total, dk), BF),
             pltpu.VMEM((total, dk), BF),
             pltpu.VMEM((total, dk), BF),
+            pltpu.VMEM((total // 2, width), BF),
             pltpu.VMEM((n_seq, dk, dk), F32),
         ],
         smem=2,
@@ -1308,7 +1336,6 @@
         name="feed",
     )
     d_got, d_own, act4, d_gu, act3_all, cot_all = stage(core(d_next), d_own, act4, d_gu, act3_all, cot_all)
-    mid_row = size // 2
     top, low = slice(0, mid_row), slice(mid_row, size)
 
     def core_sum(i, part):

time: 302 us -> 298 us (0.987)
  waiting for transfers between devices: 120 us -> 104 us
  starting transfers between devices: 52.3 us -> 65.8 us
  Pallas kernels: 75.8 us -> 71.8 us
    all_to_all x1, waiting for transfers between devices: 24.6 us -> 0.74 us  [head_plan(): out_part = lax.all_to_all(out_part, 'seq', 0, 0)]
    ppermute x9 -> x13, waiting for transfers between devices: 28.3 us -> 40.5 us  [flip(): return lax.ppermute(v, 'seq', [(s, s ^ 1) for s in range(n_seq)])]
    ppermute x0 -> x3, starting transfers between devices: none -> 6.06 us  [roll(): lax.ppermute(v, 'seq', [(s, (s // 2 + k) % half * 2 + s % 2) for s in ran...]
    ppermute x9 -> x13, starting transfers between devices: 13.8 us -> 19.8 us  [flip(): return lax.ppermute(v, 'seq', [(s, s ^ 1) for s in range(n_seq)])]
    all_gather x1, waiting for transfers between devices: 5.87 us -> 0.01 us  [head_plan(): row_top = lax.all_gather(x[:mid_row], 'seq', tiled=True)]
    reduce_scatter x1, waiting for transfers between devices: 5.3 us -> 9.58 us  [head_plan(): d_act1 = lax.psum_scatter(parts, 'seq', scatter_dimension=0, tiled=True)]
    pallas_call x14, Pallas kernels: 75.8 us -> 71.8 us  [local_call(): pl.pallas_call(kernel, out_shape=tuple(outs), in_specs=space, out_specs=t...]
    all_to_all x1, starting transfers between devices: 7.25 us -> 4.09 us  [head_plan(): got = lax.all_to_all(payload, 'seq', 0, 0)]
  transfers between devices with their start and end apart: 42 -> 49, of which waited for: 23 -> 24; matrix products, arithmetic and copies ran while one was open for 7% -> 8% of each run, Pallas kernels for 21% -> 20%
where the time goes in v1:
time: 298 us; the launch traced here: 293 us
  waiting for transfers between devices  104 us (35%)
  Pallas kernels  71.8 us (24%)
  starting transfers between devices  65.8 us (22%)
  other arithmetic  20.3 us (7%)
  local copies, waits for them, and re-layouts  17 us (6%)
  between operations  14.6 us (5%)
    pallas_call x14, Pallas kernels, local_call(): pl.pallas_call(kernel, out_shape=tuple(outs), in_specs=space, out_specs=t...  71.8 us
    ppermute x13, waiting for transfers between devices, flip(): return lax.ppermute(v, 'seq', [(s, s ^ 1) for s in range(n_seq)])  40.5 us
    ppermute x13, starting transfers between devices, flip(): return lax.ppermute(v, 'seq', [(s, s ^ 1) for s in range(n_seq)])  19.8 us
    ppermute x12, waiting for transfers between devices, across(): return lax.ppermute(v, 'row', [(r, r ^ 2) for r in range(n_row)])  17.3 us
    unnamed x94, local copies, waits for them, and re-layouts  13.3 us
    ppermute x12, starting transfers between devices, across(): return lax.ppermute(v, 'row', [(r, r ^ 2) for r in range(n_row)])  11.1 us
    reduce_scatter x1, waiting for transfers between devices, head_plan(): d_act1 = lax.psum_scatter(parts, 'seq', scatter_dimension=0, tiled=True)  9.58 us
    all_to_all x1, waiting for transfers between devices, head_plan(): lax.all_to_all((out_mine + out_y.astype(F32)).astype(BF), 'seq', 0, 0)  8.77 us
  transfers between devices with their start and end apart: 49, of which 24 were waited for; matrix products, arithmetic and copies ran while one was open for 8% of the time, Pallas kernels for 20%

profile of v1, /device:TPU:0, one launch (start us, length us, event | category | flops | bytes accessed | tf_op | source)
XLA Modules:
  0.0 293.1 jit_solution(10935149218750385107)
XLA Ops:
  8.9 5.0 %collective-permute-start.6 = (bf16[64,1024]{1,0:T(8,128)(2,1)S(1)}, bf16[64,1024]{1,0:T(8,128)(2,1)S(1)}, u32[]{:S(2)}, u32[]{:S(2)}) collective-permute-start(bf16[64,1024]{1,0:T(8,128)(2,1)S(1)} %get-tuple-element.123.refs_1_), channel_id=1, source_target_pairs={{0,24},{4,28},{8,0},{12,4},{16,8},{20,12},{24,16},{28,20},{1,25},{... | collective-permute-start | bytes 393224 | tf_op jit(solution)/shard_map/ppermute | solution.py:1175
  19.1 4.1 %all-to-all-start = ((bf16[8,144,128]{2,1,0:T(8,128)(2,1)}), bf16[8,144,128]{2,1,0:T(8,128)(2,1)S(1)}, u32[]{:S(2)}, u32[]{:S(2)}) async-start(bf16[8,144,128]{2,1,0:T(8,128)(2,1)} %lead.1), calls=%async_computation | async-start | bytes 589824 | tf_op jit(solution)/shard_map/all_to_all | solution.py:1234
  28.9 6.0 %collective-permute-done.2 = bf16[384,256]{1,0:T(8,128)(2,1)S(1)} collective-permute-done((bf16[384,256]{1,0:T(8,128)(2,1)}, bf16[384,256]{1,0:T(8,128)(2,1)S(1)}, u32[]{:S(2)}, u32[]{:S(2)}) %collective-permute-start.2) | collective-permute-done | bytes 196640 | tf_op jit(solution)/shard_map/ppermute | solution.py:1172
  38.6 6.3 %all-to-all-start.1 = ((bf16[8,32,1024]{2,1,0:T(8,128)(2,1)}), bf16[8,32,1024]{2,1,0:T(8,128)(2,1)S(1)}, u32[]{:S(2)}, u32[]{:S(2)}) async-start(bf16[8,32,1024]{2,1,0:T(8,128)(2,1)} %broadcast_in_dim.12), calls=%async_computation.1 | async-start | bytes 1048576 | tf_op jit(solution)/shard_map/all_to_all | solution.py:1242
  49.5 9.8 %collective-permute-done.7.refs_4_ = bf16[64,1024]{1,0:T(8,128)(2,1)S(1)} collective-permute-done((bf16[64,1024]{1,0:T(8,128)(2,1)S(1)}, bf16[64,1024]{1,0:T(8,128)(2,1)S(1)}, u32[]{:S(2)}, u32[]{:S(2)}) %collective-permute-start.7) | collective-permute-done | bytes 131104 | tf_op jit(solution)/shard_map/ppermute | solution.py:1172
  69.8 14.0 %front.1 = (bf16[1024,384]{1,0:T(8,128)(2,1)}, bf16[1024,1024]{1,0:T(8,128)(2,1)}, bf16[1024,384]{1,0:T(8,128)(2,1)}, f32[1024,128]{1,0:T(8,128)}, f32[1024,128]...) custom-call(s32[2]{0:T(128)} %pad_add_fusion.place_ref, ...), custom_call_target="tpu_custom_call" | custom-call | flops 4000000000 | bytes 1024 | tf_op jit(solution)/shard_map/front/pallas_call | solution.py:1132
  85.6 5.3 %all-to-all-start.2 = ((bf16[8,128,128]{2,1,0:T(8,128)(2,1)}), bf16[8,128,128]{2,1,0:T(8,128)(2,1)S(1)}, u32[]{:S(2)}, u32[]{:S(2)}) async-start(bf16[8,128,128]{2,1,0:T(8,128)(2,1)} %get-tuple-element.137), calls=%async_computation.2 | async-start | bytes 524288 | tf_op jit(solution)/shard_map/all_to_all | solution.py:1305
  93.2 8.4 %collective-permute-done.14.refs_8_ = bf16[128,1024]{1,0:T(8,128)(2,1)S(1)} collective-permute-done((bf16[128,1024]{1,0:T(8,128)(2,1)S(1)}, bf16[128,1024]{1,0:T(8,128)(2,1)S(1)}, u32[]{:S(2)}, u32[]{:S(2)}) %collective-permute-start.14) | collective-permute-done | bytes 262176 | tf_op jit(solution)/shard_map/ppermute | solution.py:1172
  101.6 6.9 %all-to-all-done.2.act2_ref = bf16[8,128,128]{2,1,0:T(8,128)(2,1)S(1)} async-done(((bf16[8,128,128]{2,1,0:T(8,128)(2,1)}), bf16[8,128,128]{2,1,0:T(8,128)(2,1)S(1)}, u32[]{:S(2)}, u32[]{:S(2)}) %all-to-all-start.2) | async-done | bytes 262176 | tf_op jit(solution)/shard_map/all_to_all | solution.py:1305
  112.2 6.0 %collective-permute-done.15.refs_1_ = bf16[128,1024]{1,0:T(8,128)(2,1)S(1)} collective-permute-done((bf16[128,1024]{1,0:T(8,128)(2,1)S(1)}, bf16[128,1024]{1,0:T(8,128)(2,1)S(1)}, u32[]{:S(2)}, u32[]{:S(2)}) %collective-permute-start.15) | collective-permute-done | bytes 262176 | tf_op jit(solution)/shard_map/ppermute | solution.py:1181
  120.8 4.2 %collective-permute-done.17.refs_3_ = bf16[128,1024]{1,0:T(8,128)(2,1)S(1)} collective-permute-done((bf16[128,1024]{1,0:T(8,128)(2,1)S(1)}, bf16[128,1024]{1,0:T(8,128)(2,1)S(1)}, u32[]{:S(2)}, u32[]{:S(2)}) %collective-permute-start.17) | collective-permute-done | bytes 262176 | tf_op jit(solution)/shard_map/ppermute | solution.py:1172
  133.6 7.6 %feed.1 = (bf16[4,128,1024]{2,1,0:T(8,128)(2,1)S(1)}, bf16[4,128,1024]{2,1,0:T(8,128)(2,1)S(1)}, bf16[1024,384]{1,0:T(8,128)(2,1)S(1)}, bf16[1024,768]{1,0:T(8,1...) custom-call(s32[2]{0:T(128)S(1)} %copy-done.23, ...), custom_call_target="tpu_custom_call" | custom-call | flops 3000000000 | bytes 1024 | tf_op jit(solution)/shard_map/feed/pallas_call | solution.py:1132
  157.8 3.8 %collective-permute-done.24.bottom_ref = bf16[64,1024]{1,0:T(8,128)(2,1)S(1)} collective-permute-done((bf16[64,1024]{1,0:T(8,128)(2,1)S(1)}, bf16[64,1024]{1,0:T(8,128)(2,1)S(1)}, u32[]{:S(2)}, u32[]{:S(2)}) %collective-permute-start.24) | collective-permute-done | bytes 131104 | tf_op jit(solution)/shard_map/ppermute | solution.py:1172
  167.9 4.5 %all-to-all-start.3 = ((bf16[8,128,128]{2,1,0:T(8,128)(2,1)}), bf16[8,128,128]{2,1,0:T(8,128)(2,1)S(1)}, u32[]{:S(2)}, u32[]{:S(2)}) async-start(bf16[8,128,128]{2,1,0:T(8,128)(2,1)} %get-tuple-element.165), calls=%async_computation.3 | async-start | bytes 524288 | tf_op jit(solution)/shard_map/all_to_all | solution.py:1369
  175.7 5.1 %mixed.1 = (bf16[4,128,1024]{2,1,0:T(8,128)(2,1)}, bf16[4,128,1024]{2,1,0:T(8,128)(2,1)}) custom-call(s32[2]{0:T(128)} %pad_add_fusion.place_ref, bf16[1024,384]{1,0:T(8,128)(2,1)} %copy-done.25, bf16[384,1024]{1,0:T(8,128)(2,1)} %copy-done.26), custom_call_target="tpu_custom_call" | custom-call | flops 5000000000 | bytes 1024 | tf_op jit(solution)/shard_map/mixed/pallas_call | solution.py:1132
  180.9 8.5 %all-to-all-done.3.refs_0_ = bf16[8,128,128]{2,1,0:T(8,128)(2,1)S(1)} async-done(((bf16[8,128,128]{2,1,0:T(8,128)(2,1)}), bf16[8,128,128]{2,1,0:T(8,128)(2,1)S(1)}, u32[]{:S(2)}, u32[]{:S(2)}) %all-to-all-start.3) | async-done | bytes 262176 | tf_op jit(solution)/shard_map/all_to_all | solution.py:1369
  190.1 16.4 %back.1 = (bf16[1024,384]{1,0:T(8,128)(2,1)}, bf16[1024,1024]{1,0:T(8,128)(2,1)}, f32[8,128]{1,0:T(8,128)}, f32[8,384]{1,0:T(8,128)}, f32[8,128]{1,0:T(8,128)}) custom-call(s32[2]{0:T(128)} %pad_add_fusion.place_ref, s32[8]{0:T(128)} %bitcast.94, bf16[8,128,128]{2,1,0:T(8,128)(2,1)} %copy-done.36, f32[1024,128]{1,0:T(8,128)} %get-tuple-element.175.refs_1_, ...), custom_call_target="tpu_custom_call" | custom-call | flops 5000000000 | bytes 1024 | tf_op jit(solution)/shard_map/back/pallas_call | solution.py:1132
  206.6 5.0 %qkv_grad.1 = (bf16[2,8,48,384]{3,2,1,0:T(8,128)(2,1)}, bf16[2,8,48,384]{3,2,1,0:T(8,128)(2,1)}) custom-call(s32[2]{0:T(128)} %pad_add_fusion.place_ref, bf16[1024,1024]{1,0:T(8,128)(2,1)} %get-tuple-element.199.act1_ref, bf16[1024,384]{1,0:T(8,128)(2,1)} %get-tuple-element.200.dproj_ref, f32[8,128]{1,0:T(8,128)} %get-tuple-element.201.dlog_ref, ...), custom_call_target="tpu_custom_call" | custom-call | flops 5000000000 | bytes 1024 | tf_op jit(solution)/shard_map/qkv_grad/pallas_call | solution.py:1132
  220.1 5.2 %collective-permute-done.30 = bf16[8,48,384]{2,1,0:T(8,128)(2,1)S(1)} collective-permute-done((bf16[8,48,384]{2,1,0:T(8,128)(2,1)S(1)}, bf16[8,48,384]{2,1,0:T(8,128)(2,1)S(1)}, u32[]{:S(2)}, u32[]{:S(2)}) %collective-permute-start.30) | collective-permute-done | bytes 294944 | tf_op jit(solution)/shard_map/ppermute | solution.py:1181
  238.7 6.8 %all-to-all-done.4.refs_0_ = bf16[8,48,384]{2,1,0:T(8,128)(2,1)S(1)} async-done(((bf16[8,48,384]{2,1,0:T(8,128)(2,1)}), bf16[8,48,384]{2,1,0:T(8,128)(2,1)S(1)}, u32[]{:S(2)}, u32[]{:S(2)}) %all-to-all-start.4) | async-done | bytes 294944 | tf_op jit(solution)/shard_map/all_to_all | solution.py:1461
  245.5 3.7 %all-to-all-start.5 = ((bf16[8,32,1024]{2,1,0:T(8,128)(2,1)}), bf16[8,32,1024]{2,1,0:T(8,128)(2,1)S(1)}, u32[]{:S(2)}, u32[]{:S(2)}) async-start(bf16[8,32,1024]{2,1,0:T(8,128)(2,1)} %fusion), calls=%async_computation.7 | async-start | bytes 1048576 | tf_op jit(solution)/shard_map/all_to_all | solution.py:1437
  254.3 8.8 %all-to-all-done.5 = bf16[8,32,1024]{2,1,0:T(8,128)(2,1)S(1)} async-done(((bf16[8,32,1024]{2,1,0:T(8,128)(2,1)}), bf16[8,32,1024]{2,1,0:T(8,128)(2,1)S(1)}, u32[]{:S(2)}, u32[]{:S(2)}) %all-to-all-start.5) | async-done | bytes 524320 | tf_op jit(solution)/shard_map/all_to_all | solution.py:1437
  267.9 4.7 %lay_feed.1 = (f32[128,5632]{1,0:T(8,128)}, f32[352,1024]{1,0:T(8,128)}, f32[1,128]{1,0:T(1,128)S(1)}) custom-call(s32[2]{0:T(128)S(1)} %copy-done.24, bf16[1152,256]{1,0:T(8,128)(2,1)S(1)} %get-tuple-element.227.refs_0_, bf16[1152,256]{1,0:T(8,128)(2,1)S(1)} %collective-permute-done.37.refs_1_, bf16[2,1152,256]{2,1,0:T(8,128)(2,1)} %collective-permute-done.38.refs_2_, ...), custom_call_target="tpu_custom_call" | custom-call | flops 3000000000 | bytes 1024 | tf_op jit(solution)/shard_map/lay_feed/pallas_call | solution.py:1132
  274.9 9.6 %reduce-scatter.5.cloned.1.call-done.part_ref = bf16[128,1024]{1,0:T(8,128)(2,1)} async-done(((bf16[1024,1024]{1,0:T(8,128)(2,1)}), bf16[128,1024]{1,0:T(8,128)(2,1)}) %reduce-scatter.5.cloned.1.call-update) | async-done | bytes 262160 | tf_op jit(solution)/shard_map/reduce_scatter | solution.py:1434
  (213 shorter events, 112.9 us)
Async XLA Ops:
  7.2 58.4 %all-gather.5.cloned.1.call-start = ((), (), s32[]{:S(2)}) async-start(), calls=%async_computation.10 | async-start | bytes 1179648 | tf_op jit(solution)/shard_map/all_gather | solution.py:1209
  8.9 28.5 %collective-permute-start.6 = (bf16[64,1024]{1,0:T(8,128)(2,1)S(1)}, bf16[64,1024]{1,0:T(8,128)(2,1)S(1)}, u32[]{:S(2)}, u32[]{:S(2)}) collective-permute-start(bf16[64,1024]{1,0:T(8,128)(2,1)S(1)} %get-tuple-element.123.refs_1_), channel_id=1, source_target_pairs={{0,24},{4,28},{8,0},{12,4},{16,8},{20,12},{24,16},{28,20},{1,25},{... | collective-permute-start | bytes 393224 | tf_op jit(solution)/shard_map/ppermute | solution.py:1175
  14.0 23.5 %collective-permute-start.5 = (bf16[64,1024]{1,0:T(8,128)(2,1)S(1)}, bf16[64,1024]{1,0:T(8,128)(2,1)S(1)}, u32[]{:S(2)}, u32[]{:S(2)}) collective-permute-start(bf16[64,1024]{1,0:T(8,128)(2,1)S(1)} %get-tuple-element.123.refs_1_), channel_id=1, source_target_pairs={{0,16},{4,20},{8,24},{12,28},{16,0},{20,4},{24,8},{28,12},{1,17},{... | collective-permute-start | bytes 393224 | tf_op jit(solution)/shard_map/ppermute | solution.py:1175
  14.0 23.5 %collective-permute-start.4 = (bf16[64,1024]{1,0:T(8,128)(2,1)S(1)}, bf16[64,1024]{1,0:T(8,128)(2,1)S(1)}, u32[]{:S(2)}, u32[]{:S(2)}) collective-permute-start(bf16[64,1024]{1,0:T(8,128)(2,1)S(1)} %get-tuple-element.123.refs_1_), channel_id=1, source_target_pairs={{0,8},{4,12},{8,16},{12,20},{16,24},{20,28},{24,0},{28,4},{1,9},{5... | collective-permute-start | bytes 393224 | tf_op jit(solution)/shard_map/ppermute | solution.py:1175
  15.0 22.5 %collective-permute-start.3 = (bf16[64,1024]{1,0:T(8,128)(2,1)S(1)}, bf16[64,1024]{1,0:T(8,128)(2,1)S(1)}, u32[]{:S(2)}, u32[]{:S(2)}) collective-permute-start(bf16[64,1024]{1,0:T(8,128)(2,1)S(1)} %get-tuple-element.123.refs_1_), channel_id=1, source_target_pairs={{0,4},{4,0},{8,12},{12,8},{16,20},{20,16},{24,28},{28,24},{1,5},{5... | collective-permute-start | bytes 393224 | tf_op jit(solution)/shard_map/ppermute | solution.py:1172
  38.6 27.0 %all-to-all-start.1 = ((bf16[8,32,1024]{2,1,0:T(8,128)(2,1)}), bf16[8,32,1024]{2,1,0:T(8,128)(2,1)S(1)}, u32[]{:S(2)}, u32[]{:S(2)}) async-start(bf16[8,32,1024]{2,1,0:T(8,128)(2,1)} %broadcast_in_dim.12), calls=%async_computation.1 | async-start | bytes 1048576 | tf_op jit(solution)/shard_map/all_to_all | solution.py:1242
  44.9 81.8 %all-gather.7.cloned.1.call-start = ((), (), s32[]{:S(2)}) async-start(), calls=%async_computation.11 | async-start | bytes 2949120 | tf_op jit(solution)/shard_map/all_gather | solution.py:1240
  45.3 20.4 %collective-permute-start.1 = (bf16[2,8,144,128]{3,2,1,0:T(8,128)(2,1)S(1)}, bf16[2,8,144,128]{3,2,1,0:T(8,128)(2,1)}, u32[]{:S(2)}, u32[]{:S(2)}) collective-permute-start(bf16[2,8,144,128]{3,2,1,0:T(8,128)(2,1)S(1)} %pad_maximum_fusion.4), channel_id=1, source_target_pairs={{0,1},{1,0},{2,3},{3,2},{4,5},{5,4},{6,7},{7,6},{8,9},{9,8},{10,11... | collective-permute-start | bytes 1769480 | tf_op jit(solution)/shard_map/ppermute | solution.py:1178
  47.5 17.4 %collective-permute-start.9 = (bf16[64,1024]{1,0:T(8,128)(2,1)S(1)}, bf16[64,1024]{1,0:T(8,128)(2,1)S(1)}, u32[]{:S(2)}, u32[]{:S(2)}) collective-permute-start(bf16[64,1024]{1,0:T(8,128)(2,1)S(1)} %collective-permute-done.6.refs_7_), channel_id=1, source_target_pairs={{0,4},{4,0},{8,12},{12,8},{16,20},{20,16},{24,28},{28,24},{1,5},{5... | collective-permute-start | bytes 393224 | tf_op jit(solution)/shard_map/ppermute | solution.py:1172
  65.6 18.9 %collective-permute-start.12 = (bf16[8,32,1024]{2,1,0:T(8,128)(2,1)S(1)}, bf16[8,32,1024]{2,1,0:T(8,128)(2,1)S(1)}, u32[]{:S(2)}, u32[]{:S(2)}) collective-permute-start(bf16[8,32,1024]{2,1,0:T(8,128)(2,1)S(1)} %all-to-all-done.1.own_ref), channel_id=1, source_target_pairs={{0,2},{1,3},{2,0},{3,1},{4,6},{5,7},{6,4},{7,5},{8,10},{9,11},{10,... | collective-permute-start | bytes 1572872 | tf_op jit(solution)/shard_map/ppermute | solution.py:1181
  66.6 17.3 %collective-permute-start.11 = (bf16[128,1024]{1,0:T(8,128)(2,1)S(1)}, bf16[128,1024]{1,0:T(8,128)(2,1)S(1)}, u32[]{:S(2)}, u32[]{:S(2)}) collective-permute-start(bf16[128,1024]{1,0:T(8,128)(2,1)S(1)} %bitcast.67), channel_id=1, source_target_pairs={{0,4},{4,0},{8,12},{12,8},{16,20},{20,16},{24,28},{28,24},{1,5},{5... | collective-permute-start | bytes 786440 | tf_op jit(solution)/shard_map/ppermute | solution.py:1172
  85.6 22.9 %collective-permute-start.13 = (bf16[2,8,32,1024]{3,2,1,0:T(8,128)(2,1)}, bf16[2,8,32,1024]{3,2,1,0:T(8,128)(2,1)}, u32[]{:S(2)}, u32[]{:S(2)}) collective-permute-start(bf16[2,8,32,1024]{3,2,1,0:T(8,128)(2,1)} %pad_maximum_fusion.1), channel_id=1, source_target_pairs={{0,1},{1,0},{2,3},{3,2},{4,5},{5,4},{6,7},{7,6},{8,9},{9,8},{10,11... | collective-permute-start | bytes 3145736 | tf_op jit(solution)/shard_map/ppermute | solution.py:1178
  85.6 22.9 %all-to-all-start.2 = ((bf16[8,128,128]{2,1,0:T(8,128)(2,1)}), bf16[8,128,128]{2,1,0:T(8,128)(2,1)S(1)}, u32[]{:S(2)}, u32[]{:S(2)}) async-start(bf16[8,128,128]{2,1,0:T(8,128)(2,1)} %get-tuple-element.137), calls=%async_computation.2 | async-start | bytes 524288 | tf_op jit(solution)/shard_map/all_to_all | solution.py:1305
  90.9 115.7 %reduce-scatter.3.cloned.1.call-start = ((), (), s32[]{:S(2)}) async-start(), calls=%async_computation.8 | async-start | bytes 2949120 | tf_op jit(solution)/shard_map/reduce_scatter | solution.py:1357
  167.9 21.4 %all-to-all-start.3 = ((bf16[8,128,128]{2,1,0:T(8,128)(2,1)}), bf16[8,128,128]{2,1,0:T(8,128)(2,1)S(1)}, u32[]{:S(2)}, u32[]{:S(2)}) async-start(bf16[8,128,128]{2,1,0:T(8,128)(2,1)} %get-tuple-element.165), calls=%async_computation.3 | async-start | bytes 524288 | tf_op jit(solution)/shard_map/all_to_all | solution.py:1369
  172.5 112.0 %reduce-scatter.5.cloned.1.call-start = ((), (), s32[]{:S(2)}) async-start(), calls=%async_computation.9 | async-start | bytes 2359296 | tf_op jit(solution)/shard_map/reduce_scatter | solution.py:1434
  189.4 17.1 %collective-permute-start.25 = (bf16[2,8,32,1024]{3,2,1,0:T(8,128)(2,1)S(1)}, bf16[2,8,32,1024]{3,2,1,0:T(8,128)(2,1)S(1)}, u32[]{:S(2)}, u32[]{:S(2)}) collective-permute-start(bf16[2,8,32,1024]{3,2,1,0:T(8,128)(2,1)S(1)} %copy-done.38), channel_id=1, source_target_pairs={{0,1},{1,0},{2,3},{3,2},{4,5},{5,4},{6,7},{7,6},{8,9},{9,8},{10,11... | collective-permute-start | bytes 3145736 | tf_op jit(solution)/shard_map/ppermute | solution.py:1178
  189.4 17.1 %collective-permute-start.26 = (bf16[4,128,1024]{2,1,0:T(8,128)(2,1)}, bf16[4,128,1024]{2,1,0:T(8,128)(2,1)}, u32[]{:S(2)}, u32[]{:S(2)}) collective-permute-start(bf16[4,128,1024]{2,1,0:T(8,128)(2,1)} %get-tuple-element.194), channel_id=1, source_target_pairs={{0,1},{1,0},{2,3},{3,2},{4,5},{5,4},{6,7},{7,6},{8,9},{9,8},{10,11... | collective-permute-start | bytes 3145736 | tf_op jit(solution)/shard_map/ppermute | solution.py:1178
  216.9 19.7 %collective-permute-start.33 = (bf16[8,32,1024]{2,1,0:T(8,128)(2,1)}, bf16[8,32,1024]{2,1,0:T(8,128)(2,1)}, u32[]{:S(2)}, u32[]{:S(2)}) collective-permute-start(bf16[8,32,1024]{2,1,0:T(8,128)(2,1)} %fusion.2), channel_id=1, source_target_pairs={{0,2},{1,3},{2,0},{3,1},{4,6},{5,7},{6,4},{7,5},{8,10},{9,11},{10,... | collective-permute-start | bytes 1572872 | tf_op jit(solution)/shard_map/ppermute | solution.py:1181
  220.0 29.2 %collective-permute-start.37 = (bf16[1152,256]{1,0:T(8,128)(2,1)S(1)}, bf16[1152,256]{1,0:T(8,128)(2,1)S(1)}, u32[]{:S(2)}, u32[]{:S(2)}) collective-permute-start(bf16[1152,256]{1,0:T(8,128)(2,1)S(1)} %get-tuple-element.227.refs_0_), channel_id=1, source_target_pairs={{0,2},{1,3},{2,0},{3,1},{4,6},{5,7},{6,4},{7,5},{8,10},{9,11},{10,... | collective-permute-start | bytes 1769480 | tf_op jit(solution)/shard_map/ppermute | solution.py:1181
  227.1 18.4 %all-to-all-start.4 = ((bf16[8,48,384]{2,1,0:T(8,128)(2,1)}), bf16[8,48,384]{2,1,0:T(8,128)(2,1)S(1)}, u32[]{:S(2)}, u32[]{:S(2)}) async-start(bf16[8,48,384]{2,1,0:T(8,128)(2,1)} %fusion.1), calls=%async_computation.6 | async-start | bytes 589824 | tf_op jit(solution)/shard_map/all_to_all | solution.py:1461
  232.9 18.9 %collective-permute-start.27 = (bf16[2,128,1024]{2,1,0:T(8,128)(2,1)}, bf16[2,128,1024]{2,1,0:T(8,128)(2,1)}, u32[]{:S(2)}, u32[]{:S(2)}) collective-permute-start(bf16[2,128,1024]{2,1,0:T(8,128)(2,1)} %pad_maximum_fusion.7), channel_id=1, source_target_pairs={{0,4},{4,0},{8,12},{12,8},{16,20},{20,16},{24,28},{28,24},{1,5},{5... | collective-permute-start | bytes 1572872 | tf_op jit(solution)/shard_map/ppermute | solution.py:1172
  245.5 17.6 %all-to-all-start.5 = ((bf16[8,32,1024]{2,1,0:T(8,128)(2,1)}), bf16[8,32,1024]{2,1,0:T(8,128)(2,1)S(1)}, u32[]{:S(2)}, u32[]{:S(2)}) async-start(bf16[8,32,1024]{2,1,0:T(8,128)(2,1)} %fusion), calls=%async_computation.7 | async-start | bytes 1048576 | tf_op jit(solution)/shard_map/all_to_all | solution.py:1437
  250.4 17.6 %collective-permute-start.38 = (bf16[2,1152,256]{2,1,0:T(8,128)(2,1)}, bf16[2,1152,256]{2,1,0:T(8,128)(2,1)}, u32[]{:S(2)}, u32[]{:S(2)}) collective-permute-start(bf16[2,1152,256]{2,1,0:T(8,128)(2,1)} %pad_maximum_fusion), channel_id=1, source_target_pairs={{0,1},{1,0},{2,3},{3,2},{4,5},{5,4},{6,7},{7,6},{8,9},{9,8},{10,11... | collective-permute-start | bytes 3538952 | tf_op jit(solution)/shard_map/ppermute | solution.py:1178
  (71 other events, 603.5 us)
Sparse Core Ops, SparseCore 0:
  16.6 48.4 all-gather.4
  67.3 55.8 all-gather.6
  155.6 50.2 reduce-scatter.2
  211.7 72.7 reduce-scatter.4

commit v2 on v1

--- a/solution.py
+++ b/solution.py
@@ -639,9 +639,9 @@
         there = lax.broadcasted_iota(jnp.int32, (size, size), 1)
         cross = ((here // (2 * span)) == (there // (2 * span))) & ((here // span) != (there // span))
         for n in range(n_seq):
-            tmp[n] = mm(inv_ref[n], jnp.where(cross, lower[n], 0.0))
+            tmp[n] = mm1(inv_ref[n], jnp.where(cross, lower[n], 0.0))
         for n in range(n_seq):
-            inv_ref[n] = inv_ref[n] - mm(tmp[n], inv_ref[n])
+            inv_ref[n] = inv_ref[n] - mm1(tmp[n], inv_ref[n])
         span *= 2
     for n in range(n_seq):
         keep, tail, whole = marks[n]
@@ -739,12 +739,12 @@
         lean = d_act2 * head_gain
         d_out = inv * (lean - ohat * jnp.mean(lean * ohat, -1, keepdims=True))
         do_scr[rows, :] = d_out
-        g_scr[rows, :] = mm(att_ref[n], d_out, TN)
+        g_scr[rows, :] = mm1(att_ref[n], d_out, TN)
     ghead_ref[...] = jnp.broadcast_to(ghead, ghead_ref.shape)
     for n in range(n_seq):
         rows = pl.ds(n * size, size)
         col, keep, tail, whole = marks[n]
-        add[n] = mm(q_scr[rows, :], (scale * keep) * do_scr[rows, :], TN) - mm(w_ref[n], keep * g_scr[rows, :], TN)
+        add[n] = mm1(q_scr[rows, :], (scale * keep) * do_scr[rows, :], TN) - mm1(w_ref[n], keep * g_scr[rows, :], TN)
     grad = jnp.zeros((dk, dk), F32)
     for n in range(n_seq - 1, -1, -1):
         x_scr[n] = grad
@@ -764,16 +764,16 @@
         value = act[:, 2 * dk :].astype(BF).astype(F32)
         grad, state, u = x_scr[n], s_ref[n], u_ref[n]
         d_out = do_scr[rows, :]
-        d_u = g_scr[rows, :] + tail * mm(key, grad)
-        d_r = mm(inv_ref[n], d_u, TN)
-        d_att = jnp.where(incl, mm(d_out, u, NT), 0.0)
-        d_low = jnp.where(strict, -mm(d_r, u, NT), 0.0)
-        d_q = keep * mm(d_out, state, NT) + mm(d_att, key)
-        d_kb = mm(d_low, key) - keep * mm(d_r, state, NT)
+        d_u = g_scr[rows, :] + tail * mm1(key, grad)
+        d_r = mm1(inv_ref[n], d_u, TN)
+        d_att = jnp.where(incl, mm1(d_out, u, NT), 0.0)
+        d_low = jnp.where(strict, -mm1(d_r, u, NT), 0.0)
+        d_q = keep * mm1(d_out, state, NT) + mm1(d_att, key)
+        d_kb = mm1(d_low, key) - keep * mm1(d_r, state, NT)
         d_k = (
-            scale * mm(d_att, q, TN)
-            + mm(d_low, rate * key_f, TN)
-            + tail * mm(u, grad, NT)
+            scale * mm1(d_att, q, TN)
+            + mm1(d_low, rate * key_f, TN)
+            + tail * mm1(u, grad, NT)
             + rate * d_kb
         )
         d_v = rate * d_r
@@ -1335,14 +1335,7 @@
         mib=24,
         name="feed",
     )
-    d_got, d_own, act4, d_gu, act3_all, cot_all = stage(core(d_next), d_own, act4, d_gu, act3_all, cot_all)
-    top, low = slice(0, mid_row), slice(mid_row, size)
-
-    def core_sum(i, part):
-        return d_own[i, part].astype(F32) + d_got[i, part].astype(F32)
-
-    d_x = flip(jnp.stack([core_sum(2, top), core_sum(3, top)]).astype(BF))
-    d_y = across(jnp.stack([core_sum(1, low), core_sum(3, low)]).astype(BF))
+    d_got = core(d_next)
     (grads,) = local_call(
         functools.partial(grads_kernel, hidden),
         [shape((half, pack_rows, 256), BF)],
@@ -1353,11 +1346,21 @@
         mib=24,
         name="grads",
     )
-    d_x, d_y, grads, act4 = stage(d_x, d_y, grads, act4)
+    d_got, d_own, act4, grads = stage(d_got, d_own, act4, grads)
     grads = lax.psum_scatter(grads, "seq", scatter_dimension=0, axis_index_groups=groups_z)
+    top, low = slice(0, mid_row), slice(mid_row, size)
+
+    def core_sum(i, part):
+        return d_own[i, part].astype(F32) + d_got[i, part].astype(F32)
+
+    d_x = flip(jnp.stack([core_sum(2, top), core_sum(3, top)]).astype(BF))
+    d_y = across(jnp.stack([core_sum(1, low), core_sum(3, low)]).astype(BF))
+    mixed_own, mixed_next = local_call(
+        mixed_kernel, [four, four], [where_at, act4, w_down], smem=1, us=5, name="mixed"
+    )
+    d_x, d_y, mixed_own, mixed_next = stage(d_x, d_y, mixed_own, mixed_next)
     d_top = across((core_sum(1, top) + d_x[1].astype(F32)).astype(BF))
     d_bottom = flip((core_sum(2, low) + d_y[1].astype(F32)).astype(BF))
-    d_top, d_bottom, act4 = stage(d_top, d_bottom, act4)
     d_resid, d_low, d_act2 = local_call(
         functools.partial(turn_kernel, n_seq),
         [shape((size, width), F32), shape((size, width), BF), shape((n_seq, size, dk), BF)],
@@ -1376,9 +1379,6 @@
         smem=1,
         us=3,
         name="out_grad",
-    )
-    mixed_own, mixed_next = local_call(
-        mixed_kernel, [four, four], [where_at, act4, w_down], smem=1, us=5, name="mixed"
     )
     d_act2, out_same, out_other, mixed_own, mixed_next = stage(d_act2, out_same, out_other, mixed_own, mixed_next)
     mixed_got = core(mixed_next)
@@ -1423,7 +1423,7 @@
             pltpu.VMEM((total, dk), BF),
         ],
         smem=2,
-        us=5,
+        us=14,
         name="back",
     )
     d_proj, parts, d_log, g_conv, g_head, out_got, mixed_got, grads = stage(
@@ -1479,7 +1479,7 @@
         [where_at, feed_part, feed_y, feed_cores, gate_up_weight, norm_gains],
         scratch=[pltpu.VMEM((n_row, 2, size, 2 * wide), BF)],
         smem=1,
-        us=3,
+        us=0,
         mib=24,
         name="lay_feed",
     )

time: 298 us -> 294 us (0.987)
    ppermute x12, waiting for transfers between devices: 17.3 us -> 26.7 us  [across(): return lax.ppermute(v, 'row', [(r, r ^ 2) for r in range(n_row)])]
    reduce_scatter x1, waiting for transfers between devices: 9.58 us -> 2.92 us  [head_plan(): d_act1 = lax.psum_scatter(parts, 'seq', scatter_dimension=0, tiled=True)]
    all_to_all x1, waiting for transfers between devices: 8.77 us -> 3.08 us  [head_plan(): lax.all_to_all((out_mine + out_y.astype(F32)).astype(BF), 'seq', 0, 0)]
    all_to_all x1, waiting for transfers between devices: 8.51 us -> 13.5 us  [head_plan(): d_act2 = lax.all_to_all(d_act2, 'seq', 0, 0)]
    unnamed x94 -> x98, local copies, waits for them, and re-layouts: 13.3 us -> 14.8 us
  transfers between devices with their start and end apart: 49 -> 49, of which waited for: 24 -> 26; matrix products, arithmetic and copies ran while one was open for 8% -> 7% of each run, Pallas kernels for 20% -> 21%
where the time goes in v2:
time: 294 us; the launch traced here: 289 us
  waiting for transfers between devices  103 us (35%)
  Pallas kernels  69.1 us (24%)
  starting transfers between devices  65.9 us (22%)
  local copies, waits for them, and re-layouts  18.5 us (6%)
  other arithmetic  18.1 us (6%)
  between operations  14.6 us (5%)
    pallas_call x14, Pallas kernels, local_call(): pl.pallas_call(kernel, out_shape=tuple(outs), in_specs=space, out_specs=t...  69.1 us
    ppermute x13, waiting for transfers between devices, flip(): return lax.ppermute(v, 'seq', [(s, s ^ 1) for s in range(n_seq)])  42.1 us
    ppermute x12, waiting for transfers between devices, across(): return lax.ppermute(v, 'row', [(r, r ^ 2) for r in range(n_row)])  26.7 us
    ppermute x13, starting transfers between devices, flip(): return lax.ppermute(v, 'seq', [(s, s ^ 1) for s in range(n_seq)])  19.8 us
    unnamed x98, local copies, waits for them, and re-layouts  14.8 us
    all_to_all x1, waiting for transfers between devices, head_plan(): d_act2 = lax.all_to_all(d_act2, 'seq', 0, 0)  13.5 us
    ppermute x12, starting transfers between devices, across(): return lax.ppermute(v, 'row', [(r, r ^ 2) for r in range(n_row)])  10.5 us
    all_to_all x1, waiting for transfers between devices, head_plan(): act2 = lax.all_to_all(act2, 'seq', 0, 0)  6.87 us
  transfers between devices with their start and end apart: 49, of which 26 were waited for; matrix products, arithmetic and copies ran while one was open for 7% of the time, Pallas kernels for 21%

profile of v2, /device:TPU:0, one launch (start us, length us, event | category | flops | bytes accessed | tf_op | source)
XLA Modules:
  0.0 289.2 jit_solution(8831360496388227791)
XLA Ops:
  8.9 5.0 %collective-permute-start.6 = (bf16[64,1024]{1,0:T(8,128)(2,1)S(1)}, bf16[64,1024]{1,0:T(8,128)(2,1)S(1)}, u32[]{:S(2)}, u32[]{:S(2)}) collective-permute-start(bf16[64,1024]{1,0:T(8,128)(2,1)S(1)} %get-tuple-element.118.refs_1_), channel_id=1, source_target_pairs={{0,24},{4,28},{8,0},{12,4},{16,8},{20,12},{24,16},{28,20},{1,25},{... | collective-permute-start | bytes 393224 | tf_op jit(solution)/shard_map/ppermute | solution.py:1175
  19.1 4.1 %all-to-all-start = ((bf16[8,144,128]{2,1,0:T(8,128)(2,1)}), bf16[8,144,128]{2,1,0:T(8,128)(2,1)S(1)}, u32[]{:S(2)}, u32[]{:S(2)}) async-start(bf16[8,144,128]{2,1,0:T(8,128)(2,1)} %lead.1), calls=%async_computation | async-start | bytes 589824 | tf_op jit(solution)/shard_map/all_to_all | solution.py:1234
  28.9 5.9 %collective-permute-done.2 = bf16[384,256]{1,0:T(8,128)(2,1)S(1)} collective-permute-done((bf16[384,256]{1,0:T(8,128)(2,1)}, bf16[384,256]{1,0:T(8,128)(2,1)S(1)}, u32[]{:S(2)}, u32[]{:S(2)}) %collective-permute-start.2) | collective-permute-done | bytes 196640 | tf_op jit(solution)/shard_map/ppermute | solution.py:1172
  38.6 6.2 %all-to-all-start.1 = ((bf16[8,32,1024]{2,1,0:T(8,128)(2,1)}), bf16[8,32,1024]{2,1,0:T(8,128)(2,1)S(1)}, u32[]{:S(2)}, u32[]{:S(2)}) async-start(bf16[8,32,1024]{2,1,0:T(8,128)(2,1)} %broadcast_in_dim.12), calls=%async_computation.1 | async-start | bytes 1048576 | tf_op jit(solution)/shard_map/all_to_all | solution.py:1242
  49.4 9.7 %collective-permute-done.7.refs_4_ = bf16[64,1024]{1,0:T(8,128)(2,1)S(1)} collective-permute-done((bf16[64,1024]{1,0:T(8,128)(2,1)}, bf16[64,1024]{1,0:T(8,128)(2,1)S(1)}, u32[]{:S(2)}, u32[]{:S(2)}) %collective-permute-start.7) | collective-permute-done | bytes 131104 | tf_op jit(solution)/shard_map/ppermute | solution.py:1172
  69.7 12.8 %front.1 = (bf16[1024,384]{1,0:T(8,128)(2,1)}, bf16[1024,1024]{1,0:T(8,128)(2,1)}, bf16[1024,384]{1,0:T(8,128)(2,1)}, f32[1024,128]{1,0:T(8,128)}, f32[1024,128]...) custom-call(s32[2]{0:T(128)} %pad_add_fusion.place_ref, ...), custom_call_target="tpu_custom_call" | custom-call | flops 4000000000 | bytes 1024 | tf_op jit(solution)/shard_map/front/pallas_call | solution.py:1132
  85.3 5.4 %all-to-all-start.2 = ((bf16[8,128,128]{2,1,0:T(8,128)(2,1)}), bf16[8,128,128]{2,1,0:T(8,128)(2,1)S(1)}, u32[]{:S(2)}, u32[]{:S(2)}) async-start(bf16[8,128,128]{2,1,0:T(8,128)(2,1)} %get-tuple-element.132), calls=%async_computation.2 | async-start | bytes 524288 | tf_op jit(solution)/shard_map/all_to_all | solution.py:1305
  93.0 8.4 %collective-permute-done.14.refs_8_ = bf16[128,1024]{1,0:T(8,128)(2,1)S(1)} collective-permute-done((bf16[128,1024]{1,0:T(8,128)(2,1)S(1)}, bf16[128,1024]{1,0:T(8,128)(2,1)S(1)}, u32[]{:S(2)}, u32[]{:S(2)}) %collective-permute-start.14) | collective-permute-done | bytes 262176 | tf_op jit(solution)/shard_map/ppermute | solution.py:1172
  101.5 6.9 %all-to-all-done.2.act2_ref = bf16[8,128,128]{2,1,0:T(8,128)(2,1)S(1)} async-done(((bf16[8,128,128]{2,1,0:T(8,128)(2,1)}), bf16[8,128,128]{2,1,0:T(8,128)(2,1)S(1)}, u32[]{:S(2)}, u32[]{:S(2)}) %all-to-all-start.2) | async-done | bytes 262176 | tf_op jit(solution)/shard_map/all_to_all | solution.py:1305
  112.0 6.0 %collective-permute-done.15.refs_1_ = bf16[128,1024]{1,0:T(8,128)(2,1)S(1)} collective-permute-done((bf16[128,1024]{1,0:T(8,128)(2,1)S(1)}, bf16[128,1024]{1,0:T(8,128)(2,1)S(1)}, u32[]{:S(2)}, u32[]{:S(2)}) %collective-permute-start.15) | collective-permute-done | bytes 262176 | tf_op jit(solution)/shard_map/ppermute | solution.py:1181
  120.6 4.2 %collective-permute-done.17.refs_3_ = bf16[128,1024]{1,0:T(8,128)(2,1)S(1)} collective-permute-done((bf16[128,1024]{1,0:T(8,128)(2,1)S(1)}, bf16[128,1024]{1,0:T(8,128)(2,1)S(1)}, u32[]{:S(2)}, u32[]{:S(2)}) %collective-permute-start.17) | collective-permute-done | bytes 262176 | tf_op jit(solution)/shard_map/ppermute | solution.py:1172
  134.4 8.6 %feed.1 = (bf16[4,128,1024]{2,1,0:T(8,128)(2,1)S(1)}, bf16[4,128,1024]{2,1,0:T(8,128)(2,1)}, bf16[1024,384]{1,0:T(8,128)(2,1)S(1)}, bf16[1024,768]{1,0:T(8,128)(...) custom-call(s32[2]{0:T(128)S(1)} %copy-done.15, ...), custom_call_target="tpu_custom_call" | custom-call | flops 3000000000 | bytes 1024 | tf_op jit(solution)/shard_map/feed/pallas_call | solution.py:1132
  152.1 4.8 %mixed.1 = (bf16[4,128,1024]{2,1,0:T(8,128)(2,1)}, bf16[4,128,1024]{2,1,0:T(8,128)(2,1)}) custom-call(s32[2]{0:T(128)} %pad_add_fusion.place_ref, bf16[1024,384]{1,0:T(8,128)(2,1)} %copy-done.26, bf16[384,1024]{1,0:T(8,128)(2,1)} %copy-done.27), custom_call_target="tpu_custom_call" | custom-call | flops 5000000000 | bytes 1024 | tf_op jit(solution)/shard_map/mixed/pallas_call | solution.py:1132
  161.1 3.8 %collective-permute-done.24.bottom_ref = bf16[64,1024]{1,0:T(8,128)(2,1)S(1)} collective-permute-done((bf16[64,1024]{1,0:T(8,128)(2,1)S(1)}, bf16[64,1024]{1,0:T(8,128)(2,1)S(1)}, u32[]{:S(2)}, u32[]{:S(2)}) %collective-permute-start.24) | collective-permute-done | bytes 131104 | tf_op jit(solution)/shard_map/ppermute | solution.py:1172
  168.7 4.5 %all-to-all-start.3 = ((bf16[8,128,128]{2,1,0:T(8,128)(2,1)}), bf16[8,128,128]{2,1,0:T(8,128)(2,1)S(1)}, u32[]{:S(2)}, u32[]{:S(2)}) async-start(bf16[8,128,128]{2,1,0:T(8,128)(2,1)} %get-tuple-element.157), calls=%async_computation.3 | async-start | bytes 524288 | tf_op jit(solution)/shard_map/all_to_all | solution.py:1372
  177.1 13.5 %all-to-all-done.3.refs_0_ = bf16[8,128,128]{2,1,0:T(8,128)(2,1)S(1)} async-done(((bf16[8,128,128]{2,1,0:T(8,128)(2,1)}), bf16[8,128,128]{2,1,0:T(8,128)(2,1)S(1)}, u32[]{:S(2)}, u32[]{:S(2)}) %all-to-all-start.3) | async-done | bytes 262176 | tf_op jit(solution)/shard_map/all_to_all | solution.py:1372
  191.2 14.6 %back.1 = (bf16[1024,384]{1,0:T(8,128)(2,1)}, bf16[1024,1024]{1,0:T(8,128)(2,1)}, f32[8,128]{1,0:T(8,128)}, f32[8,384]{1,0:T(8,128)}, f32[8,128]{1,0:T(8,128)}) custom-call(s32[2]{0:T(128)} %pad_add_fusion.place_ref, s32[8]{0:T(128)} %bitcast.94, bf16[8,128,128]{2,1,0:T(8,128)(2,1)} %copy-done.37, f32[1024,128]{1,0:T(8,128)} %get-tuple-element.165.refs_1_, ...), custom_call_target="tpu_custom_call" | custom-call | flops 14000000000 | bytes 1024 | tf_op jit(solution)/shard_map/back/pallas_call | solution.py:1132
  205.9 4.8 %qkv_grad.1 = (bf16[2,8,48,384]{3,2,1,0:T(8,128)(2,1)}, bf16[2,8,48,384]{3,2,1,0:T(8,128)(2,1)}) custom-call(s32[2]{0:T(128)} %pad_add_fusion.place_ref, bf16[1024,1024]{1,0:T(8,128)(2,1)} %get-tuple-element.189.act1_ref, bf16[1024,384]{1,0:T(8,128)(2,1)} %get-tuple-element.190.dproj_ref, f32[8,128]{1,0:T(8,128)} %get-tuple-element.191.dlog_ref, ...), custom_call_target="tpu_custom_call" | custom-call | flops 5000000000 | bytes 1024 | tf_op jit(solution)/shard_map/qkv_grad/pallas_call | solution.py:1132
  220.3 3.7 %collective-permute-done.30 = bf16[8,48,384]{2,1,0:T(8,128)(2,1)S(1)} collective-permute-done((bf16[8,48,384]{2,1,0:T(8,128)(2,1)S(1)}, bf16[8,48,384]{2,1,0:T(8,128)(2,1)S(1)}, u32[]{:S(2)}, u32[]{:S(2)}) %collective-permute-start.30) | collective-permute-done | bytes 294944 | tf_op jit(solution)/shard_map/ppermute | solution.py:1181
  237.4 4.2 %all-to-all-done.4.refs_0_ = bf16[8,48,384]{2,1,0:T(8,128)(2,1)S(1)} async-done(((bf16[8,48,384]{2,1,0:T(8,128)(2,1)}), bf16[8,48,384]{2,1,0:T(8,128)(2,1)S(1)}, u32[]{:S(2)}, u32[]{:S(2)}) %all-to-all-start.4) | async-done | bytes 294944 | tf_op jit(solution)/shard_map/all_to_all | solution.py:1461
  241.6 4.1 %all-to-all-start.5 = ((bf16[8,32,1024]{2,1,0:T(8,128)(2,1)}), bf16[8,32,1024]{2,1,0:T(8,128)(2,1)}, u32[]{:S(2)}, u32[]{:S(2)}) async-start(bf16[8,32,1024]{2,1,0:T(8,128)(2,1)} %fusion), calls=%async_computation.7 | async-start | bytes 1048576 | tf_op jit(solution)/shard_map/all_to_all | solution.py:1437
  248.1 6.1 %collective-permute-done.31.refs_1_ = bf16[8,48,384]{2,1,0:T(8,128)(2,1)S(1)} collective-permute-done((bf16[8,48,384]{2,1,0:T(8,128)(2,1)S(1)}, bf16[8,48,384]{2,1,0:T(8,128)(2,1)S(1)}, u32[]{:S(2)}, u32[]{:S(2)}) %collective-permute-start.31) | collective-permute-done | bytes 294944 | tf_op jit(solution)/shard_map/ppermute | solution.py:1181
  262.2 4.4 %collective-permute-done.34.refs_4_ = bf16[32,1024]{1,0:T(8,128)(2,1)S(1)} collective-permute-done((bf16[32,1024]{1,0:T(8,128)(2,1)S(1)}, bf16[32,1024]{1,0:T(8,128)(2,1)S(1)}, u32[]{:S(2)}, u32[]{:S(2)}) %collective-permute-start.34) | collective-permute-done | bytes 65568 | tf_op jit(solution)/shard_map/ppermute | solution.py:1181
  270.1 4.7 %lay_feed.1 = (f32[128,5632]{1,0:T(8,128)}, f32[352,1024]{1,0:T(8,128)}, f32[1,128]{1,0:T(1,128)S(1)}) custom-call(s32[2]{0:T(128)S(1)} %copy-done.16, bf16[1152,256]{1,0:T(8,128)(2,1)S(1)} %get-tuple-element.217.refs_0_, bf16[1152,256]{1,0:T(8,128)(2,1)S(1)} %collective-permute-done.37.refs_1_, bf16[2,1152,256]{2,1,0:T(8,128)(2,1)} %collective-permute-done.38.refs_2_, ...), custom_call_target="tpu_custom_call" | custom-call | bytes 1024 | tf_op jit(solution)/shard_map/lay_feed/pallas_call | solution.py:1132
  (217 shorter events, 118.0 us)
Async XLA Ops:
  7.2 58.3 %all-gather.5.cloned.1.call-start = ((), (), s32[]{:S(2)}) async-start(), calls=%async_computation.10 | async-start | bytes 1179648 | tf_op jit(solution)/shard_map/all_gather | solution.py:1209
  8.9 28.6 %collective-permute-start.6 = (bf16[64,1024]{1,0:T(8,128)(2,1)S(1)}, bf16[64,1024]{1,0:T(8,128)(2,1)S(1)}, u32[]{:S(2)}, u32[]{:S(2)}) collective-permute-start(bf16[64,1024]{1,0:T(8,128)(2,1)S(1)} %get-tuple-element.118.refs_1_), channel_id=1, source_target_pairs={{0,24},{4,28},{8,0},{12,4},{16,8},{20,12},{24,16},{28,20},{1,25},{... | collective-permute-start | bytes 393224 | tf_op jit(solution)/shard_map/ppermute | solution.py:1175
  13.9 23.6 %collective-permute-start.5 = (bf16[64,1024]{1,0:T(8,128)(2,1)S(1)}, bf16[64,1024]{1,0:T(8,128)(2,1)S(1)}, u32[]{:S(2)}, u32[]{:S(2)}) collective-permute-start(bf16[64,1024]{1,0:T(8,128)(2,1)S(1)} %get-tuple-element.118.refs_1_), channel_id=1, source_target_pairs={{0,16},{4,20},{8,24},{12,28},{16,0},{20,4},{24,8},{28,12},{1,17},{... | collective-permute-start | bytes 393224 | tf_op jit(solution)/shard_map/ppermute | solution.py:1175
  13.9 23.6 %collective-permute-start.4 = (bf16[64,1024]{1,0:T(8,128)(2,1)S(1)}, bf16[64,1024]{1,0:T(8,128)(2,1)S(1)}, u32[]{:S(2)}, u32[]{:S(2)}) collective-permute-start(bf16[64,1024]{1,0:T(8,128)(2,1)S(1)} %get-tuple-element.118.refs_1_), channel_id=1, source_target_pairs={{0,8},{4,12},{8,16},{12,20},{16,24},{20,28},{24,0},{28,4},{1,9},{5... | collective-permute-start | bytes 393224 | tf_op jit(solution)/shard_map/ppermute | solution.py:1175
  15.0 22.6 %collective-permute-start.3 = (bf16[64,1024]{1,0:T(8,128)(2,1)S(1)}, bf16[64,1024]{1,0:T(8,128)(2,1)S(1)}, u32[]{:S(2)}, u32[]{:S(2)}) collective-permute-start(bf16[64,1024]{1,0:T(8,128)(2,1)S(1)} %get-tuple-element.118.refs_1_), channel_id=1, source_target_pairs={{0,4},{4,0},{8,12},{12,8},{16,20},{20,16},{24,28},{28,24},{1,5},{5... | collective-permute-start | bytes 393224 | tf_op jit(solution)/shard_map/ppermute | solution.py:1172
  38.6 26.9 %all-to-all-start.1 = ((bf16[8,32,1024]{2,1,0:T(8,128)(2,1)}), bf16[8,32,1024]{2,1,0:T(8,128)(2,1)S(1)}, u32[]{:S(2)}, u32[]{:S(2)}) async-start(bf16[8,32,1024]{2,1,0:T(8,128)(2,1)} %broadcast_in_dim.12), calls=%async_computation.1 | async-start | bytes 1048576 | tf_op jit(solution)/shard_map/all_to_all | solution.py:1242
  44.9 81.7 %all-gather.7.cloned.1.call-start = ((), (), s32[]{:S(2)}) async-start(), calls=%async_computation.11 | async-start | bytes 2949120 | tf_op jit(solution)/shard_map/all_gather | solution.py:1240
  45.2 20.4 %collective-permute-start.1 = (bf16[2,8,144,128]{3,2,1,0:T(8,128)(2,1)S(1)}, bf16[2,8,144,128]{3,2,1,0:T(8,128)(2,1)S(1)}, u32[]{:S(2)}, u32[]{:S(2)}) collective-permute-start(bf16[2,8,144,128]{3,2,1,0:T(8,128)(2,1)S(1)} %pad_maximum_fusion.4), channel_id=1, source_target_pairs={{0,1},{1,0},{2,3},{3,2},{4,5},{5,4},{6,7},{7,6},{8,9},{9,8},{10,11... | collective-permute-start | bytes 1769480 | tf_op jit(solution)/shard_map/ppermute | solution.py:1178
  47.4 17.4 %collective-permute-start.9 = (bf16[64,1024]{1,0:T(8,128)(2,1)S(1)}, bf16[64,1024]{1,0:T(8,128)(2,1)S(1)}, u32[]{:S(2)}, u32[]{:S(2)}) collective-permute-start(bf16[64,1024]{1,0:T(8,128)(2,1)S(1)} %collective-permute-done.6.refs_7_), channel_id=1, source_target_pairs={{0,4},{4,0},{8,12},{12,8},{16,20},{20,16},{24,28},{28,24},{1,5},{5... | collective-permute-start | bytes 393224 | tf_op jit(solution)/shard_map/ppermute | solution.py:1172
  65.5 18.7 %collective-permute-start.12 = (bf16[8,32,1024]{2,1,0:T(8,128)(2,1)S(1)}, bf16[8,32,1024]{2,1,0:T(8,128)(2,1)S(1)}, u32[]{:S(2)}, u32[]{:S(2)}) collective-permute-start(bf16[8,32,1024]{2,1,0:T(8,128)(2,1)S(1)} %all-to-all-done.1.own_ref), channel_id=1, source_target_pairs={{0,2},{1,3},{2,0},{3,1},{4,6},{5,7},{6,4},{7,5},{8,10},{9,11},{10,... | collective-permute-start | bytes 1572872 | tf_op jit(solution)/shard_map/ppermute | solution.py:1181
  66.5 16.0 %collective-permute-start.11 = (bf16[128,1024]{1,0:T(8,128)(2,1)S(1)}, bf16[128,1024]{1,0:T(8,128)(2,1)S(1)}, u32[]{:S(2)}, u32[]{:S(2)}) collective-permute-start(bf16[128,1024]{1,0:T(8,128)(2,1)S(1)} %bitcast.68), channel_id=1, source_target_pairs={{0,4},{4,0},{8,12},{12,8},{16,20},{20,16},{24,28},{28,24},{1,5},{5... | collective-permute-start | bytes 786440 | tf_op jit(solution)/shard_map/ppermute | solution.py:1172
  68.2 16.1 %collective-permute-start.10 = (bf16[128,1024]{1,0:T(8,128)(2,1)S(1)}, bf16[128,1024]{1,0:T(8,128)(2,1)S(1)}, u32[]{:S(2)}, u32[]{:S(2)}) collective-permute-start(bf16[128,1024]{1,0:T(8,128)(2,1)S(1)} %bitcast.69), channel_id=1, source_target_pairs={{0,2},{1,3},{2,0},{3,1},{4,6},{5,7},{6,4},{7,5},{8,10},{9,11},{10,... | collective-permute-start | bytes 786440 | tf_op jit(solution)/shard_map/ppermute | solution.py:1181
  85.3 23.0 %collective-permute-start.13 = (bf16[2,8,32,1024]{3,2,1,0:T(8,128)(2,1)}, bf16[2,8,32,1024]{3,2,1,0:T(8,128)(2,1)}, u32[]{:S(2)}, u32[]{:S(2)}) collective-permute-start(bf16[2,8,32,1024]{3,2,1,0:T(8,128)(2,1)} %pad_maximum_fusion.1), channel_id=1, source_target_pairs={{0,1},{1,0},{2,3},{3,2},{4,5},{5,4},{6,7},{7,6},{8,9},{9,8},{10,11... | collective-permute-start | bytes 3145736 | tf_op jit(solution)/shard_map/ppermute | solution.py:1178
  85.3 23.0 %all-to-all-start.2 = ((bf16[8,128,128]{2,1,0:T(8,128)(2,1)}), bf16[8,128,128]{2,1,0:T(8,128)(2,1)S(1)}, u32[]{:S(2)}, u32[]{:S(2)}) async-start(bf16[8,128,128]{2,1,0:T(8,128)(2,1)} %get-tuple-element.132), calls=%async_computation.2 | async-start | bytes 524288 | tf_op jit(solution)/shard_map/all_to_all | solution.py:1305
  90.7 115.1 %reduce-scatter.3.cloned.1.call-start = ((), (), s32[]{:S(2)}) async-start(), calls=%async_computation.8 | async-start | bytes 2949120 | tf_op jit(solution)/shard_map/reduce_scatter | solution.py:1350
  168.7 21.8 %all-to-all-start.3 = ((bf16[8,128,128]{2,1,0:T(8,128)(2,1)}), bf16[8,128,128]{2,1,0:T(8,128)(2,1)S(1)}, u32[]{:S(2)}, u32[]{:S(2)}) async-start(bf16[8,128,128]{2,1,0:T(8,128)(2,1)} %get-tuple-element.157), calls=%async_computation.3 | async-start | bytes 524288 | tf_op jit(solution)/shard_map/all_to_all | solution.py:1372
  173.3 107.3 %reduce-scatter.5.cloned.1.call-start = ((), (), s32[]{:S(2)}) async-start(), calls=%async_computation.9 | async-start | bytes 2359296 | tf_op jit(solution)/shard_map/reduce_scatter | solution.py:1434
  215.1 20.2 %collective-permute-start.33 = (bf16[8,32,1024]{2,1,0:T(8,128)(2,1)}, bf16[8,32,1024]{2,1,0:T(8,128)(2,1)}, u32[]{:S(2)}, u32[]{:S(2)}) collective-permute-start(bf16[8,32,1024]{2,1,0:T(8,128)(2,1)} %fusion.2), channel_id=1, source_target_pairs={{0,2},{1,3},{2,0},{3,1},{4,6},{5,7},{6,4},{7,5},{8,10},{9,11},{10,... | collective-permute-start | bytes 1572872 | tf_op jit(solution)/shard_map/ppermute | solution.py:1181
  220.2 26.8 %collective-permute-start.37 = (bf16[1152,256]{1,0:T(8,128)(2,1)S(1)}, bf16[1152,256]{1,0:T(8,128)(2,1)S(1)}, u32[]{:S(2)}, u32[]{:S(2)}) collective-permute-start(bf16[1152,256]{1,0:T(8,128)(2,1)S(1)} %get-tuple-element.217.refs_0_), channel_id=1, source_target_pairs={{0,2},{1,3},{2,0},{3,1},{4,6},{5,7},{6,4},{7,5},{8,10},{9,11},{10,... | collective-permute-start | bytes 1769480 | tf_op jit(solution)/shard_map/ppermute | solution.py:1181
  224.8 16.9 %all-to-all-start.4 = ((bf16[8,48,384]{2,1,0:T(8,128)(2,1)}), bf16[8,48,384]{2,1,0:T(8,128)(2,1)S(1)}, u32[]{:S(2)}, u32[]{:S(2)}) async-start(bf16[8,48,384]{2,1,0:T(8,128)(2,1)} %fusion.1), calls=%async_computation.6 | async-start | bytes 589824 | tf_op jit(solution)/shard_map/all_to_all | solution.py:1461
  230.6 24.6 %collective-permute-start.27 = (bf16[2,128,1024]{2,1,0:T(8,128)(2,1)}, bf16[2,128,1024]{2,1,0:T(8,128)(2,1)}, u32[]{:S(2)}, u32[]{:S(2)}) collective-permute-start(bf16[2,128,1024]{2,1,0:T(8,128)(2,1)} %pad_maximum_fusion.7), channel_id=1, source_target_pairs={{0,4},{4,0},{8,12},{12,8},{16,20},{20,16},{24,28},{28,24},{1,5},{5... | collective-permute-start | bytes 1572872 | tf_op jit(solution)/shard_map/ppermute | solution.py:1172
  241.6 18.6 %all-to-all-start.5 = ((bf16[8,32,1024]{2,1,0:T(8,128)(2,1)}), bf16[8,32,1024]{2,1,0:T(8,128)(2,1)}, u32[]{:S(2)}, u32[]{:S(2)}) async-start(bf16[8,32,1024]{2,1,0:T(8,128)(2,1)} %fusion), calls=%async_computation.7 | async-start | bytes 1048576 | tf_op jit(solution)/shard_map/all_to_all | solution.py:1437
  248.1 20.6 %collective-permute-start.38 = (bf16[2,1152,256]{2,1,0:T(8,128)(2,1)}, bf16[2,1152,256]{2,1,0:T(8,128)(2,1)}, u32[]{:S(2)}, u32[]{:S(2)}) collective-permute-start(bf16[2,1152,256]{2,1,0:T(8,128)(2,1)} %pad_maximum_fusion), channel_id=1, source_target_pairs={{0,1},{1,0},{2,3},{3,2},{4,5},{5,4},{6,7},{7,6},{8,9},{9,8},{10,11... | collective-permute-start | bytes 3538952 | tf_op jit(solution)/shard_map/ppermute | solution.py:1178
  255.2 19.6 %collective-permute-start.32 = (bf16[2,8,48,384]{3,2,1,0:T(8,128)(2,1)}, bf16[2,8,48,384]{3,2,1,0:T(8,128)(2,1)}, u32[]{:S(2)}, u32[]{:S(2)}) collective-permute-start(bf16[2,8,48,384]{3,2,1,0:T(8,128)(2,1)} %pad_maximum_fusion.5), channel_id=1, source_target_pairs={{0,1},{1,0},{2,3},{3,2},{4,5},{5,4},{6,7},{7,6},{8,9},{9,8},{10,11... | collective-permute-start | bytes 1769480 | tf_op jit(solution)/shard_map/ppermute | solution.py:1178
  (73 other events, 594.2 us)
Sparse Core Ops, SparseCore 0:
  16.6 48.6 all-gather.4
  67.4 55.6 all-gather.6
  149.7 51.1 reduce-scatter.2
  206.0 74.4 reduce-scatter.4

commit v3 on v2

--- a/solution.py
+++ b/solution.py
@@ -908,8 +908,8 @@
 
 
 def feed_kernel(hidden, place_ref, *refs):
-    act3_refs, core_ref, cot_refs, cot_core_ref, packs_ref = refs[0:4], refs[4], refs[5:9], refs[9], refs[10]
-    own_ref, next_ref, act4_ref, dgu_ref, act3_ref, cot_ref, down_ref, gu, down32 = refs[11:]
+    act3_refs, core_ref, cot_refs, cot_core_ref, packs_ref = refs[0:5], refs[5], refs[6:10], refs[10], refs[11]
+    own_ref, next_ref, act4_ref, dgu_ref, act3_ref, cot_ref, down_ref, gu, down32 = refs[12:]
     place, row = place_ref[0], place_ref[1]
     side = lax.rem(place, 2)
     me = side * 4 + row
@@ -934,7 +934,11 @@
     down_ref[...] = down32[...].astype(BF)
     for i, bits in enumerate(GROUP_BITS):
         at = pl.multiple_of((me ^ bits) * size, size)
-        act3_ref[pl.ds(at, size), :] = act3_refs[i][...] if i < 4 else core_ref[i - 4]
+        if i == 3:
+            block = jnp.concatenate([act3_refs[3][...], act3_refs[4][...]], 0)
+        else:
+            block = act3_refs[i][...] if i < 3 else core_ref[i - 4]
+        act3_ref[pl.ds(at, size), :] = block
         cot_ref[pl.ds(at, size), :] = cot_refs[i][...] if i < 4 else cot_core_ref[i - 4]
     for i in range(4):
         rows = pl.ds(i * 2 * size, 2 * size)
@@ -1182,8 +1186,10 @@
 
     def group_gather(v):
         y, s = across(v), flip(v)
-        four = [v, y, s, flip(y)]
-        return [*four, core(jnp.stack(four))]
+        part = v.shape[0] // 2
+        top, bottom = flip(y[:part]), across(s[part:])
+        four = jnp.stack([v, y, s, jnp.concatenate([top, bottom], 0)])
+        return [v, y, s, top, bottom, core(four)]
 
     def row_sum(same, other):
         mine = same.astype(F32) + core(other).astype(F32)
@@ -1466,7 +1472,7 @@
         [shape((size, width), BF)],
         [d_act1, x, gains, d_resid],
         us=3,
-        mib=24,
+        mib=56,
         name="last",
     )
     red_gu, red_down, second_gain = local_call(
@@ -1480,7 +1486,7 @@
         scratch=[pltpu.VMEM((n_row, 2, size, 2 * wide), BF)],
         smem=1,
         us=0,
-        mib=24,
+        mib=56,
         name="lay_feed",
     )
     red_qkv, red_out, red_gains, red_conv, red_beta, red_head = local_call(
@@ -1496,7 +1502,7 @@
         [where_at, qkv_piece, qkv_y, qkv_cores, out_piece, out_y, out_cores, qkv_weight, beta_weight.T, norm_gains, second_gain],
         smem=1,
         us=3,
-        mib=24,
+        mib=56,
         name="lay_mix",
     )
     red_beta = red_beta.T

time: 294 us -> 292 us (level)
    ppermute x12 -> x13, waiting for transfers between devices: 26.7 us -> 22.2 us  [across(): return lax.ppermute(v, 'row', [(r, r ^ 2) for r in range(n_row)])]
    ppermute x12 -> x13, starting transfers between devices: 10.5 us -> 14.2 us  [across(): return lax.ppermute(v, 'row', [(r, r ^ 2) for r in range(n_row)])]
    ppermute x13, waiting for transfers between devices: 42.1 us -> 45.5 us  [flip(): return lax.ppermute(v, 'seq', [(s, s ^ 1) for s in range(n_seq)])]
    unnamed x98 -> x104, local copies, waits for them, and re-layouts: 14.8 us -> 13.5 us
  transfers between devices with their start and end apart: 49 -> 50, of which waited for: 26 -> 27; matrix products, arithmetic and copies ran while one was open for 7% -> 7% of each run, Pallas kernels for 21% -> 21%
where the time goes in v3:
time: 292 us; the launch traced here: 287 us
  waiting for transfers between devices  101 us (35%)
  Pallas kernels  71.5 us (24%)
  starting transfers between devices  67 us (23%)
  local copies, waits for them, and re-layouts  17.2 us (6%)
  other arithmetic  16.4 us (6%)
  between operations  14.6 us (5%)
    pallas_call x14, Pallas kernels, local_call(): pl.pallas_call(kernel, out_shape=tuple(outs), in_specs=space, out_specs=t...  71.5 us
    ppermute x13, waiting for transfers between devices, flip(): return lax.ppermute(v, 'seq', [(s, s ^ 1) for s in range(n_seq)])  45.5 us
    ppermute x13, waiting for transfers between devices, across(): return lax.ppermute(v, 'row', [(r, r ^ 2) for r in range(n_row)])  22.2 us
    ppermute x13, starting transfers between devices, flip(): return lax.ppermute(v, 'seq', [(s, s ^ 1) for s in range(n_seq)])  18.6 us
    ppermute x13, starting transfers between devices, across(): return lax.ppermute(v, 'row', [(r, r ^ 2) for r in range(n_row)])  14.2 us
    unnamed x104, local copies, waits for them, and re-layouts  13.5 us
    all_to_all x1, waiting for transfers between devices, head_plan(): d_act2 = lax.all_to_all(d_act2, 'seq', 0, 0)  12.1 us
    all_to_all x1, waiting for transfers between devices, head_plan(): act2 = lax.all_to_all(act2, 'seq', 0, 0)  6.86 us
  transfers between devices with their start and end apart: 50, of which 27 were waited for; matrix products, arithmetic and copies ran while one was open for 7% of the time, Pallas kernels for 21%

profile of v3, /device:TPU:0, one launch (start us, length us, event | category | flops | bytes accessed | tf_op | source)
XLA Modules:
  0.0 287.5 jit_solution(3908804665905326489)
XLA Ops:
  8.9 5.0 %collective-permute-start.6 = (bf16[64,1024]{1,0:T(8,128)(2,1)S(1)}, bf16[64,1024]{1,0:T(8,128)(2,1)S(1)}, u32[]{:S(2)}, u32[]{:S(2)}) collective-permute-start(bf16[64,1024]{1,0:T(8,128)(2,1)S(1)} %get-tuple-element.118.refs_1_), channel_id=1, source_target_pairs={{0,24},{4,28},{8,0},{12,4},{16,8},{20,12},{24,16},{28,20},{1,25},{... | collective-permute-start | bytes 393224 | tf_op jit(solution)/shard_map/ppermute | solution.py:1179
  19.1 4.1 %all-to-all-start = ((bf16[8,144,128]{2,1,0:T(8,128)(2,1)}), bf16[8,144,128]{2,1,0:T(8,128)(2,1)S(1)}, u32[]{:S(2)}, u32[]{:S(2)}) async-start(bf16[8,144,128]{2,1,0:T(8,128)(2,1)} %lead.1), calls=%async_computation | async-start | bytes 589824 | tf_op jit(solution)/shard_map/all_to_all | solution.py:1240
  28.9 6.0 %collective-permute-done.2 = bf16[384,256]{1,0:T(8,128)(2,1)S(1)} collective-permute-done((bf16[384,256]{1,0:T(8,128)(2,1)}, bf16[384,256]{1,0:T(8,128)(2,1)S(1)}, u32[]{:S(2)}, u32[]{:S(2)}) %collective-permute-start.2) | collective-permute-done | bytes 196640 | tf_op jit(solution)/shard_map/ppermute | solution.py:1176
  38.6 6.3 %all-to-all-start.1 = ((bf16[8,32,1024]{2,1,0:T(8,128)(2,1)}), bf16[8,32,1024]{2,1,0:T(8,128)(2,1)S(1)}, u32[]{:S(2)}, u32[]{:S(2)}) async-start(bf16[8,32,1024]{2,1,0:T(8,128)(2,1)} %broadcast_in_dim.12), calls=%async_computation.1 | async-start | bytes 1048576 | tf_op jit(solution)/shard_map/all_to_all | solution.py:1248
  49.4 9.8 %collective-permute-done.7.refs_4_ = bf16[64,1024]{1,0:T(8,128)(2,1)S(1)} collective-permute-done((bf16[64,1024]{1,0:T(8,128)(2,1)S(1)}, bf16[64,1024]{1,0:T(8,128)(2,1)S(1)}, u32[]{:S(2)}, u32[]{:S(2)}) %collective-permute-start.7) | collective-permute-done | bytes 131104 | tf_op jit(solution)/shard_map/ppermute | solution.py:1176
  59.3 3.5 %collective-permute-done.8.refs_6_ = bf16[64,1024]{1,0:T(8,128)(2,1)S(1)} collective-permute-done((bf16[64,1024]{1,0:T(8,128)(2,1)S(1)}, bf16[64,1024]{1,0:T(8,128)(2,1)S(1)}, u32[]{:S(2)}, u32[]{:S(2)}) %collective-permute-start.8) | collective-permute-done | bytes 131104 | tf_op jit(solution)/shard_map/ppermute | solution.py:1176
  69.8 12.8 %front.1 = (bf16[1024,384]{1,0:T(8,128)(2,1)}, bf16[1024,1024]{1,0:T(8,128)(2,1)}, bf16[1024,384]{1,0:T(8,128)(2,1)}, f32[1024,128]{1,0:T(8,128)}, f32[1024,128]...) custom-call(s32[2]{0:T(128)} %pad_add_fusion.place_ref, ...), custom_call_target="tpu_custom_call" | custom-call | flops 4000000000 | bytes 1024 | tf_op jit(solution)/shard_map/front/pallas_call | solution.py:1136
  85.6 5.3 %all-to-all-start.2 = ((bf16[8,128,128]{2,1,0:T(8,128)(2,1)}), bf16[8,128,128]{2,1,0:T(8,128)(2,1)S(1)}, u32[]{:S(2)}, u32[]{:S(2)}) async-start(bf16[8,128,128]{2,1,0:T(8,128)(2,1)} %get-tuple-element.132), calls=%async_computation.2 | async-start | bytes 524288 | tf_op jit(solution)/shard_map/all_to_all | solution.py:1311
  93.2 8.4 %collective-permute-done.14.refs_9_ = bf16[128,1024]{1,0:T(8,128)(2,1)S(1)} collective-permute-done((bf16[128,1024]{1,0:T(8,128)(2,1)S(1)}, bf16[128,1024]{1,0:T(8,128)(2,1)S(1)}, u32[]{:S(2)}, u32[]{:S(2)}) %collective-permute-start.14) | collective-permute-done | bytes 262176 | tf_op jit(solution)/shard_map/ppermute | solution.py:1176
  101.6 6.9 %all-to-all-done.2.act2_ref = bf16[8,128,128]{2,1,0:T(8,128)(2,1)S(1)} async-done(((bf16[8,128,128]{2,1,0:T(8,128)(2,1)}), bf16[8,128,128]{2,1,0:T(8,128)(2,1)S(1)}, u32[]{:S(2)}, u32[]{:S(2)}) %all-to-all-start.2) | async-done | bytes 262176 | tf_op jit(solution)/shard_map/all_to_all | solution.py:1311
  112.1 6.1 %collective-permute-done.16.refs_2_ = bf16[128,1024]{1,0:T(8,128)(2,1)S(1)} collective-permute-done((bf16[128,1024]{1,0:T(8,128)(2,1)S(1)}, bf16[128,1024]{1,0:T(8,128)(2,1)S(1)}, u32[]{:S(2)}, u32[]{:S(2)}) %collective-permute-start.16) | collective-permute-done | bytes 262176 | tf_op jit(solution)/shard_map/ppermute | solution.py:1176
  133.3 8.6 %feed.1 = (bf16[4,128,1024]{2,1,0:T(8,128)(2,1)S(1)}, bf16[4,128,1024]{2,1,0:T(8,128)(2,1)}, bf16[1024,384]{1,0:T(8,128)(2,1)S(1)}, bf16[1024,768]{1,0:T(8,128)(...) custom-call(s32[2]{0:T(128)S(1)} %copy-done.16, ...), custom_call_target="tpu_custom_call" | custom-call | flops 3000000000 | bytes 1024 | tf_op jit(solution)/shard_map/feed/pallas_call | solution.py:1136
  151.3 4.8 %mixed.1 = (bf16[4,128,1024]{2,1,0:T(8,128)(2,1)}, bf16[4,128,1024]{2,1,0:T(8,128)(2,1)}) custom-call(s32[2]{0:T(128)} %pad_add_fusion.place_ref, bf16[1024,384]{1,0:T(8,128)(2,1)} %copy-done.22, bf16[384,1024]{1,0:T(8,128)(2,1)} %copy-done.23), custom_call_target="tpu_custom_call" | custom-call | flops 5000000000 | bytes 1024 | tf_op jit(solution)/shard_map/mixed/pallas_call | solution.py:1136
  167.7 3.4 %all-to-all-start.3 = ((bf16[8,128,128]{2,1,0:T(8,128)(2,1)}), bf16[8,128,128]{2,1,0:T(8,128)(2,1)S(1)}, u32[]{:S(2)}, u32[]{:S(2)}) async-start(bf16[8,128,128]{2,1,0:T(8,128)(2,1)} %get-tuple-element.157), calls=%async_computation.3 | async-start | bytes 524288 | tf_op jit(solution)/shard_map/all_to_all | solution.py:1378
  175.0 12.1 %all-to-all-done.3.refs_0_ = bf16[8,128,128]{2,1,0:T(8,128)(2,1)S(1)} async-done(((bf16[8,128,128]{2,1,0:T(8,128)(2,1)}), bf16[8,128,128]{2,1,0:T(8,128)(2,1)S(1)}, u32[]{:S(2)}, u32[]{:S(2)}) %all-to-all-start.3) | async-done | bytes 262176 | tf_op jit(solution)/shard_map/all_to_all | solution.py:1378
  187.8 14.6 %back.1 = (bf16[1024,384]{1,0:T(8,128)(2,1)}, bf16[1024,1024]{1,0:T(8,128)(2,1)}, f32[8,128]{1,0:T(8,128)}, f32[8,384]{1,0:T(8,128)}, f32[8,128]{1,0:T(8,128)}) custom-call(s32[2]{0:T(128)} %pad_add_fusion.place_ref, s32[8]{0:T(128)} %bitcast.94, bf16[8,128,128]{2,1,0:T(8,128)(2,1)} %copy-done.38, f32[1024,128]{1,0:T(8,128)} %get-tuple-element.165.refs_1_, ...), custom_call_target="tpu_custom_call" | custom-call | flops 14000000000 | bytes 1024 | tf_op jit(solution)/shard_map/back/pallas_call | solution.py:1136
  202.5 4.8 %qkv_grad.1 = (bf16[2,8,48,384]{3,2,1,0:T(8,128)(2,1)}, bf16[2,8,48,384]{3,2,1,0:T(8,128)(2,1)}) custom-call(s32[2]{0:T(128)} %pad_add_fusion.place_ref, bf16[1024,1024]{1,0:T(8,128)(2,1)} %get-tuple-element.189.act1_ref, bf16[1024,384]{1,0:T(8,128)(2,1)} %get-tuple-element.190.dproj_ref, f32[8,128]{1,0:T(8,128)} %get-tuple-element.191.dlog_ref, ...), custom_call_target="tpu_custom_call" | custom-call | flops 5000000000 | bytes 1024 | tf_op jit(solution)/shard_map/qkv_grad/pallas_call | solution.py:1136
  213.2 4.4 %collective-permute-done.37 = bf16[384,256]{1,0:T(8,128)(2,1)S(1)} collective-permute-done((bf16[384,256]{1,0:T(8,128)(2,1)S(1)}, bf16[384,256]{1,0:T(8,128)(2,1)S(1)}, u32[]{:S(2)}, u32[]{:S(2)}) %collective-permute-start.37) | collective-permute-done | bytes 196640 | tf_op jit(solution)/shard_map/ppermute | solution.py:1176
  221.4 3.4 %all-to-all-start.4 = ((bf16[8,48,384]{2,1,0:T(8,128)(2,1)}), bf16[8,48,384]{2,1,0:T(8,128)(2,1)S(1)}, u32[]{:S(2)}, u32[]{:S(2)}) async-start(bf16[8,48,384]{2,1,0:T(8,128)(2,1)} %fusion.1), calls=%async_computation.6 | async-start | bytes 589824 | tf_op jit(solution)/shard_map/all_to_all | solution.py:1467
  234.0 5.4 %all-to-all-done.4.refs_0_ = bf16[8,48,384]{2,1,0:T(8,128)(2,1)S(1)} async-done(((bf16[8,48,384]{2,1,0:T(8,128)(2,1)}), bf16[8,48,384]{2,1,0:T(8,128)(2,1)S(1)}, u32[]{:S(2)}, u32[]{:S(2)}) %all-to-all-start.4) | async-done | bytes 294944 | tf_op jit(solution)/shard_map/all_to_all | solution.py:1467
  239.4 3.8 %all-to-all-start.5 = ((bf16[8,32,1024]{2,1,0:T(8,128)(2,1)}), bf16[8,32,1024]{2,1,0:T(8,128)(2,1)S(1)}, u32[]{:S(2)}, u32[]{:S(2)}) async-start(bf16[8,32,1024]{2,1,0:T(8,128)(2,1)} %fusion), calls=%async_computation.7 | async-start | bytes 1048576 | tf_op jit(solution)/shard_map/all_to_all | solution.py:1443
  245.9 5.6 %collective-permute-done.32.refs_1_ = bf16[8,48,384]{2,1,0:T(8,128)(2,1)S(1)} collective-permute-done((bf16[8,48,384]{2,1,0:T(8,128)(2,1)S(1)}, bf16[8,48,384]{2,1,0:T(8,128)(2,1)S(1)}, u32[]{:S(2)}, u32[]{:S(2)}) %collective-permute-start.32) | collective-permute-done | bytes 294944 | tf_op jit(solution)/shard_map/ppermute | solution.py:1185
  258.8 5.0 %collective-permute-done.35.refs_4_ = bf16[32,1024]{1,0:T(8,128)(2,1)S(1)} collective-permute-done((bf16[32,1024]{1,0:T(8,128)(2,1)S(1)}, bf16[32,1024]{1,0:T(8,128)(2,1)S(1)}, u32[]{:S(2)}, u32[]{:S(2)}) %collective-permute-start.35) | collective-permute-done | bytes 65568 | tf_op jit(solution)/shard_map/ppermute | solution.py:1185
  267.0 5.4 %lay_feed.1 = (f32[128,5632]{1,0:T(8,128)}, f32[352,1024]{1,0:T(8,128)}, f32[1,128]{1,0:T(1,128)}) custom-call(s32[2]{0:T(128)} %pad_add_fusion.place_ref, bf16[1152,256]{1,0:T(8,128)(2,1)} %copy-done.24, bf16[1152,256]{1,0:T(8,128)(2,1)} %copy-done.25, bf16[2,1152,256]{2,1,0:T(8,128)(2,1)} %copy-done.28, bf16[128,5632]{1,0:T(8,128)(2,1)} %refs_3_.1, ...), custom_call_target="tpu_custom_call" | custom-call | bytes 1024 | tf_op jit(solution)/shard_map/lay_feed/pallas_call | solution.py:1136
  (228 shorter events, 117.3 us)
Async XLA Ops:
  7.2 58.4 %all-gather.5.cloned.1.call-start = ((), (), s32[]{:S(2)}) async-start(), calls=%async_computation.10 | async-start | bytes 1179648 | tf_op jit(solution)/shard_map/all_gather | solution.py:1215
  8.9 28.5 %collective-permute-start.6 = (bf16[64,1024]{1,0:T(8,128)(2,1)S(1)}, bf16[64,1024]{1,0:T(8,128)(2,1)S(1)}, u32[]{:S(2)}, u32[]{:S(2)}) collective-permute-start(bf16[64,1024]{1,0:T(8,128)(2,1)S(1)} %get-tuple-element.118.refs_1_), channel_id=1, source_target_pairs={{0,24},{4,28},{8,0},{12,4},{16,8},{20,12},{24,16},{28,20},{1,25},{... | collective-permute-start | bytes 393224 | tf_op jit(solution)/shard_map/ppermute | solution.py:1179
  14.0 23.5 %collective-permute-start.5 = (bf16[64,1024]{1,0:T(8,128)(2,1)S(1)}, bf16[64,1024]{1,0:T(8,128)(2,1)S(1)}, u32[]{:S(2)}, u32[]{:S(2)}) collective-permute-start(bf16[64,1024]{1,0:T(8,128)(2,1)S(1)} %get-tuple-element.118.refs_1_), channel_id=1, source_target_pairs={{0,16},{4,20},{8,24},{12,28},{16,0},{20,4},{24,8},{28,12},{1,17},{... | collective-permute-start | bytes 393224 | tf_op jit(solution)/shard_map/ppermute | solution.py:1179
  14.0 23.5 %collective-permute-start.4 = (bf16[64,1024]{1,0:T(8,128)(2,1)S(1)}, bf16[64,1024]{1,0:T(8,128)(2,1)S(1)}, u32[]{:S(2)}, u32[]{:S(2)}) collective-permute-start(bf16[64,1024]{1,0:T(8,128)(2,1)S(1)} %get-tuple-element.118.refs_1_), channel_id=1, source_target_pairs={{0,8},{4,12},{8,16},{12,20},{16,24},{20,28},{24,0},{28,4},{1,9},{5... | collective-permute-start | bytes 393224 | tf_op jit(solution)/shard_map/ppermute | solution.py:1179
  15.0 22.5 %collective-permute-start.3 = (bf16[64,1024]{1,0:T(8,128)(2,1)S(1)}, bf16[64,1024]{1,0:T(8,128)(2,1)S(1)}, u32[]{:S(2)}, u32[]{:S(2)}) collective-permute-start(bf16[64,1024]{1,0:T(8,128)(2,1)S(1)} %get-tuple-element.118.refs_1_), channel_id=1, source_target_pairs={{0,4},{4,0},{8,12},{12,8},{16,20},{20,16},{24,28},{28,24},{1,5},{5... | collective-permute-start | bytes 393224 | tf_op jit(solution)/shard_map/ppermute | solution.py:1176
  38.6 27.0 %all-to-all-start.1 = ((bf16[8,32,1024]{2,1,0:T(8,128)(2,1)}), bf16[8,32,1024]{2,1,0:T(8,128)(2,1)S(1)}, u32[]{:S(2)}, u32[]{:S(2)}) async-start(bf16[8,32,1024]{2,1,0:T(8,128)(2,1)} %broadcast_in_dim.12), calls=%async_computation.1 | async-start | bytes 1048576 | tf_op jit(solution)/shard_map/all_to_all | solution.py:1248
  44.9 80.7 %all-gather.7.cloned.1.call-start = ((), (), s32[]{:S(2)}) async-start(), calls=%async_computation.11 | async-start | bytes 2949120 | tf_op jit(solution)/shard_map/all_gather | solution.py:1246
  45.2 20.4 %collective-permute-start.1 = (bf16[2,8,144,128]{3,2,1,0:T(8,128)(2,1)S(1)}, bf16[2,8,144,128]{3,2,1,0:T(8,128)(2,1)}, u32[]{:S(2)}, u32[]{:S(2)}) collective-permute-start(bf16[2,8,144,128]{3,2,1,0:T(8,128)(2,1)S(1)} %pad_maximum_fusion.4), channel_id=1, source_target_pairs={{0,1},{1,0},{2,3},{3,2},{4,5},{5,4},{6,7},{7,6},{8,9},{9,8},{10,11... | collective-permute-start | bytes 1769480 | tf_op jit(solution)/shard_map/ppermute | solution.py:1182
  47.4 17.4 %collective-permute-start.9 = (bf16[64,1024]{1,0:T(8,128)(2,1)S(1)}, bf16[64,1024]{1,0:T(8,128)(2,1)S(1)}, u32[]{:S(2)}, u32[]{:S(2)}) collective-permute-start(bf16[64,1024]{1,0:T(8,128)(2,1)S(1)} %collective-permute-done.6.refs_7_), channel_id=1, source_target_pairs={{0,4},{4,0},{8,12},{12,8},{16,20},{20,16},{24,28},{28,24},{1,5},{5... | collective-permute-start | bytes 393224 | tf_op jit(solution)/shard_map/ppermute | solution.py:1176
  65.6 18.9 %collective-permute-start.12 = (bf16[8,32,1024]{2,1,0:T(8,128)(2,1)S(1)}, bf16[8,32,1024]{2,1,0:T(8,128)(2,1)S(1)}, u32[]{:S(2)}, u32[]{:S(2)}) collective-permute-start(bf16[8,32,1024]{2,1,0:T(8,128)(2,1)S(1)} %all-to-all-done.1.own_ref), channel_id=1, source_target_pairs={{0,2},{1,3},{2,0},{3,1},{4,6},{5,7},{6,4},{7,5},{8,10},{9,11},{10,... | collective-permute-start | bytes 1572872 | tf_op jit(solution)/shard_map/ppermute | solution.py:1185
  66.5 16.1 %collective-permute-start.11 = (bf16[128,1024]{1,0:T(8,128)(2,1)S(1)}, bf16[128,1024]{1,0:T(8,128)(2,1)S(1)}, u32[]{:S(2)}, u32[]{:S(2)}) collective-permute-start(bf16[128,1024]{1,0:T(8,128)(2,1)S(1)} %bitcast.67), channel_id=1, source_target_pairs={{0,4},{4,0},{8,12},{12,8},{16,20},{20,16},{24,28},{28,24},{1,5},{5... | collective-permute-start | bytes 786440 | tf_op jit(solution)/shard_map/ppermute | solution.py:1176
  68.2 16.3 %collective-permute-start.10 = (bf16[128,1024]{1,0:T(8,128)(2,1)S(1)}, bf16[128,1024]{1,0:T(8,128)(2,1)S(1)}, u32[]{:S(2)}, u32[]{:S(2)}) collective-permute-start(bf16[128,1024]{1,0:T(8,128)(2,1)S(1)} %bitcast.68), channel_id=1, source_target_pairs={{0,2},{1,3},{2,0},{3,1},{4,6},{5,7},{6,4},{7,5},{8,10},{9,11},{10,... | collective-permute-start | bytes 786440 | tf_op jit(solution)/shard_map/ppermute | solution.py:1185
  85.6 22.9 %collective-permute-start.13 = (bf16[2,8,32,1024]{3,2,1,0:T(8,128)(2,1)}, bf16[2,8,32,1024]{3,2,1,0:T(8,128)(2,1)}, u32[]{:S(2)}, u32[]{:S(2)}) collective-permute-start(bf16[2,8,32,1024]{3,2,1,0:T(8,128)(2,1)} %pad_maximum_fusion.1), channel_id=1, source_target_pairs={{0,1},{1,0},{2,3},{3,2},{4,5},{5,4},{6,7},{7,6},{8,9},{9,8},{10,11... | collective-permute-start | bytes 3145736 | tf_op jit(solution)/shard_map/ppermute | solution.py:1182
  85.6 22.9 %all-to-all-start.2 = ((bf16[8,128,128]{2,1,0:T(8,128)(2,1)}), bf16[8,128,128]{2,1,0:T(8,128)(2,1)S(1)}, u32[]{:S(2)}, u32[]{:S(2)}) async-start(bf16[8,128,128]{2,1,0:T(8,128)(2,1)} %get-tuple-element.132), calls=%async_computation.2 | async-start | bytes 524288 | tf_op jit(solution)/shard_map/all_to_all | solution.py:1311
  90.9 111.6 %reduce-scatter.3.cloned.1.call-start = ((), (), s32[]{:S(2)}) async-start(), calls=%async_computation.8 | async-start | bytes 2949120 | tf_op jit(solution)/shard_map/reduce_scatter | solution.py:1356
  167.7 19.4 %all-to-all-start.3 = ((bf16[8,128,128]{2,1,0:T(8,128)(2,1)}), bf16[8,128,128]{2,1,0:T(8,128)(2,1)S(1)}, u32[]{:S(2)}, u32[]{:S(2)}) async-start(bf16[8,128,128]{2,1,0:T(8,128)(2,1)} %get-tuple-element.157), calls=%async_computation.3 | async-start | bytes 524288 | tf_op jit(solution)/shard_map/all_to_all | solution.py:1378
  171.1 107.4 %reduce-scatter.5.cloned.1.call-start = ((), (), s32[]{:S(2)}) async-start(), calls=%async_computation.9 | async-start | bytes 2359296 | tf_op jit(solution)/shard_map/reduce_scatter | solution.py:1440
  211.8 20.1 %collective-permute-start.34 = (bf16[8,32,1024]{2,1,0:T(8,128)(2,1)S(1)}, bf16[8,32,1024]{2,1,0:T(8,128)(2,1)}, u32[]{:S(2)}, u32[]{:S(2)}) collective-permute-start(bf16[8,32,1024]{2,1,0:T(8,128)(2,1)S(1)} %fusion.2), channel_id=1, source_target_pairs={{0,2},{1,3},{2,0},{3,1},{4,6},{5,7},{6,4},{7,5},{8,10},{9,11},{10,... | collective-permute-start | bytes 1572872 | tf_op jit(solution)/shard_map/ppermute | solution.py:1185
  217.7 27.0 %collective-permute-start.38 = (bf16[1152,256]{1,0:T(8,128)(2,1)S(1)}, bf16[1152,256]{1,0:T(8,128)(2,1)S(1)}, u32[]{:S(2)}, u32[]{:S(2)}) collective-permute-start(bf16[1152,256]{1,0:T(8,128)(2,1)S(1)} %get-tuple-element.217.refs_0_), channel_id=1, source_target_pairs={{0,2},{1,3},{2,0},{3,1},{4,6},{5,7},{6,4},{7,5},{8,10},{9,11},{10,... | collective-permute-start | bytes 1769480 | tf_op jit(solution)/shard_map/ppermute | solution.py:1185
  221.4 18.0 %all-to-all-start.4 = ((bf16[8,48,384]{2,1,0:T(8,128)(2,1)}), bf16[8,48,384]{2,1,0:T(8,128)(2,1)S(1)}, u32[]{:S(2)}, u32[]{:S(2)}) async-start(bf16[8,48,384]{2,1,0:T(8,128)(2,1)} %fusion.1), calls=%async_computation.6 | async-start | bytes 589824 | tf_op jit(solution)/shard_map/all_to_all | solution.py:1467
  227.3 25.1 %collective-permute-start.28 = (bf16[2,128,1024]{2,1,0:T(8,128)(2,1)}, bf16[2,128,1024]{2,1,0:T(8,128)(2,1)}, u32[]{:S(2)}, u32[]{:S(2)}) collective-permute-start(bf16[2,128,1024]{2,1,0:T(8,128)(2,1)} %pad_maximum_fusion.7), channel_id=1, source_target_pairs={{0,4},{4,0},{8,12},{12,8},{16,20},{20,16},{24,28},{28,24},{1,5},{5... | collective-permute-start | bytes 1572872 | tf_op jit(solution)/shard_map/ppermute | solution.py:1176
  239.4 18.1 %all-to-all-start.5 = ((bf16[8,32,1024]{2,1,0:T(8,128)(2,1)}), bf16[8,32,1024]{2,1,0:T(8,128)(2,1)S(1)}, u32[]{:S(2)}, u32[]{:S(2)}) async-start(bf16[8,32,1024]{2,1,0:T(8,128)(2,1)} %fusion), calls=%async_computation.7 | async-start | bytes 1048576 | tf_op jit(solution)/shard_map/all_to_all | solution.py:1443
  245.9 20.1 %collective-permute-start.39 = (bf16[2,1152,256]{2,1,0:T(8,128)(2,1)}, bf16[2,1152,256]{2,1,0:T(8,128)(2,1)S(1)}, u32[]{:S(2)}, u32[]{:S(2)}) collective-permute-start(bf16[2,1152,256]{2,1,0:T(8,128)(2,1)} %pad_maximum_fusion), channel_id=1, source_target_pairs={{0,1},{1,0},{2,3},{3,2},{4,5},{5,4},{6,7},{7,6},{8,9},{9,8},{10,11... | collective-permute-start | bytes 3538952 | tf_op jit(solution)/shard_map/ppermute | solution.py:1182
  252.4 20.0 %collective-permute-start.33 = (bf16[2,8,48,384]{3,2,1,0:T(8,128)(2,1)}, bf16[2,8,48,384]{3,2,1,0:T(8,128)(2,1)}, u32[]{:S(2)}, u32[]{:S(2)}) collective-permute-start(bf16[2,8,48,384]{3,2,1,0:T(8,128)(2,1)} %pad_maximum_fusion.5), channel_id=1, source_target_pairs={{0,1},{1,0},{2,3},{3,2},{4,5},{5,4},{6,7},{7,6},{8,9},{9,8},{10,11... | collective-permute-start | bytes 1769480 | tf_op jit(solution)/shard_map/ppermute | solution.py:1182
  (77 other events, 690.2 us)
Sparse Core Ops, SparseCore 0:
  16.6 48.4 all-gather.4
  67.3 55.8 all-gather.6
  148.6 50.6 reduce-scatter.2
  202.8 75.7 reduce-scatter.4
